TPU v7x, 32 devices: a whole 2x2x4 slice. The times are simulated.
32 devices in a mesh: sweep: 8 (over y, x, core), span: 4 (over z).
Axes of the slice: x: 2, y: 2, z: 4, core: 2. Of those that a mesh axis runs over, the one named last changes fastest.
Arguments:
- right_side: float32 [16, 4, 625, 512], P('sweep', 'span'), may hold values from -6 to 6
- start_field: float32 [16, 4, 625, 512], P('sweep', 'span'), may hold values from -6 to 6
- block_inverse: float32 [16, 4, 625, 625], P('sweep', 'span'), may hold values from -0.25 to 0.25
- upwind_block: float32 [16, 4, 625, 125], P('sweep', 'span'), may hold values from -1 to 1
- south_block: float32 [16, 4, 625, 125], P('sweep', 'span'), may hold values from -0.625 to 0.625
- north_block: float32 [16, 4, 625, 125], P('sweep', 'span'), may hold values from -0.625 to 0.625
Outputs:
- solution: float32 [16, 4, 625, 512], P('sweep', 'span')
All inputs are finite; a program needn't handle non-finite values.
Results may differ from a plain program's by a relative error of at most 0.00022.
Values sent between devices are 32-bit elements; how exact they have to be, the bound alone decides.
No kernel may reach another device: no remote copies, remote signals or barrier semaphores. Data moves between devices by JAX's collectives and lax.ppermute only.
A program may use at most 128 MiB of HBM per device.

v0:
```python
import jax
import jax.numpy as jnp
from jax import lax
from jax.sharding import PartitionSpec as P

VARS = 5
NODE = 5
FACE = 125
FRONTS = 4
SWEEPS = 2


def passed_along(shard, axis, by):
    count = lax.axis_size(axis)
    pairs = [(i, i + by) for i in range(count) if 0 <= i + by < count]
    return lax.ppermute(shard, axis, pairs)


def from_behind(shard, axis, by):
    count = lax.axis_size(axis)
    return lax.ppermute(shard, axis, [(i, (i + by) % count) for i in range(count)])


def face_grid(field):
    leading = field.shape[:-2]
    return field.reshape(leading + (VARS, NODE, NODE, NODE, field.shape[-1]))


def down_face(field):
    leading = field.shape[:-2]
    return face_grid(field)[..., :, NODE - 1, :, :, :].reshape(leading + (FACE, field.shape[-1]))


def high_face(field):
    leading = field.shape[:-2]
    return face_grid(field)[..., :, :, NODE - 1, :, :].reshape(leading + (FACE, field.shape[-1]))


def low_face(field):
    leading = field.shape[:-2]
    return face_grid(field)[..., :, :, 0, :, :].reshape(leading + (FACE, field.shape[-1]))


def product(matrix, vectors):
    return jnp.dot(
        matrix, vectors, precision=lax.Precision.HIGHEST, preferred_element_type=jnp.float32
    )


def batched_product(matrix, vectors):
    return jnp.einsum("eab,ebr->ear", matrix, vectors, precision=lax.Precision.HIGHEST)


def slab_solve(inverse_local, upwind_local, inflow, forcing):
    pieces = []
    for element in range(forcing.shape[0]):
        residual = forcing[element] - product(upwind_local[element], inflow)
        solved = product(inverse_local[element], residual)
        pieces.append(solved)
        inflow = down_face(solved)
    return (jnp.stack(pieces), inflow)


def front_chain(inverse_local, upwind_local, forcing, sections, device_pos):
    columns = forcing.shape[-1]
    panel_width = columns // FRONTS

    def section_step(step_no, state_pair):
        field_new, outgoing = state_pair
        incoming = passed_along(outgoing, "sweep", 1)
        front_no = step_no - device_pos
        active = jnp.logical_and(front_no >= 0, front_no < FRONTS)
        chosen = jnp.clip(front_no, 0, FRONTS - 1) * panel_width

        def advance(current):
            panel_rhs = lax.dynamic_slice_in_dim(forcing, chosen, panel_width, 2)
            solved, leaving = slab_solve(inverse_local, upwind_local, incoming, panel_rhs)
            return (lax.dynamic_update_slice_in_dim(current, solved, chosen, 2), leaving)

        def remain(current):
            return (current, jnp.zeros_like(incoming))

        return lax.cond(active, advance, remain, field_new)

    initial = (jnp.zeros_like(forcing), jnp.zeros((FACE, panel_width), jnp.float32))
    field_new, _ = lax.fori_loop(0, sections + FRONTS - 1, section_step, initial)
    return field_new


def per_device(right_side, start_field, block_inverse, upwind_block, south_block, north_block):
    rhs_local = right_side[:, 0]
    field = start_field[:, 0]
    inverse_local = block_inverse[:, 0]
    upwind_local = upwind_block[:, 0]
    south_local = south_block[:, 0]
    north_local = north_block[:, 0]
    sections = lax.axis_size("sweep")
    device_pos = lax.axis_index("sweep")
    for sweep_no in range(SWEEPS):
        south_traces = from_behind(high_face(field), "span", 1)
        north_traces = from_behind(low_face(field), "span", -1)
        forcing = (
            rhs_local
            - batched_product(south_local, south_traces)
            - batched_product(north_local, north_traces)
        )
        field = front_chain(inverse_local, upwind_local, forcing, sections, device_pos)
    return field[:, None]


def solution(mesh):
    return jax.shard_map(
        per_device,
        mesh=mesh,
        in_specs=(
            P("sweep", "span", None, None),
            P("sweep", "span", None, None),
            P("sweep", "span", None, None),
            P("sweep", "span", None, None),
            P("sweep", "span", None, None),
            P("sweep", "span", None, None),
        ),
        out_specs=P("sweep", "span", None, None),
        check_vma=False,
    )
```

profile of v0, /device:TPU:23, one launch (start us, length us, event | category | flops | bytes accessed | tf_op | source)
XLA Modules:
  0.0 472.0 jit_solution(9073482315633233413)
XLA Ops:
  0.0 3.0 copy.15
  8.6 8.9 %collective-permute-done.2 = f32[2,125,512]{2,1,0:T(8,128)} collective-permute-done((f32[2,125,512]{2,1,0:T(8,128)}, f32[2,125,512]{2,1,0:T(8,128)}, u32[]{:S(2)}, u32[]{:S(2)}) %collective-permute-start.2) | collective-permute-done | bytes 512032 | tf_op jit(solution)/shard_map/ppermute | solution.py:21
  17.5 3.4 fusion.31
  21.0 7.6 %collective-permute-done.3 = f32[2,125,512]{2,1,0:T(8,128)} collective-permute-done((f32[2,125,512]{2,1,0:T(8,128)}, f32[2,125,512]{2,1,0:T(8,128)}, u32[]{:S(2)}, u32[]{:S(2)}) %collective-permute-start.3) | collective-permute-done | bytes 512032 | tf_op jit(solution)/shard_map/ppermute | solution.py:21
  28.6 5.0 %fusion.22 = f32[2,625,512]{2,1,0:T(8,128)} fusion(f32[2,625,512]{2,1,0:T(8,128)S(1)} %fusion.31, f32[2,1,625,512]{3,1,2,0:T(1,128)S(1)} %copy-done.4, f32[2,125,512]{2,1,0:T(8,128)} %collective-permute-done.3, f32[2,1,625,125]{3,1,2,0:T(1,128)S(1)} %copy-done.7), kind=kOutput, calls=%fused_computation.39 | convolution fusion | flops 961280000 | bytes 8817000 | tf_op jit(solution)/shard_map/eab,ebr->ear/dot_general | solution.py:51
  33.6 1.8 broadcast.12.clone
  36.1 222.3 %while.36 = (s32[]{:T(128)}, f32[2,625,512]{2,1,0:T(8,128)}, f32[125,128]{1,0:T(8,128)}, s32[]{:T(128)}, f32[2,625,512]{2,1,0:T(8,128)}, /*index=5*/f32[2,625,12...) while((s32[]{:T(128)}, f32[2,625,512]{2,1,0:T(8,128)}, f32[125,128]{1,0:T(8,128)}, ...), condition=%wide.region_3.4_spmd, body=%wide.region_0.3_spmd.sunk | while | flops 1440320000 | bytes 12480909 | solution.py:86
  37.4 6.6 %collective-permute-done = f32[125,128]{1,0:T(8,128)S(1)} collective-permute-done((f32[125,128]{1,0:T(8,128)}, f32[125,128]{1,0:T(8,128)S(1)}, u32[]{:S(2)}, u32[]{:S(2)}) %collective-permute-start) | collective-permute-done | bytes 64032 | tf_op jit(solution)/shard_map/while/body/eval_jaxpr/ppermute | solution.py:16
  45.9 4.5 collective-permute-done
  52.3 4.5 collective-permute-done
  58.7 4.5 collective-permute-done
  65.1 4.5 collective-permute-done
  71.6 4.5 collective-permute-done
  78.0 4.5 collective-permute-done
  84.4 92.6 %collective-permute-done = f32[125,128]{1,0:T(8,128)S(1)} collective-permute-done((f32[125,128]{1,0:T(8,128)}, f32[125,128]{1,0:T(8,128)S(1)}, u32[]{:S(2)}, u32[]{:S(2)}) %collective-permute-start) | collective-permute-done | bytes 64032 | tf_op jit(solution)/shard_map/while/body/eval_jaxpr/ppermute | solution.py:16
  176.9 15.4 %conditional.4 = (f32[2,625,512]{2,1,0:T(8,128)}, f32[125,128]{1,0:T(8,128)}) conditional(s32[]{:T(128)} %convert_element_type.16, f32[2,625,512]{2,1,0:T(8,128)} %get-tuple-element.490, (s32[]{:T(128)}, f32[2,625,512]{2,1,0:T(8,128)}, f32[2,625,125]{2,1,0:T(8,128)}, f32[125,128]{1,0:T(8,128)S(1)}, f32[2,625,625]{2,1,0:T(8,128)S(1)}, ...), branch_computations={%region_1.1_spmd, %region_2.2_spmd} | conditional | flops 1440320000 | bytes 12224682 | solution.py:83
  178.7 2.4 fusion.2
  181.0 1.8 reshape.15
  188.9 1.8 reshape.16
  193.6 5.3 %collective-permute-done = f32[125,128]{1,0:T(8,128)S(1)} collective-permute-done((f32[125,128]{1,0:T(8,128)}, f32[125,128]{1,0:T(8,128)S(1)}, u32[]{:S(2)}, u32[]{:S(2)}) %collective-permute-start) | collective-permute-done | bytes 64032 | tf_op jit(solution)/shard_map/while/body/eval_jaxpr/ppermute | solution.py:16
  198.9 15.3 %conditional.4 = (f32[2,625,512]{2,1,0:T(8,128)}, f32[125,128]{1,0:T(8,128)}) conditional(s32[]{:T(128)} %convert_element_type.16, f32[2,625,512]{2,1,0:T(8,128)} %get-tuple-element.490, (s32[]{:T(128)}, f32[2,625,512]{2,1,0:T(8,128)}, f32[2,625,125]{2,1,0:T(8,128)}, f32[125,128]{1,0:T(8,128)S(1)}, f32[2,625,625]{2,1,0:T(8,128)S(1)}, ...), branch_computations={%region_1.1_spmd, %region_2.2_spmd} | conditional | flops 1440320000 | bytes 12224682 | solution.py:83
  200.6 2.4 fusion.2
  203.0 1.8 reshape.15
  210.8 1.8 reshape.16
  215.5 5.5 %collective-permute-done = f32[125,128]{1,0:T(8,128)S(1)} collective-permute-done((f32[125,128]{1,0:T(8,128)}, f32[125,128]{1,0:T(8,128)S(1)}, u32[]{:S(2)}, u32[]{:S(2)}) %collective-permute-start) | collective-permute-done | bytes 64032 | tf_op jit(solution)/shard_map/while/body/eval_jaxpr/ppermute | solution.py:16
  221.0 15.4 %conditional.4 = (f32[2,625,512]{2,1,0:T(8,128)}, f32[125,128]{1,0:T(8,128)}) conditional(s32[]{:T(128)} %convert_element_type.16, f32[2,625,512]{2,1,0:T(8,128)} %get-tuple-element.490, (s32[]{:T(128)}, f32[2,625,512]{2,1,0:T(8,128)}, f32[2,625,125]{2,1,0:T(8,128)}, f32[125,128]{1,0:T(8,128)S(1)}, f32[2,625,625]{2,1,0:T(8,128)S(1)}, ...), branch_computations={%region_1.1_spmd, %region_2.2_spmd} | conditional | flops 1440320000 | bytes 12224682 | solution.py:83
  222.7 2.4 fusion.2
  225.1 1.8 reshape.15
  233.0 1.8 reshape.16
  237.6 5.4 %collective-permute-done = f32[125,128]{1,0:T(8,128)S(1)} collective-permute-done((f32[125,128]{1,0:T(8,128)}, f32[125,128]{1,0:T(8,128)S(1)}, u32[]{:S(2)}, u32[]{:S(2)}) %collective-permute-start) | collective-permute-done | bytes 64032 | tf_op jit(solution)/shard_map/while/body/eval_jaxpr/ppermute | solution.py:16
  243.0 15.4 %conditional.4 = (f32[2,625,512]{2,1,0:T(8,128)}, f32[125,128]{1,0:T(8,128)}) conditional(s32[]{:T(128)} %convert_element_type.16, f32[2,625,512]{2,1,0:T(8,128)} %get-tuple-element.490, (s32[]{:T(128)}, f32[2,625,512]{2,1,0:T(8,128)}, f32[2,625,125]{2,1,0:T(8,128)}, f32[125,128]{1,0:T(8,128)S(1)}, f32[2,625,625]{2,1,0:T(8,128)S(1)}, ...), branch_computations={%region_1.1_spmd, %region_2.2_spmd} | conditional | flops 1440320000 | bytes 12224682 | solution.py:83
  244.7 2.4 fusion.2
  247.1 1.8 reshape.15
  255.0 1.8 reshape.16
  258.4 3.7 copy.18
  265.7 11.6 %collective-permute-done.4 = f32[2,125,512]{2,1,0:T(8,128)} collective-permute-done((f32[2,125,512]{2,1,0:T(8,128)}, f32[2,125,512]{2,1,0:T(8,128)}, u32[]{:S(2)}, u32[]{:S(2)}) %collective-permute-start.4) | collective-permute-done | bytes 512032 | tf_op jit(solution)/shard_map/ppermute | solution.py:21
  277.3 3.5 fusion.29
  280.8 5.0 %fusion.23 = f32[2,625,512]{2,1,0:T(8,128)} fusion(f32[2,512,625]{1,2,0:T(8,128)S(1)} %fusion.29, f32[2,1,625,512]{3,1,2,0:T(1,128)S(1)} %copy-done.5, f32[2,125,512]{2,1,0:T(8,128)} %collective-permute-done.5, f32[2,1,625,125]{3,1,2,0:T(1,128)S(1)} %copy-done.8), kind=kOutput, calls=%fused_computation.40 | convolution fusion | flops 961280000 | bytes 8817000 | tf_op jit(solution)/shard_map/eab,ebr->ear/dot_general | solution.py:51
  285.8 1.8 broadcast.12
  288.3 177.9 %while.37 = (s32[]{:T(128)}, f32[2,625,512]{2,1,0:T(8,128)}, f32[125,128]{1,0:T(8,128)}, s32[]{:T(128)}, f32[2,625,512]{2,1,0:T(8,128)}, /*index=5*/f32[2,625,12...) while((s32[]{:T(128)}, f32[2,625,512]{2,1,0:T(8,128)}, f32[125,128]{1,0:T(8,128)}, ...), condition=%wide.region_7.8_spmd, body=%wide.region_4.7_spmd.sunk | while | flops 1440320000 | bytes 12480909 | solution.py:86
  289.6 2.0 collective-permute-done.1
  293.6 2.0 collective-permute-done.1
  297.5 4.1 collective-permute-done.1
  303.6 4.5 collective-permute-done.1
  310.0 4.5 collective-permute-done.1
  316.4 4.5 collective-permute-done.1
  322.8 4.5 collective-permute-done.1
  329.2 55.5 %collective-permute-done.1 = f32[125,128]{1,0:T(8,128)S(1)} collective-permute-done((f32[125,128]{1,0:T(8,128)}, f32[125,128]{1,0:T(8,128)S(1)}, u32[]{:S(2)}, u32[]{:S(2)}) %collective-permute-start.1) | collective-permute-done | bytes 64032 | tf_op jit(solution)/shard_map/while/body/eval_jaxpr/ppermute | solution.py:16
  384.8 15.4 %conditional.5 = (f32[2,625,512]{2,1,0:T(8,128)}, f32[125,128]{1,0:T(8,128)}) conditional(s32[]{:T(128)} %convert_element_type.17, f32[2,625,512]{2,1,0:T(8,128)} %get-tuple-element.520, (s32[]{:T(128)}, f32[2,625,512]{2,1,0:T(8,128)}, f32[2,625,125]{2,1,0:T(8,128)}, f32[125,128]{1,0:T(8,128)S(1)}, f32[2,625,625]{2,1,0:T(8,128)S(1)}, ...), branch_computations={%region_5.5_spmd, %region_6.6_spmd} | conditional | flops 1440320000 | bytes 12224682 | solution.py:83
  386.5 2.4 fusion.13
  388.9 1.8 reshape.17
  396.8 1.8 reshape.18
  401.4 5.3 %collective-permute-done.1 = f32[125,128]{1,0:T(8,128)S(1)} collective-permute-done((f32[125,128]{1,0:T(8,128)}, f32[125,128]{1,0:T(8,128)S(1)}, u32[]{:S(2)}, u32[]{:S(2)}) %collective-permute-start.1) | collective-permute-done | bytes 64032 | tf_op jit(solution)/shard_map/while/body/eval_jaxpr/ppermute | solution.py:16
  406.7 15.3 %conditional.5 = (f32[2,625,512]{2,1,0:T(8,128)}, f32[125,128]{1,0:T(8,128)}) conditional(s32[]{:T(128)} %convert_element_type.17, f32[2,625,512]{2,1,0:T(8,128)} %get-tuple-element.520, (s32[]{:T(128)}, f32[2,625,512]{2,1,0:T(8,128)}, f32[2,625,125]{2,1,0:T(8,128)}, f32[125,128]{1,0:T(8,128)S(1)}, f32[2,625,625]{2,1,0:T(8,128)S(1)}, ...), branch_computations={%region_5.5_spmd, %region_6.6_spmd} | conditional | flops 1440320000 | bytes 12224682 | solution.py:83
  408.4 2.4 fusion.13
  418.7 1.8 reshape.18
  423.3 5.5 %collective-permute-done.1 = f32[125,128]{1,0:T(8,128)S(1)} collective-permute-done((f32[125,128]{1,0:T(8,128)}, f32[125,128]{1,0:T(8,128)S(1)}, u32[]{:S(2)}, u32[]{:S(2)}) %collective-permute-start.1) | collective-permute-done | bytes 64032 | tf_op jit(solution)/shard_map/while/body/eval_jaxpr/ppermute | solution.py:16
  428.8 15.4 %conditional.5 = (f32[2,625,512]{2,1,0:T(8,128)}, f32[125,128]{1,0:T(8,128)}) conditional(s32[]{:T(128)} %convert_element_type.17, f32[2,625,512]{2,1,0:T(8,128)} %get-tuple-element.520, (s32[]{:T(128)}, f32[2,625,512]{2,1,0:T(8,128)}, f32[2,625,125]{2,1,0:T(8,128)}, f32[125,128]{1,0:T(8,128)S(1)}, f32[2,625,625]{2,1,0:T(8,128)S(1)}, ...), branch_computations={%region_5.5_spmd, %region_6.6_spmd} | conditional | flops 1440320000 | bytes 12224682 | solution.py:83
  430.5 2.4 fusion.13
  432.9 1.8 reshape.17
  445.5 5.4 %collective-permute-done.1 = f32[125,128]{1,0:T(8,128)S(1)} collective-permute-done((f32[125,128]{1,0:T(8,128)}, f32[125,128]{1,0:T(8,128)S(1)}, u32[]{:S(2)}, u32[]{:S(2)}) %collective-permute-start.1) | collective-permute-done | bytes 64032 | tf_op jit(solution)/shard_map/while/body/eval_jaxpr/ppermute | solution.py:16
  450.8 15.4 %conditional.5 = (f32[2,625,512]{2,1,0:T(8,128)}, f32[125,128]{1,0:T(8,128)}) conditional(s32[]{:T(128)} %convert_element_type.17, f32[2,625,512]{2,1,0:T(8,128)} %get-tuple-element.520, (s32[]{:T(128)}, f32[2,625,512]{2,1,0:T(8,128)}, f32[2,625,125]{2,1,0:T(8,128)}, f32[125,128]{1,0:T(8,128)S(1)}, f32[2,625,625]{2,1,0:T(8,128)S(1)}, ...), branch_computations={%region_5.5_spmd, %region_6.6_spmd} | conditional | flops 1440320000 | bytes 12224682 | solution.py:83
  452.6 2.4 fusion.13
  466.2 5.8 %copy.21 = f32[2,1,625,512]{3,1,2,0:T(1,128)} copy(f32[2,1,625,512]{3,2,0,1:T(8,128)} %bitcast.134) | data formatting | bytes 5120000 | tf_op jit(solution)/shard_map/broadcast_in_dim | solution.py:108
  (177 shorter events, 137.6 us)
Async XLA Ops:
  3.0 3.6 copy-start.6
  4.3 13.2 %collective-permute-start.2 = (f32[2,125,512]{2,1,0:T(8,128)}, f32[2,125,512]{2,1,0:T(8,128)}, u32[]{:S(2)}, u32[]{:S(2)}) collective-permute-start(f32[2,125,512]{2,1,0:T(8,128)} %copy.16), channel_id=1, source_target_pairs={{0,1},{1,2},{2,3},{3,0},{4,5},{5,6},{6,7},{7,4},{8,9},{9,10},{10,1... | collective-permute-start | bytes 1536008 | tf_op jit(solution)/shard_map/ppermute | solution.py:21
  6.5 22.1 %collective-permute-start.3 = (f32[2,125,512]{2,1,0:T(8,128)}, f32[2,125,512]{2,1,0:T(8,128)}, u32[]{:S(2)}, u32[]{:S(2)}) collective-permute-start(f32[2,125,512]{2,1,0:T(8,128)} %copy.17), channel_id=1, source_target_pairs={{0,3},{1,0},{2,1},{3,2},{4,7},{5,4},{6,5},{7,6},{8,11},{9,8},{10,9... | collective-permute-start | bytes 1536008 | tf_op jit(solution)/shard_map/ppermute | solution.py:21
  6.7 1.1 copy-start.9
  8.6 20.0 %copy-start.4 = (f32[2,1,625,512]{3,1,2,0:T(1,128)S(1)}, f32[2,1,625,512]{3,1,2,0:T(1,128)}, u32[]{:S(2)}) copy-start(f32[2,1,625,512]{3,1,2,0:T(1,128)} %param.14) | copy-start | bytes 7680004
  8.6 20.0 %copy-start.7 = (f32[2,1,625,125]{3,1,2,0:T(1,128)S(1)}, f32[2,1,625,125]{3,1,2,0:T(1,128)}, u32[]{:S(2)}) copy-start(f32[2,1,625,125]{3,1,2,0:T(1,128)} %param.19) | copy-start | bytes 1875004
  36.1 7.9 %collective-permute-start = (f32[125,128]{1,0:T(8,128)}, f32[125,128]{1,0:T(8,128)S(1)}, u32[]{:S(2)}, u32[]{:S(2)}) collective-permute-start(f32[125,128]{1,0:T(8,128)} %get-tuple-element.491), channel_id=1, source_target_pairs={{0,4},{4,8},{8,12},{12,16},{16,20},{20,24},{24,28},{1,5},{5,9},{9,... | collective-permute-start | bytes 192008 | tf_op jit(solution)/shard_map/while/body/eval_jaxpr/ppermute | solution.py:16
  44.6 5.8 %collective-permute-start = (f32[125,128]{1,0:T(8,128)}, f32[125,128]{1,0:T(8,128)S(1)}, u32[]{:S(2)}, u32[]{:S(2)}) collective-permute-start(f32[125,128]{1,0:T(8,128)} %get-tuple-element.491), channel_id=1, source_target_pairs={{0,4},{4,8},{8,12},{12,16},{16,20},{20,24},{24,28},{1,5},{5,9},{9,... | collective-permute-start | bytes 192008 | tf_op jit(solution)/shard_map/while/body/eval_jaxpr/ppermute | solution.py:16
  51.0 5.8 %collective-permute-start = (f32[125,128]{1,0:T(8,128)}, f32[125,128]{1,0:T(8,128)S(1)}, u32[]{:S(2)}, u32[]{:S(2)}) collective-permute-start(f32[125,128]{1,0:T(8,128)} %get-tuple-element.491), channel_id=1, source_target_pairs={{0,4},{4,8},{8,12},{12,16},{16,20},{20,24},{24,28},{1,5},{5,9},{9,... | collective-permute-start | bytes 192008 | tf_op jit(solution)/shard_map/while/body/eval_jaxpr/ppermute | solution.py:16
  57.4 5.8 %collective-permute-start = (f32[125,128]{1,0:T(8,128)}, f32[125,128]{1,0:T(8,128)S(1)}, u32[]{:S(2)}, u32[]{:S(2)}) collective-permute-start(f32[125,128]{1,0:T(8,128)} %get-tuple-element.491), channel_id=1, source_target_pairs={{0,4},{4,8},{8,12},{12,16},{16,20},{20,24},{24,28},{1,5},{5,9},{9,... | collective-permute-start | bytes 192008 | tf_op jit(solution)/shard_map/while/body/eval_jaxpr/ppermute | solution.py:16
  63.8 5.8 %collective-permute-start = (f32[125,128]{1,0:T(8,128)}, f32[125,128]{1,0:T(8,128)S(1)}, u32[]{:S(2)}, u32[]{:S(2)}) collective-permute-start(f32[125,128]{1,0:T(8,128)} %get-tuple-element.491), channel_id=1, source_target_pairs={{0,4},{4,8},{8,12},{12,16},{16,20},{20,24},{24,28},{1,5},{5,9},{9,... | collective-permute-start | bytes 192008 | tf_op jit(solution)/shard_map/while/body/eval_jaxpr/ppermute | solution.py:16
  70.3 5.8 %collective-permute-start = (f32[125,128]{1,0:T(8,128)}, f32[125,128]{1,0:T(8,128)S(1)}, u32[]{:S(2)}, u32[]{:S(2)}) collective-permute-start(f32[125,128]{1,0:T(8,128)} %get-tuple-element.491), channel_id=1, source_target_pairs={{0,4},{4,8},{8,12},{12,16},{16,20},{20,24},{24,28},{1,5},{5,9},{9,... | collective-permute-start | bytes 192008 | tf_op jit(solution)/shard_map/while/body/eval_jaxpr/ppermute | solution.py:16
  76.7 5.8 %collective-permute-start = (f32[125,128]{1,0:T(8,128)}, f32[125,128]{1,0:T(8,128)S(1)}, u32[]{:S(2)}, u32[]{:S(2)}) collective-permute-start(f32[125,128]{1,0:T(8,128)} %get-tuple-element.491), channel_id=1, source_target_pairs={{0,4},{4,8},{8,12},{12,16},{16,20},{20,24},{24,28},{1,5},{5,9},{9,... | collective-permute-start | bytes 192008 | tf_op jit(solution)/shard_map/while/body/eval_jaxpr/ppermute | solution.py:16
  83.1 93.9 %collective-permute-start = (f32[125,128]{1,0:T(8,128)}, f32[125,128]{1,0:T(8,128)S(1)}, u32[]{:S(2)}, u32[]{:S(2)}) collective-permute-start(f32[125,128]{1,0:T(8,128)} %get-tuple-element.491), channel_id=1, source_target_pairs={{0,4},{4,8},{8,12},{12,16},{16,20},{20,24},{24,28},{1,5},{5,9},{9,... | collective-permute-start | bytes 192008 | tf_op jit(solution)/shard_map/while/body/eval_jaxpr/ppermute | solution.py:16
  183.8 4.2 copy-start.2
  187.2 0.7 copy-start
  192.3 6.6 %collective-permute-start = (f32[125,128]{1,0:T(8,128)}, f32[125,128]{1,0:T(8,128)S(1)}, u32[]{:S(2)}, u32[]{:S(2)}) collective-permute-start(f32[125,128]{1,0:T(8,128)} %get-tuple-element.491), channel_id=1, source_target_pairs={{0,4},{4,8},{8,12},{12,16},{16,20},{20,24},{24,28},{1,5},{5,9},{9,... | collective-permute-start | bytes 192008 | tf_op jit(solution)/shard_map/while/body/eval_jaxpr/ppermute | solution.py:16
  205.7 4.2 copy-start.2
  209.2 0.7 copy-start
  214.2 6.8 %collective-permute-start = (f32[125,128]{1,0:T(8,128)}, f32[125,128]{1,0:T(8,128)S(1)}, u32[]{:S(2)}, u32[]{:S(2)}) collective-permute-start(f32[125,128]{1,0:T(8,128)} %get-tuple-element.491), channel_id=1, source_target_pairs={{0,4},{4,8},{8,12},{12,16},{16,20},{20,24},{24,28},{1,5},{5,9},{9,... | collective-permute-start | bytes 192008 | tf_op jit(solution)/shard_map/while/body/eval_jaxpr/ppermute | solution.py:16
  227.8 4.2 copy-start.2
  231.3 0.7 copy-start
  236.3 6.7 %collective-permute-start = (f32[125,128]{1,0:T(8,128)}, f32[125,128]{1,0:T(8,128)S(1)}, u32[]{:S(2)}, u32[]{:S(2)}) collective-permute-start(f32[125,128]{1,0:T(8,128)} %get-tuple-element.491), channel_id=1, source_target_pairs={{0,4},{4,8},{8,12},{12,16},{16,20},{20,24},{24,28},{1,5},{5,9},{9,... | collective-permute-start | bytes 192008 | tf_op jit(solution)/shard_map/while/body/eval_jaxpr/ppermute | solution.py:16
  249.9 4.2 copy-start.2
  253.3 0.7 copy-start
  263.3 14.0 %collective-permute-start.4 = (f32[2,125,512]{2,1,0:T(8,128)}, f32[2,125,512]{2,1,0:T(8,128)}, u32[]{:S(2)}, u32[]{:S(2)}) collective-permute-start(f32[2,125,512]{2,1,0:T(8,128)} %copy.19), channel_id=1, source_target_pairs={{0,1},{1,2},{2,3},{3,0},{4,5},{5,6},{6,7},{7,4},{8,9},{9,10},{10,1... | collective-permute-start | bytes 1536008 | tf_op jit(solution)/shard_map/ppermute | solution.py:21
  265.5 15.3 %collective-permute-start.5 = (f32[2,125,512]{2,1,0:T(8,128)}, f32[2,125,512]{2,1,0:T(8,128)}, u32[]{:S(2)}, u32[]{:S(2)}) collective-permute-start(f32[2,125,512]{2,1,0:T(8,128)} %copy.20), channel_id=1, source_target_pairs={{0,3},{1,0},{2,1},{3,2},{4,7},{5,4},{6,5},{7,6},{8,11},{9,8},{10,9... | collective-permute-start | bytes 1536008 | tf_op jit(solution)/shard_map/ppermute | solution.py:21
  265.7 15.1 %copy-start.5 = (f32[2,1,625,512]{3,1,2,0:T(1,128)S(1)}, f32[2,1,625,512]{3,1,2,0:T(1,128)}, u32[]{:S(2)}) copy-start(f32[2,1,625,512]{3,1,2,0:T(1,128)} %param.14) | copy-start | bytes 7680004
  265.7 15.1 %copy-start.8 = (f32[2,1,625,125]{3,1,2,0:T(1,128)S(1)}, f32[2,1,625,125]{3,1,2,0:T(1,128)}, u32[]{:S(2)}) copy-start(f32[2,1,625,125]{3,1,2,0:T(1,128)} %param.19) | copy-start | bytes 1875004
  288.3 3.3 collective-permute-start.1
  292.3 3.3 collective-permute-start.1
  296.2 5.4 %collective-permute-start.1 = (f32[125,128]{1,0:T(8,128)}, f32[125,128]{1,0:T(8,128)S(1)}, u32[]{:S(2)}, u32[]{:S(2)}) collective-permute-start(f32[125,128]{1,0:T(8,128)} %get-tuple-element.521), channel_id=1, source_target_pairs={{0,4},{4,8},{8,12},{12,16},{16,20},{20,24},{24,28},{1,5},{5,9},{9,... | collective-permute-start | bytes 192008 | tf_op jit(solution)/shard_map/while/body/eval_jaxpr/ppermute | solution.py:16
  302.3 5.8 %collective-permute-start.1 = (f32[125,128]{1,0:T(8,128)}, f32[125,128]{1,0:T(8,128)S(1)}, u32[]{:S(2)}, u32[]{:S(2)}) collective-permute-start(f32[125,128]{1,0:T(8,128)} %get-tuple-element.521), channel_id=1, source_target_pairs={{0,4},{4,8},{8,12},{12,16},{16,20},{20,24},{24,28},{1,5},{5,9},{9,... | collective-permute-start | bytes 192008 | tf_op jit(solution)/shard_map/while/body/eval_jaxpr/ppermute | solution.py:16
  308.7 5.8 %collective-permute-start.1 = (f32[125,128]{1,0:T(8,128)}, f32[125,128]{1,0:T(8,128)S(1)}, u32[]{:S(2)}, u32[]{:S(2)}) collective-permute-start(f32[125,128]{1,0:T(8,128)} %get-tuple-element.521), channel_id=1, source_target_pairs={{0,4},{4,8},{8,12},{12,16},{16,20},{20,24},{24,28},{1,5},{5,9},{9,... | collective-permute-start | bytes 192008 | tf_op jit(solution)/shard_map/while/body/eval_jaxpr/ppermute | solution.py:16
  315.1 5.8 %collective-permute-start.1 = (f32[125,128]{1,0:T(8,128)}, f32[125,128]{1,0:T(8,128)S(1)}, u32[]{:S(2)}, u32[]{:S(2)}) collective-permute-start(f32[125,128]{1,0:T(8,128)} %get-tuple-element.521), channel_id=1, source_target_pairs={{0,4},{4,8},{8,12},{12,16},{16,20},{20,24},{24,28},{1,5},{5,9},{9,... | collective-permute-start | bytes 192008 | tf_op jit(solution)/shard_map/while/body/eval_jaxpr/ppermute | solution.py:16
  321.5 5.8 %collective-permute-start.1 = (f32[125,128]{1,0:T(8,128)}, f32[125,128]{1,0:T(8,128)S(1)}, u32[]{:S(2)}, u32[]{:S(2)}) collective-permute-start(f32[125,128]{1,0:T(8,128)} %get-tuple-element.521), channel_id=1, source_target_pairs={{0,4},{4,8},{8,12},{12,16},{16,20},{20,24},{24,28},{1,5},{5,9},{9,... | collective-permute-start | bytes 192008 | tf_op jit(solution)/shard_map/while/body/eval_jaxpr/ppermute | solution.py:16
  327.9 56.8 %collective-permute-start.1 = (f32[125,128]{1,0:T(8,128)}, f32[125,128]{1,0:T(8,128)S(1)}, u32[]{:S(2)}, u32[]{:S(2)}) collective-permute-start(f32[125,128]{1,0:T(8,128)} %get-tuple-element.521), channel_id=1, source_target_pairs={{0,4},{4,8},{8,12},{12,16},{16,20},{20,24},{24,28},{1,5},{5,9},{9,... | collective-permute-start | bytes 192008 | tf_op jit(solution)/shard_map/while/body/eval_jaxpr/ppermute | solution.py:16
  391.6 4.2 copy-start.3
  395.1 0.7 copy-start.1
  400.1 6.6 %collective-permute-start.1 = (f32[125,128]{1,0:T(8,128)}, f32[125,128]{1,0:T(8,128)S(1)}, u32[]{:S(2)}, u32[]{:S(2)}) collective-permute-start(f32[125,128]{1,0:T(8,128)} %get-tuple-element.521), channel_id=1, source_target_pairs={{0,4},{4,8},{8,12},{12,16},{16,20},{20,24},{24,28},{1,5},{5,9},{9,... | collective-permute-start | bytes 192008 | tf_op jit(solution)/shard_map/while/body/eval_jaxpr/ppermute | solution.py:16
  413.6 4.2 copy-start.3
  417.0 0.7 copy-start.1
  422.0 6.8 %collective-permute-start.1 = (f32[125,128]{1,0:T(8,128)}, f32[125,128]{1,0:T(8,128)S(1)}, u32[]{:S(2)}, u32[]{:S(2)}) collective-permute-start(f32[125,128]{1,0:T(8,128)} %get-tuple-element.521), channel_id=1, source_target_pairs={{0,4},{4,8},{8,12},{12,16},{16,20},{20,24},{24,28},{1,5},{5,9},{9,... | collective-permute-start | bytes 192008 | tf_op jit(solution)/shard_map/while/body/eval_jaxpr/ppermute | solution.py:16
  435.7 4.2 copy-start.3
  439.1 0.7 copy-start.1
  444.2 6.7 %collective-permute-start.1 = (f32[125,128]{1,0:T(8,128)}, f32[125,128]{1,0:T(8,128)S(1)}, u32[]{:S(2)}, u32[]{:S(2)}) collective-permute-start(f32[125,128]{1,0:T(8,128)} %get-tuple-element.521), channel_id=1, source_target_pairs={{0,4},{4,8},{8,12},{12,16},{16,20},{20,24},{24,28},{1,5},{5,9},{9,... | collective-permute-start | bytes 192008 | tf_op jit(solution)/shard_map/while/body/eval_jaxpr/ppermute | solution.py:16
  457.7 4.2 copy-start.3
  461.1 0.7 copy-start.1
where the time goes:
time: 474 us; the launch traced here: 472 us
  waiting for transfers between devices  268 us (57%)
  local copies, waits for them, and re-layouts  87 us (18%)
  matrix products  77.2 us (16%)
  starting transfers between devices  31.1 us (7%)
  other arithmetic  7.71 us (2%)
    ppermute x22, waiting for transfers between devices, passed_along(): return lax.ppermute(shard, axis, pairs)  240 us
    dot_general x32, matrix products, product(): jnp.dot(matrix, vectors, precision=lax.Precision.HIGHEST, preferred_eleme...  60.2 us
    reshape x16, local copies, waits for them, and re-layouts, face_grid(): return field.reshape(leading + (VARS, NODE, NODE, NODE, field.shape[-1]))  29.4 us
    ppermute x22, starting transfers between devices, passed_along(): return lax.ppermute(shard, axis, pairs)  28.2 us
    ppermute x4, waiting for transfers between devices, from_behind(): lax.ppermute(shard, axis, [(i, (i + by) % count) for i in range(count)])  28.1 us
    cond x48, local copies, waits for them, and re-layouts  20.1 us
    dot_general x4, matrix products, batched_product(): jnp.einsum('eab,ebr->ear', matrix, vectors, precision=lax.Precision.HIGHEST)  17 us
    another operation x18, local copies, waits for them, and re-layouts  13.6 us
  transfers between devices with their start and end apart: 26, of which 25 were waited for; matrix products, arithmetic and copies ran while one was open for 2% of the time, Pallas kernels for 0%

commit v1 on v0

v1 whole, which is shorter than its diff:
```python
import functools

import jax
import jax.numpy as jnp
from jax import lax
from jax.experimental import pallas as pl
from jax.experimental.pallas import tpu as pltpu
from jax.sharding import PartitionSpec as P

VARS = 5
NODE = 5
SWEEPS = 2
CORES = 2
LIMIT = 32 * 1024 * 1024


def face_runs(kind):
    if kind == "down":
        return [
            (var * NODE**3 + (NODE - 1) * NODE**2, NODE**2) for var in range(VARS)
        ]
    b = NODE - 1 if kind == "high" else 0
    return [
        (var * NODE**3 + a * NODE**2 + b * NODE, NODE)
        for var in range(VARS)
        for a in range(NODE)
    ]


def face_size():
    return VARS * NODE**2


def padded(size):
    return -(-size // 128) * 128


def take_face(kind, read, write):
    at = 0
    for first, length in face_runs(kind):
        write(at, length, read(first, length))
        at += length


def split(x):
    top = x.astype(jnp.bfloat16)
    return top, (x - top.astype(jnp.float32)).astype(jnp.bfloat16)


def mul(a, b):
    ah, al = a if isinstance(a, tuple) else split(a)
    bh, bl = b if isinstance(b, tuple) else split(b)
    dot = functools.partial(jnp.dot, preferred_element_type=jnp.float32)
    return dot(ah, bh) + (dot(ah, bl) + dot(al, bh))


def call(kernel, outs, *args, scratch=(), smem=0, name=None):
    return pl.pallas_call(
        kernel,
        out_shape=[jax.ShapeDtypeStruct(s, jnp.float32) for s in outs],
        in_specs=[pl.BlockSpec(memory_space=pltpu.SMEM)] * smem
        + [pl.BlockSpec(memory_space=pltpu.VMEM)] * (len(args) - smem),
        out_specs=[pl.BlockSpec(memory_space=pltpu.VMEM)] * len(outs),
        scratch_shapes=list(scratch),
        compiler_params=pltpu.CompilerParams(vmem_limit_bytes=LIMIT),
        name=name,
    )(*args)


def start_faces(field_ref, high_ref, low_ref):
    face = face_size()
    for e in range(field_ref.shape[0]):
        for kind, out in (("high", high_ref), ("low", low_ref)):
            out[e, face:, :] = jnp.zeros((out.shape[1] - face, out.shape[2]), jnp.float32)
            at = 0
            for first, length in face_runs(kind):
                out[e, at : at + length, :] = field_ref[e, first : first + length, :]
                at += length


def fold_blocks(inv_ref, rhs_ref, up_ref, south_ref, north_ref,
                c_ref, b_ref, fc_ref, fb_ref, resp_ref, step_ref):
    face = face_size()
    wide = padded(face)
    elements = inv_ref.shape[0]
    for e in range(elements):
        inverse = split(inv_ref[e])
        c_ref[e] = mul(inverse, rhs_ref[e])
        b_ref[e] = jnp.zeros(b_ref.shape[1:], jnp.float32)
        for k, block in enumerate((south_ref, north_ref, up_ref)):
            b_ref[e, :, k * wide : k * wide + face] = mul(inverse, block[e])
        fc_ref[e] = jnp.zeros(fc_ref.shape[1:], jnp.float32)
        fb_ref[e] = jnp.zeros(fb_ref.shape[1:], jnp.float32)
        for f, kind in enumerate(("down", "high", "low")):
            at = f * wide
            for first, length in face_runs(kind):
                fc_ref[e, at : at + length, :] = c_ref[e, first : first + length, :]
                fb_ref[e, at : at + length, :] = b_ref[e, first : first + length, :]
                at += length
        own = fb_ref[e, :, 2 * wide :]
        if e == 0:
            resp_ref[e] = -own
        else:
            resp_ref[e] = -mul(own, resp_ref[e - 1, :wide, :])
    step_ref[...] = resp_ref[elements - 1, :wide, :]


def faces_without_inflow(rows, fc_ref, fb_ref, s_ref, n_ref, q_ref, g_ref):
    wide = s_ref.shape[1]
    elements = fc_ref.shape[0]
    for e in range(elements):
        q = fc_ref[e, :rows, :] - (
            mul(fb_ref[e, :rows, :wide], s_ref[e])
            + mul(fb_ref[e, :rows, wide : 2 * wide], n_ref[e])
        )
        if e:
            q = q - mul(fb_ref[e, :rows, 2 * wide :], q_ref[e - 1, :wide, :])
        q_ref[e] = q
    g_ref[...] = q_ref[elements - 1, :wide, :]


def pair_trace(core_ref, own_ref, other_ref, steps_ref, first_ref, chip_ref):
    half = other_ref.shape[1]
    chip = core_ref[1]

    @pl.when(core_ref[0] == 0)
    def _():
        first_ref[...] = own_ref[:, :half]
        chip_ref[...] = other_ref[...]

    @pl.when(core_ref[0] == 1)
    def _():
        first_ref[...] = other_ref[...]
        chip_ref[...] = own_ref[:, half:]

    chip_ref[...] += mul(steps_ref[2 * chip + 1], first_ref[...])


def inflow_of_cores(core_ref, first_ref, chips_ref, steps_ref, keep_ref, send_ref):
    chip = core_ref[1]
    keep_ref[...] = jnp.zeros_like(keep_ref)
    for m in range(chips_ref.shape[0] - 1):

        @pl.when(m < chip)
        def _():
            passed = mul(steps_ref[2 * m], keep_ref[...])
            keep_ref[...] = chips_ref[m] + mul(steps_ref[2 * m + 1], passed)

    send_ref[...] = first_ref[...] + mul(steps_ref[2 * chip], keep_ref[...])

    @pl.when(core_ref[0] == 1)
    def _():
        held = keep_ref[...]
        keep_ref[...] = send_ref[...]
        send_ref[...] = held


def join(core_ref, keep_ref, got_ref, inflow_ref):
    half = keep_ref.shape[1]

    @pl.when(core_ref[0] == 0)
    def _():
        inflow_ref[:, :half] = keep_ref[...]
        inflow_ref[:, half:] = got_ref[...]

    @pl.when(core_ref[0] == 1)
    def _():
        inflow_ref[:, :half] = got_ref[...]
        inflow_ref[:, half:] = keep_ref[...]


def next_faces(core_ref, q_ref, resp_ref, keep_ref, got_ref, high_ref, low_ref, inflow_ref):
    join(core_ref, keep_ref, got_ref, inflow_ref)
    wide = inflow_ref.shape[0]
    inflow = split(inflow_ref[...])
    for e in range(q_ref.shape[0]):
        high_ref[e] = q_ref[e, wide : 2 * wide, :] + mul(resp_ref[e, wide : 2 * wide, :], inflow)
        low_ref[e] = q_ref[e, 2 * wide :, :] + mul(resp_ref[e, 2 * wide :, :], inflow)


def whole_field(core_ref, c_ref, b_ref, s_ref, n_ref, keep_ref, got_ref, out_ref, inflow_ref):
    join(core_ref, keep_ref, got_ref, inflow_ref)
    wide = inflow_ref.shape[0]
    for e in range(c_ref.shape[0]):
        if e:
            at = 0
            for first, length in face_runs("down"):
                inflow_ref[at : at + length, :] = out_ref[e - 1, first : first + length, :]
                at += length
        out_ref[e] = c_ref[e] - (
            mul(b_ref[e, :, :wide], s_ref[e])
            + mul(b_ref[e, :, wide : 2 * wide], n_ref[e])
            + mul(b_ref[e, :, 2 * wide :], inflow_ref[...])
        )


def ring(axis, by):
    count = lax.axis_size(axis)
    return [(i, (i + by) % count) for i in range(count)]


def per_device(right_side, start_field, block_inverse, upwind_block, south_block, north_block):
    rhs, start = right_side[:, 0], start_field[:, 0]
    inverse, upwind = block_inverse[:, 0], upwind_block[:, 0]
    south, north = south_block[:, 0], north_block[:, 0]
    elements, unknowns, columns = rhs.shape
    wide = padded(face_size())
    half = columns // CORES
    devices = lax.axis_size("sweep")
    place = lax.axis_index("sweep")
    where = jnp.stack([place % CORES, place // CORES]).astype(jnp.int32)
    swap = [(i, i ^ 1) for i in range(devices)]
    like = [[c + CORES * k for k in range(devices // CORES)] for c in range(CORES)]
    trace = (elements, wide, columns)

    high, low = call(start_faces, [trace, trace], start, name="start_faces")
    for sweep_no in range(SWEEPS):
        last = sweep_no == SWEEPS - 1
        below = lax.ppermute(high, "span", ring("span", 1))
        above = lax.ppermute(low, "span", ring("span", -1))
        if sweep_no == 0:
            c, b, fc, fb, resp, step = call(
                fold_blocks,
                [
                    (elements, unknowns, columns),
                    (elements, unknowns, 3 * wide),
                    (elements, 3 * wide, columns),
                    (elements, 3 * wide, 3 * wide),
                    (elements, 3 * wide, wide),
                    (wide, wide),
                ],
                inverse, rhs, upwind, south, north,
                name="fold_blocks",
            )
            steps = lax.all_gather(step, "sweep")
        rows = wide if last else 3 * wide
        q, g = call(
            functools.partial(faces_without_inflow, rows),
            [(elements, rows, columns), (wide, columns)],
            fc, fb, below, above,
            name="faces_without_inflow",
        )
        away = lax.dynamic_slice_in_dim(g, (1 - place % CORES) * half, half, 1)
        other = lax.ppermute(away, "sweep", swap)
        first, chip = call(
            pair_trace, [(wide, half)] * 2, where, g, other, steps, smem=1, name="pair_trace"
        )
        chips = lax.all_gather(chip, "sweep", axis_index_groups=like)
        keep, send = call(
            inflow_of_cores, [(wide, half)] * 2, where, first, chips, steps, smem=1,
            name="inflow_of_cores",
        )
        got = lax.ppermute(send, "sweep", swap)
        held = [pltpu.VMEM((wide, columns), jnp.float32)]
        if not last:
            high, low = call(
                next_faces, [trace, trace], where, q, resp, keep, got,
                smem=1, scratch=held, name="next_faces",
            )
        else:
            (field,) = call(
                whole_field, [(elements, unknowns, columns)],
                where, c, b, below, above, keep, got,
                smem=1, scratch=held, name="whole_field",
            )
    return field[:, None]


def solution(mesh):
    spec = P("sweep", "span", None, None)
    return jax.shard_map(
        per_device, mesh=mesh, in_specs=(spec,) * 6, out_specs=spec, check_vma=False
    )
```

time: 474 us -> 109 us (0.23)
  the two profiles are of different devices: /device:TPU:23 before, /device:TPU:1 now
where the time goes in v1:
time: 109 us; the launch traced here: 108 us
  waiting for transfers between devices  30.6 us (28%)
  blocking collectives  27.8 us (26%)
  Pallas kernels  21.9 us (20%)
  local copies, waits for them, and re-layouts  14.6 us (13%)
  starting transfers between devices  13.4 us (12%)
    pallas_call x10, Pallas kernels, call(): pl.pallas_call(kernel, out_shape=[jax.ShapeDtypeStruct(s, jnp.float32) fo...  21.9 us
    all_gather x2, blocking collectives, per_device(): chips = lax.all_gather(chip, 'sweep', axis_index_groups=like)  18.1 us
    ppermute x2, waiting for transfers between devices, per_device(): above = lax.ppermute(low, 'span', ring('span', -1))  15.9 us
    ppermute x2, waiting for transfers between devices, per_device(): below = lax.ppermute(high, 'span', ring('span', 1))  11.7 us
    unnamed x13, local copies, waits for them, and re-layouts  10.5 us
    all_gather x1, blocking collectives, per_device(): steps = lax.all_gather(step, 'sweep')  9.71 us
    ppermute x2, starting transfers between devices, per_device(): above = lax.ppermute(low, 'span', ring('span', -1))  4.44 us
    broadcast_in_dim x1, local copies, waits for them, and re-layouts, per_device(): return field[:, None]  4.1 us
  transfers between devices with their start and end apart: 8, of which 6 were waited for; matrix products, arithmetic and copies ran while one was open for 6% of the time, Pallas kernels for 8%

profile of v1, /device:TPU:1, one launch (start us, length us, event | category | flops | bytes accessed | tf_op | source)
XLA Modules:
  0.0 108.4 jit_solution(2741837756743844023)
XLA Ops:
  0.0 2.0 %copy.22 = f32[2,1,625,512]{3,2,1,0:T(8,128)S(1)} copy(f32[2,1,625,512]{3,1,2,0:T(1,128)} %param.7) | data formatting | bytes 5120000
  2.0 1.2 %start_faces.1 = (f32[2,128,512]{2,1,0:T(8,128)}, f32[2,128,512]{2,1,0:T(8,128)}) custom-call(f32[2,625,512]{2,1,0:T(8,128)S(1)} %bitcast.28), custom_call_target="tpu_custom_call" | custom-call | tf_op jit(solution)/shard_map/start_faces/pallas_call | solution.py:58
  3.2 2.1 %collective-permute-start = (f32[2,128,512]{2,1,0:T(8,128)}, f32[2,128,512]{2,1,0:T(8,128)}, u32[]{:S(2)}, u32[]{:S(2)}) collective-permute-start(f32[2,128,512]{2,1,0:T(8,128)} %get-tuple-element.30), channel_id=1, source_target_pairs={{0,1},{1,2},{2,3},{3,0},{4,5},{5,6},{6,7},{7,4},{8,9},{9,10},{10,1... | collective-permute-start | bytes 1572872 | tf_op jit(solution)/shard_map/ppermute | solution.py:219
  5.3 2.0 %collective-permute-start.1 = (f32[2,128,512]{2,1,0:T(8,128)}, f32[2,128,512]{2,1,0:T(8,128)}, u32[]{:S(2)}, u32[]{:S(2)}) collective-permute-start(f32[2,128,512]{2,1,0:T(8,128)} %get-tuple-element.31), channel_id=1, source_target_pairs={{0,3},{1,0},{2,1},{3,2},{4,7},{5,4},{6,5},{7,6},{8,11},{9,8},{10,9... | collective-permute-start | bytes 1572872 | tf_op jit(solution)/shard_map/ppermute | solution.py:220
  7.3 0.0 copy-start.2
  7.3 2.3 %copy.21 = f32[2,1,625,625]{3,2,1,0:T(8,128)S(1)} copy(f32[2,1,625,625]{3,1,2,0:T(1,128)} %param.8) | data formatting | bytes 6250000
  9.6 0.4 copy-done.2
  10.0 0.0 copy-start.3
  10.0 1.8 %copy.23 = f32[2,1,625,512]{3,2,1,0:T(8,128)} copy(f32[2,1,625,512]{3,1,2,0:T(1,128)S(1)} %copy-done.2) | data formatting | bytes 5120000
  11.8 0.0 copy-done.3
  11.8 0.9 copy.24
  12.6 0.0 copy-start.1
  12.7 1.4 %copy_bitcast_fusion.3 = (f32[2,625,125]{2,1,0:T(8,128)S(1)}, f32[2,625,125]{2,1,0:T(8,128)S(1)}) fusion(f32[2,1,625,125]{3,1,2,0:T(1,128)} %param.11, f32[2,1,625,125]{3,1,2,0:T(1,128)} %param.10), kind=kLoop, calls=%fused_computation.3 | loop fusion | bytes 2500000
  14.1 0.0 copy-done.1
  14.1 0.0 copy-start
  14.1 1.7 %copy-done = f32[2,1,625,512]{3,2,1,0:T(8,128)S(1)} copy-done((f32[2,1,625,512]{3,2,1,0:T(8,128)S(1)}, f32[2,1,625,512]{3,2,1,0:T(8,128)}, u32[]{:S(2)}) %copy-start) | copy-done | bytes 2560024
  15.8 8.3 %fold_blocks.1 = (f32[2,625,512]{2,1,0:T(8,128)S(1)}, f32[2,625,384]{2,1,0:T(8,128)S(1)}, f32[2,384,512]{2,1,0:T(8,128)S(1)}, f32[2,384,384]{2,1,0:T(8,128)S(1)}...) custom-call(f32[2,625,625]{2,1,0:T(8,128)S(1)} %bitcast.26, f32[2,625,512]{2,1,0:T(8,128)S(1)} %bitcast.29, ...), custom_call_target="tpu_custom_call" | custom-call | tf_op jit(solution)/shard_map/fold_blocks/pallas_call | solution.py:58
  24.2 0.0 collective-permute-done.s_ref
  24.2 5.9 %collective-permute-done.1.n_ref = f32[2,128,512]{2,1,0:T(8,128)} collective-permute-done((f32[2,128,512]{2,1,0:T(8,128)}, f32[2,128,512]{2,1,0:T(8,128)}, u32[]{:S(2)}, u32[]{:S(2)}) %collective-permute-start.1) | collective-permute-done | bytes 524320 | tf_op jit(solution)/shard_map/ppermute | solution.py:220
  30.1 2.9 %faces_without_inflow.2 = (f32[2,384,512]{2,1,0:T(8,128)S(1)}, f32[128,512]{1,0:T(8,128)S(1)}) custom-call(f32[2,384,512]{2,1,0:T(8,128)S(1)} %get-tuple-element.28.fc_ref, f32[2,384,384]{2,1,0:T(8,128)S(1)} %get-tuple-element.29.fb_ref, f32[2,128,512]{2,1,0:T(8,128)} %collective-permute-done.s_ref, f32[2,128,512]{2,1,0:T(8,128)} %collective-permute-done.1.n_ref), custom_call_target="tpu_custom_call" | custom-call | tf_op jit(solution)/shard_map/faces_without_inflow/pallas_call | solution.py:58
  33.0 1.2 %collective-permute-start.2 = (f32[128,256]{1,0:T(8,128)S(1)}, f32[128,256]{1,0:T(8,128)S(1)}, u32[]{:S(2)}, u32[]{:S(2)}) collective-permute-start(f32[128,256]{1,0:T(8,128)S(1)} %constant_dynamic-slice_fusion.1), channel_id=1, source_target_pairs={{0,4},{4,0},{8,12},{12,8},{16,20},{20,16},{24,28},{28,24},{1,5},{5... | collective-permute-start | bytes 393224 | tf_op jit(solution)/shard_map/ppermute | solution.py:244
  34.2 0.1 pad_add_fusion.core_ref
  34.3 9.7 %all-gather = f32[1024,128]{1,0:T(8,128)S(1)} all-gather(f32[128,128]{1,0:T(8,128)S(1)} %get-tuple-element.35), channel_id=2, replica_groups=mesh['sweep'=8,'span'=4] {'sweep'}, dimensions={0}, use_global_device_ids=true | all-gather | bytes 589824 | tf_op jit(solution)/shard_map/all_gather | solution.py:235
  44.0 0.0 collective-permute-done.2.other_ref
  44.0 0.8 pair_trace.2
  44.8 9.0 %all-gather.1 = f32[512,256]{1,0:T(8,128)S(1)} all-gather(f32[128,256]{1,0:T(8,128)S(1)} %get-tuple-element.37), channel_id=3, replica_groups={{0,8,16,24},{4,12,20,28},{1,9,17,25},{5,13,21,29},{2,10,18,26},{6,14,22..., dimensions={0}, use_global_device_ids=true | all-gather | bytes 655360 | tf_op jit(solution)/shard_map/all_gather | solution.py:248
  53.7 0.8 inflow_of_cores.2
  54.5 1.6 %collective-permute-start.3 = (f32[128,256]{1,0:T(8,128)S(1)}, f32[128,256]{1,0:T(8,128)S(1)}, u32[]{:S(2)}, u32[]{:S(2)}) collective-permute-start(f32[128,256]{1,0:T(8,128)S(1)} %get-tuple-element.39), channel_id=1, source_target_pairs={{0,4},{4,0},{8,12},{12,8},{16,20},{20,16},{24,28},{28,24},{1,5},{5... | collective-permute-start | bytes 393224 | tf_op jit(solution)/shard_map/ppermute | solution.py:253
  56.1 1.0 collective-permute-done.3.got_ref
  57.1 1.1 %next_faces.1 = (f32[2,128,512]{2,1,0:T(8,128)S(1)}, f32[2,128,512]{2,1,0:T(8,128)S(1)}) custom-call(s32[2]{0:T(128)S(1)} %pad_add_fusion.core_ref, f32[2,384,512]{2,1,0:T(8,128)S(1)} %get-tuple-element.32.q_ref, f32[2,384,128]{2,1,0:T(8,128)S(1)} %get-tuple-element.33.resp_ref, f32[128,256]{1,0:T(8,128)S(1)} %get-tuple-element.38.keep_ref, ...), custom_call_target="tpu_custom_call" | custom-call | tf_op jit(solution)/shard_map/next_faces/pallas_call | solution.py:58
  58.3 0.9 collective-permute-start.4
  59.2 2.4 %collective-permute-start.5 = (f32[2,128,512]{2,1,0:T(8,128)S(1)}, f32[2,128,512]{2,1,0:T(8,128)S(1)}, u32[]{:S(2)}, u32[]{:S(2)}) collective-permute-start(f32[2,128,512]{2,1,0:T(8,128)S(1)} %get-tuple-element.41), channel_id=1, source_target_pairs={{0,3},{1,0},{2,1},{3,2},{4,7},{5,4},{6,5},{7,6},{8,11},{9,8},{10,9... | collective-permute-start | bytes 1572872 | tf_op jit(solution)/shard_map/ppermute | solution.py:220
  61.6 11.7 %collective-permute-done.4.s_ref = f32[2,128,512]{2,1,0:T(8,128)S(1)} collective-permute-done((f32[2,128,512]{2,1,0:T(8,128)S(1)}, f32[2,128,512]{2,1,0:T(8,128)S(1)}, u32[]{:S(2)}, u32[]{:S(2)}) %collective-permute-start.4) | collective-permute-done | bytes 524320 | tf_op jit(solution)/shard_map/ppermute | solution.py:219
  73.3 10.0 %collective-permute-done.5.n_ref = f32[2,128,512]{2,1,0:T(8,128)S(1)} collective-permute-done((f32[2,128,512]{2,1,0:T(8,128)S(1)}, f32[2,128,512]{2,1,0:T(8,128)S(1)}, u32[]{:S(2)}, u32[]{:S(2)}) %collective-permute-start.5) | collective-permute-done | bytes 524320 | tf_op jit(solution)/shard_map/ppermute | solution.py:220
  83.3 1.5 %faces_without_inflow.3 = (f32[2,128,512]{2,1,0:T(8,128)}, f32[128,512]{1,0:T(8,128)S(1)}) custom-call(f32[2,384,512]{2,1,0:T(8,128)S(1)} %get-tuple-element.28.fc_ref, f32[2,384,384]{2,1,0:T(8,128)S(1)} %get-tuple-element.29.fb_ref, f32[2,128,512]{2,1,0:T(8,128)S(1)} %collective-permute-done.4.s_ref, f32[2,128,512]{2,1,0:T(8,128)S(1)} %collective-permute-done.5.n_ref), custom_call_target="tpu_custom_call" | custom-call | tf_op jit(solution)/shard_map/faces_without_inflow/pallas_call | solution.py:58
  84.8 1.5 %collective-permute-start.6 = (f32[128,256]{1,0:T(8,128)S(1)}, f32[128,256]{1,0:T(8,128)S(1)}, u32[]{:S(2)}, u32[]{:S(2)}) collective-permute-start(f32[128,256]{1,0:T(8,128)S(1)} %constant_dynamic-slice_fusion), channel_id=1, source_target_pairs={{0,4},{4,0},{8,12},{12,8},{16,20},{20,16},{24,28},{28,24},{1,5},{5... | collective-permute-start | bytes 393224 | tf_op jit(solution)/shard_map/ppermute | solution.py:244
  86.3 1.0 collective-permute-done.6.other_ref
  87.3 0.8 pair_trace.3
  88.1 9.1 %all-gather.2 = f32[512,256]{1,0:T(8,128)S(1)} all-gather(f32[128,256]{1,0:T(8,128)S(1)} %get-tuple-element.44), channel_id=4, replica_groups={{0,8,16,24},{4,12,20,28},{1,9,17,25},{5,13,21,29},{2,10,18,26},{6,14,22..., dimensions={0}, use_global_device_ids=true | all-gather | bytes 655360 | tf_op jit(solution)/shard_map/all_gather | solution.py:248
  97.1 0.8 inflow_of_cores.3
  97.9 1.6 %collective-permute-start.7 = (f32[128,256]{1,0:T(8,128)S(1)}, f32[128,256]{1,0:T(8,128)S(1)}, u32[]{:S(2)}, u32[]{:S(2)}) collective-permute-start(f32[128,256]{1,0:T(8,128)S(1)} %get-tuple-element.46), channel_id=1, source_target_pairs={{0,4},{4,0},{8,12},{12,8},{16,20},{20,16},{24,28},{28,24},{1,5},{5... | collective-permute-start | bytes 393224 | tf_op jit(solution)/shard_map/ppermute | solution.py:253
  99.5 1.0 collective-permute-done.7.got_ref
  100.5 3.8 %whole_field.1 = f32[2,625,512]{2,1,0:T(8,128)S(1)} custom-call(s32[2]{0:T(128)S(1)} %pad_add_fusion.core_ref, f32[2,625,512]{2,1,0:T(8,128)S(1)} %get-tuple-element.26.c_ref, f32[2,625,384]{2,1,0:T(8,128)S(1)} %get-tuple-element.27.b_ref, f32[2,128,512]{2,1,0:T(8,128)S(1)} %collective-permute-done.4.s_ref, f32[2,128,512]{2,1,0:T(8,128)S(1)} %collective-permute-done.5.n_ref, ...), custom_call_target="tpu_custom_call" | custom-call | tf_op jit(solution)/shard_map/whole_field/pallas_call | solution.py:58
  104.3 4.1 %copy.8 = f32[2,1,625,512]{3,1,2,0:T(1,128)} copy(f32[2,1,625,512]{3,2,0,1:T(8,128)S(1)} %bitcast.27) | data formatting | bytes 5120000 | tf_op jit(solution)/shard_map/broadcast_in_dim | solution.py:266
  (2 shorter events, 0.0 us)
Async XLA Ops:
  3.2 21.0 %collective-permute-start = (f32[2,128,512]{2,1,0:T(8,128)}, f32[2,128,512]{2,1,0:T(8,128)}, u32[]{:S(2)}, u32[]{:S(2)}) collective-permute-start(f32[2,128,512]{2,1,0:T(8,128)} %get-tuple-element.30), channel_id=1, source_target_pairs={{0,1},{1,2},{2,3},{3,0},{4,5},{5,6},{6,7},{7,4},{8,9},{9,10},{10,1... | collective-permute-start | bytes 1572872 | tf_op jit(solution)/shard_map/ppermute | solution.py:219
  5.3 24.8 %collective-permute-start.1 = (f32[2,128,512]{2,1,0:T(8,128)}, f32[2,128,512]{2,1,0:T(8,128)}, u32[]{:S(2)}, u32[]{:S(2)}) collective-permute-start(f32[2,128,512]{2,1,0:T(8,128)} %get-tuple-element.31), channel_id=1, source_target_pairs={{0,3},{1,0},{2,1},{3,2},{4,7},{5,4},{6,5},{7,6},{8,11},{9,8},{10,9... | collective-permute-start | bytes 1572872 | tf_op jit(solution)/shard_map/ppermute | solution.py:220
  7.3 2.7 %copy-start.2 = (f32[2,1,625,512]{3,1,2,0:T(1,128)S(1)}, f32[2,1,625,512]{3,1,2,0:T(1,128)}, u32[]{:S(2)}) copy-start(f32[2,1,625,512]{3,1,2,0:T(1,128)} %param.6) | copy-start | bytes 7680004
  10.0 1.8 %copy-start.3 = (f32[2,1,625,125]{3,1,2,0:T(1,128)S(1)}, f32[2,1,625,125]{3,1,2,0:T(1,128)}, u32[]{:S(2)}) copy-start(f32[2,1,625,125]{3,1,2,0:T(1,128)} %param.9) | copy-start | bytes 1875004
  12.6 1.5 %copy-start.1 = (f32[2,1,625,125]{3,2,1,0:T(8,128)S(1)}, f32[2,1,625,125]{3,2,1,0:T(8,128)}, u32[]{:S(2)}) copy-start(f32[2,1,625,125]{3,2,1,0:T(8,128)} %copy.24) | copy-start | bytes 1875004
  14.1 1.7 %copy-start = (f32[2,1,625,512]{3,2,1,0:T(8,128)S(1)}, f32[2,1,625,512]{3,2,1,0:T(8,128)}, u32[]{:S(2)}) copy-start(f32[2,1,625,512]{3,2,1,0:T(8,128)} %copy.23) | copy-start | bytes 7680004
  33.0 11.0 %collective-permute-start.2 = (f32[128,256]{1,0:T(8,128)S(1)}, f32[128,256]{1,0:T(8,128)S(1)}, u32[]{:S(2)}, u32[]{:S(2)}) collective-permute-start(f32[128,256]{1,0:T(8,128)S(1)} %constant_dynamic-slice_fusion.1), channel_id=1, source_target_pairs={{0,4},{4,0},{8,12},{12,8},{16,20},{20,16},{24,28},{28,24},{1,5},{5... | collective-permute-start | bytes 393224 | tf_op jit(solution)/shard_map/ppermute | solution.py:244
  54.5 2.6 %collective-permute-start.3 = (f32[128,256]{1,0:T(8,128)S(1)}, f32[128,256]{1,0:T(8,128)S(1)}, u32[]{:S(2)}, u32[]{:S(2)}) collective-permute-start(f32[128,256]{1,0:T(8,128)S(1)} %get-tuple-element.39), channel_id=1, source_target_pairs={{0,4},{4,0},{8,12},{12,8},{16,20},{20,16},{24,28},{28,24},{1,5},{5... | collective-permute-start | bytes 393224 | tf_op jit(solution)/shard_map/ppermute | solution.py:253
  58.3 15.0 %collective-permute-start.4 = (f32[2,128,512]{2,1,0:T(8,128)S(1)}, f32[2,128,512]{2,1,0:T(8,128)S(1)}, u32[]{:S(2)}, u32[]{:S(2)}) collective-permute-start(f32[2,128,512]{2,1,0:T(8,128)S(1)} %get-tuple-element.40), channel_id=1, source_target_pairs={{0,1},{1,2},{2,3},{3,0},{4,5},{5,6},{6,7},{7,4},{8,9},{9,10},{10,1... | collective-permute-start | bytes 1572872 | tf_op jit(solution)/shard_map/ppermute | solution.py:219
  59.2 24.1 %collective-permute-start.5 = (f32[2,128,512]{2,1,0:T(8,128)S(1)}, f32[2,128,512]{2,1,0:T(8,128)S(1)}, u32[]{:S(2)}, u32[]{:S(2)}) collective-permute-start(f32[2,128,512]{2,1,0:T(8,128)S(1)} %get-tuple-element.41), channel_id=1, source_target_pairs={{0,3},{1,0},{2,1},{3,2},{4,7},{5,4},{6,5},{7,6},{8,11},{9,8},{10,9... | collective-permute-start | bytes 1572872 | tf_op jit(solution)/shard_map/ppermute | solution.py:220
  84.8 2.5 %collective-permute-start.6 = (f32[128,256]{1,0:T(8,128)S(1)}, f32[128,256]{1,0:T(8,128)S(1)}, u32[]{:S(2)}, u32[]{:S(2)}) collective-permute-start(f32[128,256]{1,0:T(8,128)S(1)} %constant_dynamic-slice_fusion), channel_id=1, source_target_pairs={{0,4},{4,0},{8,12},{12,8},{16,20},{20,16},{24,28},{28,24},{1,5},{5... | collective-permute-start | bytes 393224 | tf_op jit(solution)/shard_map/ppermute | solution.py:244
  97.9 2.6 %collective-permute-start.7 = (f32[128,256]{1,0:T(8,128)S(1)}, f32[128,256]{1,0:T(8,128)S(1)}, u32[]{:S(2)}, u32[]{:S(2)}) collective-permute-start(f32[128,256]{1,0:T(8,128)S(1)} %get-tuple-element.46), channel_id=1, source_target_pairs={{0,4},{4,0},{8,12},{12,8},{16,20},{20,16},{24,28},{28,24},{1,5},{5... | collective-permute-start | bytes 393224 | tf_op jit(solution)/shard_map/ppermute | solution.py:253

commit v2 on v0

v2 whole, which is shorter than its diff:
```python
import functools

import jax
import jax.numpy as jnp
from jax import lax
from jax.experimental import pallas as pl
from jax.experimental.pallas import tpu as pltpu
from jax.sharding import PartitionSpec as P

VARS = 5
NODE = 5
FACE = VARS * NODE**2
WIDE = 128
SWEEPS = 2
CORES = 2
LIMIT = 24 * 1024 * 1024
MOST = 48 * 1024 * 1024
ANY = pl.ANY
HBM = pltpu.HBM
VMEM = pltpu.VMEM
SMEM = pltpu.SMEM


def face_runs(kind):
    if kind == "down":
        return [(var * NODE**3 + (NODE - 1) * NODE**2, NODE**2) for var in range(VARS)]
    b = NODE - 1 if kind == "high" else 0
    return [
        (var * NODE**3 + a * NODE**2 + b * NODE, NODE)
        for var in range(VARS)
        for a in range(NODE)
    ]


def split(x):
    top = x.astype(jnp.bfloat16)
    return top, (x - top.astype(jnp.float32)).astype(jnp.bfloat16)


def left(x):
    high, low = split(x)
    return jnp.concatenate([high, high, low], axis=1)


def right(x):
    high, low = split(x)
    return jnp.concatenate([high, low, high], axis=0)


def stacked(a, b):
    return jnp.dot(a, b, preferred_element_type=jnp.float32)


def padded(x, rows):
    short = rows - x.shape[0]
    return jnp.concatenate([x, jnp.zeros((short, x.shape[1]), x.dtype)], axis=0) if short else x


def call(kernel, outs, *args, scratch=(), us=1, after=(), limit=LIMIT):
    args = list(args) + [(ANY, x) for x in after]

    def body(*refs):
        given = len(args) - len(after)
        kernel(*refs[:given], *refs[len(args) :])

    return pl.pallas_call(
        body,
        out_shape=[jax.ShapeDtypeStruct(shape, kind) for _, shape, kind in outs],
        in_specs=[pl.BlockSpec(memory_space=space) for space, _ in args],
        out_specs=[pl.BlockSpec(memory_space=space) for space, _, _ in outs],
        scratch_shapes=list(scratch),
        compiler_params=pltpu.CompilerParams(vmem_limit_bytes=limit),
        cost_estimate=pl.CostEstimate(flops=int(us * 10**9), bytes_accessed=0, transcendentals=0),
        name=getattr(kernel, "func", kernel).__name__,
    )(*[array for _, array in args])


def start_faces(core_ref, field_ref, *refs):
    outs, sems = refs[:-1], refs[-1]
    half = outs[0].shape[-1]
    copies = []
    for k, out in enumerate(outs):
        other, low = divmod(k, 2)
        first = 0 if low else (NODE - 1) * NODE
        own = core_ref[0] if other == 0 else 1 - core_ref[0]
        at = pl.multiple_of(own * half, half)
        copies.append(
            pltpu.make_async_copy(
                field_ref.at[:, :, pl.ds(first, NODE), :, pl.ds(at, half)], out, sems.at[k]
            )
        )
    for copy in copies:
        copy.start()
    for copy in copies:
        copy.wait()


def load_rows(pairs, sems):
    copies = []
    for k, (source, held) in enumerate(pairs):
        copies.append(pltpu.make_async_copy(source, held, sems.at[k]))
        copies[-1].start()
    return copies


def load_blocks(inv_ref, rhs_ref, up_ref, south_ref, north_ref, inv, rhs, blocks, sems):
    return [
        load_rows(
            [
                (inv_ref.at[e, :, 0, :], inv.at[e]),
                (rhs_ref.at[e, :, 0, :], rhs.at[e]),
                (south_ref.at[e, :, 0, :], blocks.at[e, 0]),
                (north_ref.at[e, :, 0, :], blocks.at[e, 1]),
                (up_ref.at[e, :, 0, :], blocks.at[e, 2]),
            ],
            sems.at[e],
        )
        for e in range(inv_ref.shape[0])
    ]


def fill_columns(e, depth, rhs, blocks, columns):
    wide = rhs.shape[2]
    columns[:, :wide] = right(padded(rhs[e], depth))
    for k in range(3):
        at = wide + k * WIDE
        block = right(padded(blocks[e, k], depth))
        columns[:, at : at + FACE] = block


def fold_blocks(inv_ref, rhs_ref, up_ref, south_ref, north_ref,
                c_ref, bsn_ref, bu_ref, faces_ref,
                inv, rhs, blocks, rows, columns, whole, sems):
    elements, unknowns = inv.shape[:2]
    depth, wide = rows.shape[1], rhs.shape[2]
    half = wide // CORES
    copies = load_blocks(inv_ref, rhs_ref, up_ref, south_ref, north_ref, inv, rhs, blocks, sems)
    rows[...] = jnp.zeros_like(rows)
    columns[...] = jnp.zeros_like(columns)
    faces_ref[...] = jnp.zeros_like(faces_ref)
    for e in range(elements):
        for copy in copies[e]:
            copy.wait()
        rows[:unknowns, :unknowns] = inv[e]
        fill_columns(e, depth, rhs, blocks, columns)
        whole[...] = stacked(left(rows[...]), columns[...])
        c_ref[e] = whole[:, :wide]
        bsn_ref[e] = left(whole[:, wide : wide + 2 * WIDE])
        bu_ref[e] = left(whole[:, wide + 2 * WIDE :])

        for f, kind in enumerate(("down", "high", "low")):
            at = f * WIDE
            for first, length in face_runs(kind):
                to, of = slice(at, at + length), slice(first, first + length)
                block = whole[of, :]
                for k in range(CORES):
                    faces_ref[k, e, to, :half] = block[:, k * half : (k + 1) * half]
                    faces_ref[k, e, to, half:] = block[:, wide:]
                at += length


def chip_blocks(faces_ref, fc_ref, fsn_ref, fu_ref, resp_ref, step_ref, held):
    elements, half = faces_ref.shape[1], fc_ref.shape[2]
    for e in range(CORES * elements):
        source = faces_ref.at[e // elements, e % elements]
        fc_ref[e] = source[:, :half]
        fsn_ref[e] = left(source[:, half : half + 2 * WIDE])
        own = source[:, half + 2 * WIDE :]
        fu_ref[e] = left(own)
        held[...] = -stacked(fu_ref[e], right(held[:WIDE, :])) if e else -own
        resp_ref[e] = left(held[...])
    step_ref[...] = held[:WIDE, :]


def halo_columns(s, n):
    return right(jnp.concatenate([padded(s, WIDE), padded(n, WIDE)], axis=0))


def first_faces(core_ref, fc_ref, fsn_ref, fu_ref, step_ref, *refs):
    halos, (q_ref, out_ref, held, sems) = refs[:4], refs[4:]
    elements = held.shape[2]
    copies = []
    for k, halo in enumerate(halos):
        for e in range(elements):
            copy = pltpu.make_async_copy(halo.at[e, :, 0, :], held.at[k // 2, k % 2, e], sems.at[k, e])
            copy.start()
            copies.append(copy)
    for copy in copies:
        copy.wait()
    half = fc_ref.shape[2]
    for e in range(CORES * elements):
        owner, of = divmod(e, elements)
        other = lax.rem(core_ref[0] + owner, 2)
        q = fc_ref[e] - stacked(fsn_ref[e], halo_columns(held[other, 0, of], held[other, 1, of]))
        if e:
            q = q - stacked(fu_ref[e], right(q_ref[e - 1, :WIDE, :]))
        q_ref[e] = q
    out_ref[:, :half] = q_ref[CORES * elements - 1, :WIDE, :]
    out_ref[:, half:] = step_ref[...]


def last_faces(core_ref, fc_ref, fsn_ref, fu_ref, below_ref, above_ref, q_ref, out_ref, away_ref):
    count = fc_ref.shape[0]
    elements = count // CORES
    for e in range(count):
        q = fc_ref[e, :WIDE, :] - stacked(fsn_ref[e, :WIDE, :], halo_columns(below_ref[e], above_ref[e]))
        if e:
            q = q - stacked(fu_ref[e, :WIDE, :], right(q_ref[e - 1]))
        q_ref[e] = q
    out_ref[...] = q_ref[count - 1]
    other = (1 - core_ref[0]) * elements
    for e in range(elements):
        away_ref[0, e] = below_ref[other + e]
        away_ref[1, e] = above_ref[other + e]


def through_chips(core_ref, inflow_ref, chips, steps):
    half = inflow_ref.shape[1]
    inflow_ref[...] = jnp.zeros_like(inflow_ref)
    for back in range(len(chips), 0, -1):

        @pl.when(core_ref[1] >= back)
        def _():
            passed = stacked(left(steps[back - 1][:, half:]), right(inflow_ref[...]))
            inflow_ref[...] = chips[back - 1][:, :half] + passed


def next_faces(core_ref, q_ref, resp_ref, *refs):
    high_ref, low_ref, inflow_ref = refs[-3:]
    through_chips(core_ref, inflow_ref, refs[:-3], refs[:-3])
    inflow = right(inflow_ref[...])
    for e in range(q_ref.shape[0]):
        faces = q_ref[e, WIDE:, :] + stacked(resp_ref[e, WIDE:, :], inflow)
        high_ref[e] = faces[:WIDE]
        low_ref[e] = faces[WIDE:]


def inflow_of_cores(core_ref, q_ref, resp_ref, *refs):
    keep_ref, send_ref = refs[-2:]
    count = (len(refs) - 2) // 2
    through_chips(core_ref, keep_ref, refs[:count], refs[count:-2])
    last = q_ref.shape[0] // CORES - 1

    @pl.when(core_ref[0] == 0)
    def _():
        send_ref[...] = q_ref[last] + stacked(resp_ref[last, :WIDE, :], right(keep_ref[...]))

    @pl.when(core_ref[0] == 1)
    def _():
        send_ref[...] = keep_ref[...]
        keep_ref[...] = q_ref[last] + stacked(resp_ref[last, :WIDE, :], right(send_ref[...]))


def join(core_ref, keep_ref, got_ref, inflow_ref):
    half = keep_ref.shape[1]

    @pl.when(core_ref[0] == 0)
    def _():
        inflow_ref[:, :half] = keep_ref[...]
        inflow_ref[:, half:] = got_ref[...]

    @pl.when(core_ref[0] == 1)
    def _():
        inflow_ref[:, :half] = got_ref[...]
        inflow_ref[:, half:] = keep_ref[...]


def field_without_inflow(core_ref, c_ref, bsn_ref, below_ref, above_ref, got_ref, p_ref, halo):
    elements, half = c_ref.shape[0], below_ref.shape[2]
    for e in range(elements):

        def place(own):
            mine, other = slice(own * half, (own + 1) * half), slice((1 - own) * half, (2 - own) * half)
            for k, ref in enumerate((below_ref, above_ref)):
                rows = slice(k * WIDE, (k + 1) * WIDE)
                halo[rows, mine] = ref[own * elements + e]
                halo[rows, other] = got_ref[k, e]

        for k in range(CORES):
            pl.when(core_ref[0] == k)(functools.partial(place, k))
        p_ref[e] = c_ref[e] - stacked(bsn_ref[e], right(halo[...]))


def whole_field(core_ref, p_ref, bu_ref, keep_ref, got_ref, out_ref, inflow_ref, held, sems):
    join(core_ref, keep_ref, got_ref, inflow_ref)
    elements, unknowns = held.shape[:2]
    copies = []
    for e in range(elements):
        if e:
            at = 0
            for first, length in face_runs("down"):
                inflow_ref[at : at + length, :] = held[e - 1, first : first + length, :]
                at += length
        value = p_ref[e] - stacked(bu_ref[e], right(inflow_ref[...]))
        held[e] = value[:unknowns]
        copy = pltpu.make_async_copy(held.at[e], out_ref.at[e, :, 0, :], sems.at[e])
        copy.start()
        copies.append(copy)
    for copy in copies:
        copy.wait()


def ring(axis, by):
    count = lax.axis_size(axis)
    return [(i, (i + by) % count) for i in range(count)]


def per_device(right_side, start_field, block_inverse, upwind_block, south_block, north_block):
    by_row = lambda x: x.transpose(0, 2, 1, 3)
    rhs, start, inverse, upwind, south, north = map(
        by_row, (right_side, start_field, block_inverse, upwind_block, south_block, north_block)
    )
    elements, unknowns, _, columns = rhs.shape
    depth = -(-unknowns // 128) * 128
    half = columns // CORES
    count = CORES * elements
    devices, spans = lax.axis_size("sweep"), lax.axis_size("span")
    place = lax.axis_index("sweep")
    where = jnp.stack([place % CORES, place // CORES]).astype(jnp.int32)
    dma = pltpu.SemaphoreType.DMA
    f32, bf16 = jnp.float32, jnp.bfloat16
    core = (SMEM, where)
    face = (elements, FACE, 1, half)

    def held(arrays):
        return [(VMEM, x) for x in arrays]

    def swap(x):
        return lax.ppermute(x, "sweep", [(i, i ^ 1) for i in range(devices)])

    def from_chips(x):
        return [
            lax.ppermute(x, "sweep", ring("sweep", CORES * back))
            for back in range(1, devices // CORES)
        ]

    def along_span(x, by, other_core):
        pairs = [
            (i * spans + j, (i ^ other_core) * spans + (j + by) % spans)
            for i in range(devices)
            for j in range(spans)
        ]
        return lax.ppermute(x, ("sweep", "span"), pairs)

    runs = start.reshape(elements, NODE**2, VARS * NODE, 1, columns)
    found = call(
        start_faces,
        [(VMEM, (elements, NODE**2, NODE, 1, half), f32)] * 4,
        core, (HBM, runs),
        scratch=[dma((4,))],
        limit=MOST,
    )
    found = [x.reshape(face) for x in found]
    halos = [along_span(found[k], -1 if k % 2 else 1, k // 2) for k in range(4)]
    c, bsn, bu, own = call(
        fold_blocks,
        [
            (VMEM, (elements, depth, columns), f32),
            (VMEM, (elements, depth, 6 * WIDE), bf16),
            (VMEM, (elements, depth, 3 * WIDE), bf16),
            (VMEM, (CORES, elements, 3 * WIDE, half + 3 * WIDE), f32),
        ],
        *[(HBM, x) for x in (inverse, rhs, upwind, south, north)],
        scratch=[
            VMEM((elements, unknowns, unknowns), f32),
            VMEM((elements, unknowns, columns), f32),
            VMEM((elements, 3, unknowns, FACE), f32),
            VMEM((depth, depth), f32),
            VMEM((3 * depth, columns + 3 * WIDE), bf16),
            VMEM((depth, columns + 3 * WIDE), f32),
            dma((elements, 5)),
        ],
        us=0,
        limit=MOST,
        after=found,
    )
    cores = lax.all_to_all(
        own, "sweep", 0, 0, axis_index_groups=[[i, i + 1] for i in range(0, devices, CORES)]
    )
    fc, fsn, fu, resp, step = call(
        chip_blocks,
        [
            (VMEM, (count, 3 * WIDE, half), f32),
            (VMEM, (count, 3 * WIDE, 6 * WIDE), bf16),
            (VMEM, (count, 3 * WIDE, 3 * WIDE), bf16),
            (VMEM, (count, 3 * WIDE, 3 * WIDE), bf16),
            (VMEM, (WIDE, WIDE), f32),
        ],
        (VMEM, cores),
        scratch=[VMEM((3 * WIDE, WIDE), f32)],
        us=0,
    )
    q, out = call(
        first_faces,
        [(VMEM, (count, 3 * WIDE, half), f32), (VMEM, (WIDE, half + WIDE), f32)],
        core, *held((fc, fsn, fu, step)), *[(HBM, x) for x in halos],
        scratch=[VMEM((2, 2, elements, FACE, half), f32), dma((4, elements))],
        us=2,
    )
    chips = from_chips(out)
    high, low = call(
        next_faces,
        [(VMEM, (count, WIDE, half), f32)] * 2,
        core, *held((q, resp, *chips)),
        scratch=[VMEM((WIDE, half), f32)],
        us=2,
    )
    below, above = along_span(high, 1, 0), along_span(low, -1, 0)
    q, out, away = call(
        last_faces,
        [
            (VMEM, (count, WIDE, half), f32),
            (VMEM, (WIDE, half), f32),
            (VMEM, (2, elements, WIDE, half), f32),
        ],
        core, *held((fc, fsn, fu, below, above)),
        us=1,
    )
    last_chips = from_chips(out)
    (part,) = call(
        field_without_inflow,
        [(VMEM, (elements, depth, columns), f32)],
        core, *held((c, bsn, below, above, swap(away))),
        scratch=[VMEM((2 * WIDE, columns), f32)],
        us=2,
    )
    keep, send = call(
        inflow_of_cores,
        [(VMEM, (WIDE, half), f32)] * 2,
        core, *held((q, resp, *last_chips, *chips)),
        after=[part],
    )
    (field,) = call(
        whole_field,
        [(HBM, rhs.shape, f32)],
        core, *held((part, bu, keep, swap(send))),
        scratch=[
            VMEM((WIDE, columns), f32),
            VMEM((elements, unknowns, columns), f32),
            dma((elements,)),
        ],
        us=2,
    )
    return by_row(field)


def solution(mesh):
    spec = P("sweep", "span", None, None)
    return jax.shard_map(
        per_device, mesh=mesh, in_specs=(spec,) * 6, out_specs=spec, check_vma=False
    )
```

time: 474 us -> 89.3 us (0.19)
  the two profiles are of different devices: /device:TPU:23 before, /device:TPU:1 now
where the time goes in v2:
time: 89.3 us; the launch traced here: 88.8 us
  waiting for transfers between devices  34.6 us (39%)
  Pallas kernels  23.2 us (26%)
  starting transfers between devices  20.9 us (23%)
  blocking collectives  8.03 us (9%)
  local copies, waits for them, and re-layouts  1.86 us (2%)
    pallas_call x9, Pallas kernels, call(): pl.pallas_call(body, out_shape=[jax.ShapeDtypeStruct(shape, kind) for _,...  23.2 us
    ppermute x6, waiting for transfers between devices, along_span(): return lax.ppermute(x, ('sweep', 'span'), pairs)  20.1 us
    ppermute x6, waiting for transfers between devices, from_chips(): lax.ppermute(x, 'sweep', ring('sweep', CORES * back))  13.6 us
    ppermute x6, starting transfers between devices, along_span(): return lax.ppermute(x, ('sweep', 'span'), pairs)  11.9 us
    all_to_all x1, blocking collectives, per_device(): lax.all_to_all(own, 'sweep', 0, 0, axis_index_groups=[[i, i + 1] for i in...  8.03 us
    ppermute x6, starting transfers between devices, from_chips(): lax.ppermute(x, 'sweep', ring('sweep', CORES * back))  5.35 us
    ppermute x2, starting transfers between devices, swap(): return lax.ppermute(x, 'sweep', [(i, i ^ 1) for i in range(devices)])  3.62 us
    unnamed x10, local copies, waits for them, and re-layouts  1.86 us
  transfers between devices with their start and end apart: 14, of which 8 were waited for; matrix products, arithmetic and copies ran while one was open for 0% of the time, Pallas kernels for 15%

profile of v2, /device:TPU:1, one launch (start us, length us, event | category | flops | bytes accessed | tf_op | source)
XLA Modules:
  0.0 88.8 jit_solution(4512390281976053279)
XLA Ops:
  0.0 0.0 copy-start.3
  0.0 0.0 copy-start.2
  0.0 0.0 copy-start.1
  0.0 0.1 pad_add_fusion.refs_0_
  0.1 0.0 copy-start.4
  0.1 1.8 %copy-done.4 = f32[2,1,625,512]{3,1,2,0:T(1,128)S(1)} copy-done((f32[2,1,625,512]{3,1,2,0:T(1,128)S(1)}, f32[2,1,625,512]{3,1,2,0:T(1,128)}, u32[]{:S(2)}) %copy-start.4) | copy-done | bytes 2560024
  1.9 0.9 %start_faces.1 = (f32[2,25,5,1,256]{4,3,2,1,0:T(1,128)S(1)}, f32[2,25,5,1,256]{4,3,2,1,0:T(1,128)S(1)}, f32[2,25,5,1,256]{4,3,2,1,0:T(1,128)S(1)}, f32[2,25,5,1,256]{4,3,2,1,0:T(1,128)S(1)}) custom-call(s32[2]{0:T(128)S(1)} %pad_add_fusion.refs_0_, f32[2,25,25,1,512]{4,3,2,1,0:T(1,128)S(1)} %bitcast.24), custom_call_target="tpu_custom_call" | custom-call | flops 1000000000 | tf_op jit(solution)/shard_map/start_faces/pallas_call | solution.py:66
  2.9 4.2 %collective-permute-start.1 = (f32[2,125,1,256]{3,2,1,0:T(1,128)S(1)}, f32[2,125,1,256]{3,2,1,0:T(1,128)S(1)}, u32[]{:S(2)}, u32[]{:S(2)}) collective-permute-start(f32[2,125,1,256]{3,2,1,0:T(1,128)S(1)} %bitcast.22), channel_id=1, source_target_pairs={{0,3},{1,0},{2,1},{3,2},{4,7},{5,4},{6,5},{7,6},{8,11},{9,8},{10,9... | collective-permute-start | bytes 768008 | tf_op jit(solution)/shard_map/ppermute | solution.py:343
  7.1 0.0 collective-permute-start
  7.1 0.6 collective-permute-start.2
  7.7 3.8 %collective-permute-start.3 = (f32[2,125,1,256]{3,2,1,0:T(1,128)S(1)}, f32[2,125,1,256]{3,2,1,0:T(1,128)S(1)}, u32[]{:S(2)}, u32[]{:S(2)}) collective-permute-start(f32[2,125,1,256]{3,2,1,0:T(1,128)S(1)} %bitcast.16), channel_id=1, source_target_pairs={{0,7},{1,4},{2,5},{3,6},{4,3},{5,0},{6,1},{7,2},{8,15},{9,12},{10,... | collective-permute-start | bytes 768008 | tf_op jit(solution)/shard_map/ppermute | solution.py:343
  11.5 0.0 copy-done.3
  11.5 0.0 copy-done.2
  11.5 0.0 copy-done.1
  11.5 10.6 %fold_blocks.1 = (f32[2,640,512]{2,1,0:T(8,128)}, bf16[2,640,768]{2,1,0:T(8,128)(2,1)S(1)}, bf16[2,640,384]{2,1,0:T(8,128)(2,1)S(1)}, f32[2,2,384,640]{3,2,1,0:T(8,128)}) custom-call(f32[2,625,1,625]{3,2,1,0:T(1,128)} %bitcast.25, f32[2,625,1,512]{3,2,1,0:T(1,128)} %bitcast.26, f32[2,625,1,125]{3,2,1,0:T(1,128)S(1)} %bitcast.13, ...), custom_call_target="tpu_custom_call" | custom-call | tf_op jit(solution)/shard_map/fold_blocks/pallas_call | solution.py:66
  22.1 8.0 %all_to_all.5.refs_0_ = f32[2,2,384,640]{3,2,1,0:T(8,128)S(1)} all-to-all(f32[2,2,384,640]{3,2,1,0:T(8,128)} %get-tuple-element.33), channel_id=1, replica_groups={{0,4},{8,12},{16,20},{24,28},{1,5},{9,13},{17,21},{25,29},{2,6},{10,14}..., dimensions={0} | all-to-all | bytes 7864320 | tf_op jit(solution)/shard_map/all_to_all | solution.py:377
  30.1 1.1 %chip_blocks.1 = (f32[4,384,256]{2,1,0:T(8,128)S(1)}, bf16[4,384,768]{2,1,0:T(8,128)(2,1)S(1)}, bf16[4,384,384]{2,1,0:T(8,128)(2,1)S(1)}, bf16[4,384,384]{2,1,0:T(8,128)(2,1)S(1)}, f32[128,128]{1,0:T(8,128)S(1)}) custom-call(f32[2,2,384,640]{3,2,1,0:T(8,128)S(1)} %all_to_all.5.refs_0_), custom_call_target="tpu_custom_call" | custom-call | tf_op jit(solution)/shard_map/chip_blocks/pallas_call | solution.py:66
  31.3 0.0 collective-permute-done.1.refs_6_
  31.3 0.0 collective-permute-done.refs_5_
  31.3 0.0 collective-permute-done.2.refs_7_
  31.3 0.0 collective-permute-done.3.refs_8_
  31.3 2.6 %first_faces.1 = (f32[4,384,256]{2,1,0:T(8,128)S(1)}, f32[128,384]{1,0:T(8,128)S(1)}) custom-call(s32[2]{0:T(128)S(1)} %pad_add_fusion.refs_0_, f32[4,384,256]{2,1,0:T(8,128)S(1)} %get-tuple-element.34.refs_1_, bf16[4,384,768]{2,1,0:T(8,128)(2,1)S(1)} %get-tuple-element.35.refs_2_, bf16[4,384,384]{2,1,0:T(8,128)(2,1)S(1)} %get-tuple-element.36.refs_3_, ...), custom_call_target="tpu_custom_call" | custom-call | flops 2000000000 | tf_op jit(solution)/shard_map/first_faces/pallas_call | solution.py:66
  34.0 2.2 %collective-permute-start.6 = (f32[128,384]{1,0:T(8,128)S(1)}, f32[128,384]{1,0:T(8,128)S(1)}, u32[]{:S(2)}, u32[]{:S(2)}) collective-permute-start(f32[128,384]{1,0:T(8,128)S(1)} %get-tuple-element.40), channel_id=1, source_target_pairs={{0,24},{4,28},{8,0},{12,4},{16,8},{20,12},{24,16},{28,20},{1,25},{... | collective-permute-start | bytes 589832 | tf_op jit(solution)/shard_map/ppermute | solution.py:333
  36.2 0.2 collective-permute-start.5
  36.4 0.3 collective-permute-start.4
  36.7 3.4 %collective-permute-done.6.refs_5_.refs_8_ = f32[128,384]{1,0:T(8,128)S(1)} collective-permute-done((f32[128,384]{1,0:T(8,128)S(1)}, f32[128,384]{1,0:T(8,128)S(1)}, u32[]{:S(2)}, u32[]{:S(2)}) %collective-permute-start.6) | collective-permute-done | bytes 196640 | tf_op jit(solution)/shard_map/ppermute | solution.py:333
  40.1 2.7 %collective-permute-done.5.refs_4_.refs_7_ = f32[128,384]{1,0:T(8,128)S(1)} collective-permute-done((f32[128,384]{1,0:T(8,128)S(1)}, f32[128,384]{1,0:T(8,128)S(1)}, u32[]{:S(2)}, u32[]{:S(2)}) %collective-permute-start.5) | collective-permute-done | bytes 196640 | tf_op jit(solution)/shard_map/ppermute | solution.py:333
  42.8 2.5 %collective-permute-done.4.refs_3_.refs_6_ = f32[128,384]{1,0:T(8,128)S(1)} collective-permute-done((f32[128,384]{1,0:T(8,128)S(1)}, f32[128,384]{1,0:T(8,128)S(1)}, u32[]{:S(2)}, u32[]{:S(2)}) %collective-permute-start.4) | collective-permute-done | bytes 196640 | tf_op jit(solution)/shard_map/ppermute | solution.py:333
  45.3 1.0 %next_faces.1 = (f32[4,128,256]{2,1,0:T(8,128)S(1)}, f32[4,128,256]{2,1,0:T(8,128)S(1)}) custom-call(s32[2]{0:T(128)S(1)} %pad_add_fusion.refs_0_, f32[4,384,256]{2,1,0:T(8,128)S(1)} %get-tuple-element.38.refs_1_, bf16[4,384,384]{2,1,0:T(8,128)(2,1)S(1)} %get-tuple-element.39.refs_2_, f32[128,384]{1,0:T(8,128)S(1)} %collective-permute-done.4.refs_3_.refs_6_, ...), custom_call_target="tpu_custom_call" | custom-call | flops 2000000000 | tf_op jit(solution)/shard_map/next_faces/pallas_call | solution.py:66
  46.3 0.1 collective-permute-start.7
  46.4 0.0 copy-start
  46.4 3.3 %collective-permute-start.8 = (f32[4,128,256]{2,1,0:T(8,128)S(1)}, f32[4,128,256]{2,1,0:T(8,128)S(1)}, u32[]{:S(2)}, u32[]{:S(2)}) collective-permute-start(f32[4,128,256]{2,1,0:T(8,128)S(1)} %get-tuple-element.42), channel_id=1, source_target_pairs={{0,3},{1,0},{2,1},{3,2},{4,7},{5,4},{6,5},{7,6},{8,11},{9,8},{10,9... | collective-permute-start | bytes 1572872 | tf_op jit(solution)/shard_map/ppermute | solution.py:343
  49.7 9.6 %collective-permute-done.7.refs_4_.refs_3_ = f32[4,128,256]{2,1,0:T(8,128)S(1)} collective-permute-done((f32[4,128,256]{2,1,0:T(8,128)S(1)}, f32[4,128,256]{2,1,0:T(8,128)S(1)}, u32[]{:S(2)}, u32[]{:S(2)}) %collective-permute-start.7) | collective-permute-done | bytes 524320 | tf_op jit(solution)/shard_map/ppermute | solution.py:343
  59.3 10.4 %collective-permute-done.8.refs_5_.refs_4_ = f32[4,128,256]{2,1,0:T(8,128)S(1)} collective-permute-done((f32[4,128,256]{2,1,0:T(8,128)S(1)}, f32[4,128,256]{2,1,0:T(8,128)S(1)}, u32[]{:S(2)}, u32[]{:S(2)}) %collective-permute-start.8) | collective-permute-done | bytes 524320 | tf_op jit(solution)/shard_map/ppermute | solution.py:343
  69.7 1.4 %last_faces.1 = (f32[4,128,256]{2,1,0:T(8,128)S(1)}, f32[128,256]{1,0:T(8,128)S(1)}, f32[2,2,128,256]{3,2,1,0:T(8,128)S(1)}) custom-call(s32[2]{0:T(128)S(1)} %pad_add_fusion.refs_0_, f32[4,384,256]{2,1,0:T(8,128)S(1)} %get-tuple-element.34.refs_1_, bf16[4,384,768]{2,1,0:T(8,128)(2,1)S(1)} %get-tuple-element.35.refs_2_, ...), custom_call_target="tpu_custom_call" | custom-call | flops 1000000000 | tf_op jit(solution)/shard_map/last_faces/pallas_call | solution.py:66
  71.2 2.4 %collective-permute-start.9 = (f32[2,2,128,256]{3,2,1,0:T(8,128)S(1)}, f32[2,2,128,256]{3,2,1,0:T(8,128)S(1)}, u32[]{:S(2)}, u32[]{:S(2)}) collective-permute-start(f32[2,2,128,256]{3,2,1,0:T(8,128)S(1)} %get-tuple-element.43), channel_id=1, source_target_pairs={{0,4},{4,0},{8,12},{12,8},{16,20},{20,16},{24,28},{28,24},{1,5},{5... | collective-permute-start | bytes 1572872 | tf_op jit(solution)/shard_map/ppermute | solution.py:329
  73.5 2.0 %collective-permute-start.12 = (f32[128,256]{1,0:T(8,128)S(1)}, f32[128,256]{1,0:T(8,128)S(1)}, u32[]{:S(2)}, u32[]{:S(2)}) collective-permute-start(f32[128,256]{1,0:T(8,128)S(1)} %get-tuple-element.46), channel_id=1, source_target_pairs={{0,24},{4,28},{8,0},{12,4},{16,8},{20,12},{24,16},{28,20},{1,25},{... | collective-permute-start | bytes 393224 | tf_op jit(solution)/shard_map/ppermute | solution.py:333
  75.6 0.6 collective-permute-start.11
  76.1 0.0 collective-permute-start.10
  76.1 0.0 collective-permute-done.9.refs_5_
  76.1 0.0 copy-done
  76.1 2.0 %field_without_inflow.1.refs_9_.refs_1_ = f32[2,640,512]{2,1,0:T(8,128)S(1)} custom-call(s32[2]{0:T(128)S(1)} %pad_add_fusion.refs_0_, f32[2,640,512]{2,1,0:T(8,128)S(1)} %copy-done, bf16[2,640,768]{2,1,0:T(8,128)(2,1)S(1)} %get-tuple-element.32.refs_2_, f32[4,128,256]{2,1,0:T(8,128)S(1)} %collective-permute-done.7.refs_4_.refs_3_, ...), custom_call_target="tpu_custom_call" | custom-call | flops 2000000000 | tf_op jit(solution)/shard_map/field_without_inflow/pallas_call | solution.py:66
  78.1 0.5 collective-permute-done.12.refs_5_
  78.6 4.5 %collective-permute-done.11.refs_4_ = f32[128,256]{1,0:T(8,128)S(1)} collective-permute-done((f32[128,256]{1,0:T(8,128)S(1)}, f32[128,256]{1,0:T(8,128)S(1)}, u32[]{:S(2)}, u32[]{:S(2)}) %collective-permute-start.11) | collective-permute-done | bytes 131104 | tf_op jit(solution)/shard_map/ppermute | solution.py:333
  83.1 0.0 collective-permute-done.10.refs_3_
  83.1 0.8 inflow_of_cores.1
  83.9 1.2 %collective-permute-start.13 = (f32[128,256]{1,0:T(8,128)S(1)}, f32[128,256]{1,0:T(8,128)S(1)}, u32[]{:S(2)}, u32[]{:S(2)}) collective-permute-start(f32[128,256]{1,0:T(8,128)S(1)} %get-tuple-element.48), channel_id=1, source_target_pairs={{0,4},{4,0},{8,12},{12,8},{16,20},{20,16},{24,28},{28,24},{1,5},{5... | collective-permute-start | bytes 393224 | tf_op jit(solution)/shard_map/ppermute | solution.py:329
  85.1 1.0 %collective-permute-done.13.refs_4_ = f32[128,256]{1,0:T(8,128)S(1)} collective-permute-done((f32[128,256]{1,0:T(8,128)S(1)}, f32[128,256]{1,0:T(8,128)S(1)}, u32[]{:S(2)}, u32[]{:S(2)}) %collective-permute-start.13) | collective-permute-done | bytes 131104 | tf_op jit(solution)/shard_map/ppermute | solution.py:329
  86.1 2.7 %whole_field.1 = f32[2,625,1,512]{3,2,1,0:T(1,128)} custom-call(s32[2]{0:T(128)S(1)} %pad_add_fusion.refs_0_, f32[2,640,512]{2,1,0:T(8,128)S(1)} %field_without_inflow.1.refs_9_.refs_1_, bf16[2,640,384]{2,1,0:T(8,128)(2,1)S(1)} %get-tuple-element.44.refs_2_, f32[128,256]{1,0:T(8,128)S(1)} %get-tuple-element.47.refs_3_, ...), custom_call_target="tpu_custom_call" | custom-call | flops 2000000000 | tf_op jit(solution)/shard_map/whole_field/pallas_call | solution.py:66
Async XLA Ops:
  0.0 11.5 %copy-start.3 = (f32[2,1,625,125]{3,1,2,0:T(1,128)S(1)}, f32[2,1,625,125]{3,1,2,0:T(1,128)}, u32[]{:S(2)}) copy-start(f32[2,1,625,125]{3,1,2,0:T(1,128)} %param.11) | copy-start | bytes 1875004
  0.0 11.5 %copy-start.2 = (f32[2,1,625,125]{3,1,2,0:T(1,128)S(1)}, f32[2,1,625,125]{3,1,2,0:T(1,128)}, u32[]{:S(2)}) copy-start(f32[2,1,625,125]{3,1,2,0:T(1,128)} %param.10) | copy-start | bytes 1875004
  0.0 11.5 %copy-start.1 = (f32[2,1,625,125]{3,1,2,0:T(1,128)S(1)}, f32[2,1,625,125]{3,1,2,0:T(1,128)}, u32[]{:S(2)}) copy-start(f32[2,1,625,125]{3,1,2,0:T(1,128)} %param.9) | copy-start | bytes 1875004
  0.1 1.8 %copy-start.4 = (f32[2,1,625,512]{3,1,2,0:T(1,128)S(1)}, f32[2,1,625,512]{3,1,2,0:T(1,128)}, u32[]{:S(2)}) copy-start(f32[2,1,625,512]{3,1,2,0:T(1,128)} %param.7) | copy-start | bytes 7680004
  2.9 28.4 %collective-permute-start.1 = (f32[2,125,1,256]{3,2,1,0:T(1,128)S(1)}, f32[2,125,1,256]{3,2,1,0:T(1,128)S(1)}, u32[]{:S(2)}, u32[]{:S(2)}) collective-permute-start(f32[2,125,1,256]{3,2,1,0:T(1,128)S(1)} %bitcast.22), channel_id=1, source_target_pairs={{0,3},{1,0},{2,1},{3,2},{4,7},{5,4},{6,5},{7,6},{8,11},{9,8},{10,9... | collective-permute-start | bytes 768008 | tf_op jit(solution)/shard_map/ppermute | solution.py:343
  7.1 24.2 %collective-permute-start = (f32[2,125,1,256]{3,2,1,0:T(1,128)S(1)}, f32[2,125,1,256]{3,2,1,0:T(1,128)S(1)}, u32[]{:S(2)}, u32[]{:S(2)}) collective-permute-start(f32[2,125,1,256]{3,2,1,0:T(1,128)S(1)} %bitcast.20), channel_id=1, source_target_pairs={{0,1},{1,2},{2,3},{3,0},{4,5},{5,6},{6,7},{7,4},{8,9},{9,10},{10,1... | collective-permute-start | bytes 768008 | tf_op jit(solution)/shard_map/ppermute | solution.py:343
  7.1 24.2 %collective-permute-start.2 = (f32[2,125,1,256]{3,2,1,0:T(1,128)S(1)}, f32[2,125,1,256]{3,2,1,0:T(1,128)S(1)}, u32[]{:S(2)}, u32[]{:S(2)}) collective-permute-start(f32[2,125,1,256]{3,2,1,0:T(1,128)S(1)} %bitcast.18), channel_id=1, source_target_pairs={{0,5},{1,6},{2,7},{3,4},{4,1},{5,2},{6,3},{7,0},{8,13},{9,14},{10,... | collective-permute-start | bytes 768008 | tf_op jit(solution)/shard_map/ppermute | solution.py:343
  7.7 23.6 %collective-permute-start.3 = (f32[2,125,1,256]{3,2,1,0:T(1,128)S(1)}, f32[2,125,1,256]{3,2,1,0:T(1,128)S(1)}, u32[]{:S(2)}, u32[]{:S(2)}) collective-permute-start(f32[2,125,1,256]{3,2,1,0:T(1,128)S(1)} %bitcast.16), channel_id=1, source_target_pairs={{0,7},{1,4},{2,5},{3,6},{4,3},{5,0},{6,1},{7,2},{8,15},{9,12},{10,... | collective-permute-start | bytes 768008 | tf_op jit(solution)/shard_map/ppermute | solution.py:343
  34.0 6.2 %collective-permute-start.6 = (f32[128,384]{1,0:T(8,128)S(1)}, f32[128,384]{1,0:T(8,128)S(1)}, u32[]{:S(2)}, u32[]{:S(2)}) collective-permute-start(f32[128,384]{1,0:T(8,128)S(1)} %get-tuple-element.40), channel_id=1, source_target_pairs={{0,24},{4,28},{8,0},{12,4},{16,8},{20,12},{24,16},{28,20},{1,25},{... | collective-permute-start | bytes 589832 | tf_op jit(solution)/shard_map/ppermute | solution.py:333
  36.2 6.6 %collective-permute-start.5 = (f32[128,384]{1,0:T(8,128)S(1)}, f32[128,384]{1,0:T(8,128)S(1)}, u32[]{:S(2)}, u32[]{:S(2)}) collective-permute-start(f32[128,384]{1,0:T(8,128)S(1)} %get-tuple-element.40), channel_id=1, source_target_pairs={{0,16},{4,20},{8,24},{12,28},{16,0},{20,4},{24,8},{28,12},{1,17},{... | collective-permute-start | bytes 589832 | tf_op jit(solution)/shard_map/ppermute | solution.py:333
  36.4 8.9 %collective-permute-start.4 = (f32[128,384]{1,0:T(8,128)S(1)}, f32[128,384]{1,0:T(8,128)S(1)}, u32[]{:S(2)}, u32[]{:S(2)}) collective-permute-start(f32[128,384]{1,0:T(8,128)S(1)} %get-tuple-element.40), channel_id=1, source_target_pairs={{0,8},{4,12},{8,16},{12,20},{16,24},{20,28},{24,0},{28,4},{1,9},{5... | collective-permute-start | bytes 589832 | tf_op jit(solution)/shard_map/ppermute | solution.py:333
  46.3 13.0 %collective-permute-start.7 = (f32[4,128,256]{2,1,0:T(8,128)S(1)}, f32[4,128,256]{2,1,0:T(8,128)S(1)}, u32[]{:S(2)}, u32[]{:S(2)}) collective-permute-start(f32[4,128,256]{2,1,0:T(8,128)S(1)} %get-tuple-element.41), channel_id=1, source_target_pairs={{0,1},{1,2},{2,3},{3,0},{4,5},{5,6},{6,7},{7,4},{8,9},{9,10},{10,1... | collective-permute-start | bytes 1572872 | tf_op jit(solution)/shard_map/ppermute | solution.py:343
  46.4 29.7 %copy-start = (f32[2,640,512]{2,1,0:T(8,128)S(1)}, f32[2,640,512]{2,1,0:T(8,128)}, u32[]{:S(2)}) copy-start(f32[2,640,512]{2,1,0:T(8,128)} %get-tuple-element.31.refs_1_) | copy-start | bytes 7864324
  46.4 23.3 %collective-permute-start.8 = (f32[4,128,256]{2,1,0:T(8,128)S(1)}, f32[4,128,256]{2,1,0:T(8,128)S(1)}, u32[]{:S(2)}, u32[]{:S(2)}) collective-permute-start(f32[4,128,256]{2,1,0:T(8,128)S(1)} %get-tuple-element.42), channel_id=1, source_target_pairs={{0,3},{1,0},{2,1},{3,2},{4,7},{5,4},{6,5},{7,6},{8,11},{9,8},{10,9... | collective-permute-start | bytes 1572872 | tf_op jit(solution)/shard_map/ppermute | solution.py:343
  71.2 5.0 %collective-permute-start.9 = (f32[2,2,128,256]{3,2,1,0:T(8,128)S(1)}, f32[2,2,128,256]{3,2,1,0:T(8,128)S(1)}, u32[]{:S(2)}, u32[]{:S(2)}) collective-permute-start(f32[2,2,128,256]{3,2,1,0:T(8,128)S(1)} %get-tuple-element.43), channel_id=1, source_target_pairs={{0,4},{4,0},{8,12},{12,8},{16,20},{20,16},{24,28},{28,24},{1,5},{5... | collective-permute-start | bytes 1572872 | tf_op jit(solution)/shard_map/ppermute | solution.py:329
  73.5 5.1 %collective-permute-start.12 = (f32[128,256]{1,0:T(8,128)S(1)}, f32[128,256]{1,0:T(8,128)S(1)}, u32[]{:S(2)}, u32[]{:S(2)}) collective-permute-start(f32[128,256]{1,0:T(8,128)S(1)} %get-tuple-element.46), channel_id=1, source_target_pairs={{0,24},{4,28},{8,0},{12,4},{16,8},{20,12},{24,16},{28,20},{1,25},{... | collective-permute-start | bytes 393224 | tf_op jit(solution)/shard_map/ppermute | solution.py:333
  75.6 7.5 %collective-permute-start.11 = (f32[128,256]{1,0:T(8,128)S(1)}, f32[128,256]{1,0:T(8,128)S(1)}, u32[]{:S(2)}, u32[]{:S(2)}) collective-permute-start(f32[128,256]{1,0:T(8,128)S(1)} %get-tuple-element.46), channel_id=1, source_target_pairs={{0,16},{4,20},{8,24},{12,28},{16,0},{20,4},{24,8},{28,12},{1,17},{... | collective-permute-start | bytes 393224 | tf_op jit(solution)/shard_map/ppermute | solution.py:333
  76.1 7.0 %collective-permute-start.10 = (f32[128,256]{1,0:T(8,128)S(1)}, f32[128,256]{1,0:T(8,128)S(1)}, u32[]{:S(2)}, u32[]{:S(2)}) collective-permute-start(f32[128,256]{1,0:T(8,128)S(1)} %get-tuple-element.46), channel_id=1, source_target_pairs={{0,8},{4,12},{8,16},{12,20},{16,24},{20,28},{24,0},{28,4},{1,9},{5... | collective-permute-start | bytes 393224 | tf_op jit(solution)/shard_map/ppermute | solution.py:333
  83.9 2.2 %collective-permute-start.13 = (f32[128,256]{1,0:T(8,128)S(1)}, f32[128,256]{1,0:T(8,128)S(1)}, u32[]{:S(2)}, u32[]{:S(2)}) collective-permute-start(f32[128,256]{1,0:T(8,128)S(1)} %get-tuple-element.48), channel_id=1, source_target_pairs={{0,4},{4,0},{8,12},{12,8},{16,20},{20,16},{24,28},{28,24},{1,5},{5... | collective-permute-start | bytes 393224 | tf_op jit(solution)/shard_map/ppermute | solution.py:329

commit v3 on v2

v3 whole, which is shorter than its diff:
```python
import functools

import jax
import jax.numpy as jnp
from jax import lax
from jax.experimental import pallas as pl
from jax.experimental.pallas import tpu as pltpu
from jax.sharding import PartitionSpec as P

VARS = 5
NODE = 5
FACE = VARS * NODE**2
WIDE = 128
SWEEPS = 2
CORES = 2
PANELS = 1
ORDER = (3, 1, 2, 0)
LIMIT = 24 * 1024 * 1024
MOST = 62 * 1024 * 1024
ANY = pl.ANY
HBM = pltpu.HBM
VMEM = pltpu.VMEM
SMEM = pltpu.SMEM


def face_runs(kind):
    if kind == "down":
        return [(var * NODE**3 + (NODE - 1) * NODE**2, NODE**2) for var in range(VARS)]
    b = NODE - 1 if kind == "high" else 0
    return [
        (var * NODE**3 + a * NODE**2 + b * NODE, NODE)
        for var in range(VARS)
        for a in range(NODE)
    ]


def split(x):
    top = x.astype(jnp.bfloat16)
    return top, (x - top.astype(jnp.float32)).astype(jnp.bfloat16)


def left(x):
    high, low = split(x)
    return jnp.concatenate([high, high, low], axis=1)


def right(x):
    high, low = split(x)
    return jnp.concatenate([high, low, high], axis=0)


def stacked(a, b):
    return jnp.dot(a, b, preferred_element_type=jnp.float32)


def padded(x, rows):
    short = rows - x.shape[0]
    return jnp.concatenate([x, jnp.zeros((short, x.shape[1]), x.dtype)], axis=0) if short else x


def call(kernel, outs, *args, scratch=(), us=1, after=(), limit=LIMIT, aliases=None):
    args = list(args) + [(ANY, x) for x in after]

    def body(*refs):
        given = len(args) - len(after)
        kernel(*refs[:given], *refs[len(args) :])

    return pl.pallas_call(
        body,
        out_shape=[jax.ShapeDtypeStruct(shape, kind) for _, shape, kind in outs],
        in_specs=[pl.BlockSpec(memory_space=space) for space, _ in args],
        out_specs=[pl.BlockSpec(memory_space=space) for space, _, _ in outs],
        scratch_shapes=list(scratch),
        input_output_aliases=aliases or {},
        compiler_params=pltpu.CompilerParams(vmem_limit_bytes=limit),
        cost_estimate=pl.CostEstimate(flops=int(us * 10**9), bytes_accessed=0, transcendentals=0),
        name=getattr(kernel, "func", kernel).__name__,
    )(*[array for _, array in args])


def start_faces(core_ref, field_ref, *refs):
    outs, sems = refs[:-1], refs[-1]
    half = outs[0].shape[-1]
    parts = []
    for k, out in enumerate(outs):
        own = core_ref[0] if k < 2 else 1 - core_ref[0]
        low = core_ref[2] if k % 2 == 0 else 1 - core_ref[2]
        part = pltpu.make_async_copy(
            field_ref.at[
                :, :, pl.ds((1 - low) * (NODE - 1) * NODE, NODE), :,
                pl.ds(pl.multiple_of(own * half, half), half),
            ],
            out,
            sems.at[k],
        )
        part.start()
        parts.append(part)
    for part in parts:
        part.wait()


def load_rows(pairs, sems):
    copies = []
    for k, (source, held) in enumerate(pairs):
        copies.append(pltpu.make_async_copy(source, held, sems.at[k]))
        copies[-1].start()
    return copies


def load_blocks(inv_ref, rhs_ref, up_ref, south_ref, north_ref, inv, rhs, blocks, sems):
    return [
        load_rows(
            [
                (inv_ref.at[e, :, 0, :], inv.at[e]),
                (rhs_ref.at[e, :, 0, :], rhs.at[e]),
                (south_ref.at[e, :, 0, :], blocks.at[e, 0]),
                (north_ref.at[e, :, 0, :], blocks.at[e, 1]),
                (up_ref.at[e, :, 0, :], blocks.at[e, 2]),
            ],
            sems.at[e],
        )
        for e in range(inv_ref.shape[0])
    ]


def fill_columns(e, depth, rhs, blocks, columns):
    wide = rhs.shape[2]
    columns[:, :wide] = right(padded(rhs[e], depth))
    for k in range(3):
        at = wide + k * WIDE
        block = right(padded(blocks[e, k], depth))
        columns[:, at : at + FACE] = block


def fold_faces(inv_ref, rhs_ref, up_ref, south_ref, north_ref, faces_ref,
               inv, rhs, blocks, rows, columns, sems):
    elements, depth, wide = inv.shape[0], rows.shape[1], rhs.shape[2]
    half = wide // CORES
    copies = load_blocks(inv_ref, rhs_ref, up_ref, south_ref, north_ref, inv, rhs, blocks, sems)
    rows[...] = jnp.zeros_like(rows)
    columns[...] = jnp.zeros_like(columns)
    for e in range(elements):
        copies[e][0].wait()
        for f, kind in enumerate(("down", "high", "low")):
            at = f * WIDE
            for first, length in face_runs(kind):
                rows[at : at + length, : inv.shape[2]] = inv[e, first : first + length, :]
                at += length
        for copy in copies[e][1:]:
            copy.wait()
        fill_columns(e, depth, rhs, blocks, columns)
        product = stacked(left(rows[...]), columns[...])
        for k in range(CORES):
            faces_ref[k, e, :, :half] = product[:, k * half : (k + 1) * half]
            faces_ref[k, e, :, half:] = product[:, wide:]


def fold_rows(inv_ref, rhs_ref, up_ref, south_ref, north_ref, c_ref, bsn_ref, bu_ref,
              inv, rhs, blocks, rows, columns, sems):
    elements, unknowns = inv.shape[:2]
    depth, wide = rows.shape[1], rhs.shape[2]
    copies = load_blocks(inv_ref, rhs_ref, up_ref, south_ref, north_ref, inv, rhs, blocks, sems)
    rows[...] = jnp.zeros_like(rows)
    columns[...] = jnp.zeros_like(columns)
    for e in range(elements):
        for copy in copies[e]:
            copy.wait()
        rows[:unknowns, :unknowns] = inv[e]
        fill_columns(e, depth, rhs, blocks, columns)
        product = stacked(left(rows[...]), columns[...])
        c_ref[e] = product[:, :wide]
        bsn_ref[e] = left(product[:, wide : wide + 2 * WIDE])
        bu_ref[e] = left(product[:, wide + 2 * WIDE :])


def chip_blocks(faces_ref, fc_ref, fsn_ref, fu_ref, resp_ref, step_ref, held):
    elements, half = faces_ref.shape[1], fc_ref.shape[2]
    for e in range(CORES * elements):
        source = faces_ref.at[e // elements, e % elements]
        fc_ref[e] = source[:, :half]
        fsn_ref[e] = left(source[:, half : half + 2 * WIDE])
        own = source[:, half + 2 * WIDE :]
        fu_ref[e] = left(own)
        held[...] = -stacked(fu_ref[e], right(held[:WIDE, :])) if e else -own
        resp_ref[e] = left(held[...])
    step_ref[...] = held[:WIDE, :]


def south_north(core_ref, k):
    return pl.multiple_of(((1 - core_ref[2]) if k == 0 else core_ref[2]) * WIDE, WIDE)


def first_traces(core_ref, fc_ref, fsn_ref, fu_ref, *refs):
    halos, (q_ref, out_ref, columns_ref, held, sems) = refs[:4], refs[4:]
    elements = held.shape[2]
    copies = []
    for k, halo in zip(ORDER, halos):
        north = 1 - core_ref[2] if k % 2 == 0 else core_ref[2]
        for e in range(elements):
            copy = pltpu.make_async_copy(halo.at[e, :, 0, :], held.at[k // 2, north, e], sems.at[k, e])
            copy.start()
            copies.append(copy)
    for copy in copies:
        copy.wait()
    for e in range(CORES * elements):
        owner, of = divmod(e, elements)
        other = lax.rem(core_ref[0] + owner, 2)
        both = [padded(held[other, k, of], WIDE) for k in range(2)]
        columns_ref[e] = right(jnp.concatenate(both, axis=0))
        q = fc_ref[e, :WIDE, :] - stacked(fsn_ref[e, :WIDE, :], columns_ref[e])
        if e:
            q = q - stacked(fu_ref[e, :WIDE, :], right(q_ref[e - 1]))
        q_ref[e] = q
    out_ref[...] = q_ref[CORES * elements - 1]


def other_faces(fc_ref, fsn_ref, fu_ref, columns_ref, q_ref, faces_ref):
    for e in range(fc_ref.shape[0]):
        faces = fc_ref[e, WIDE:, :] - stacked(fsn_ref[e, WIDE:, :], columns_ref[e])
        if e:
            faces = faces - stacked(fu_ref[e, WIDE:, :], right(q_ref[e - 1]))
        faces_ref[e] = faces


def last_faces(panel, core_ref, fc_ref, fsn_ref, fu_ref, first_ref, second_ref, q_ref, out_ref, away_ref, halo):
    count, width = fc_ref.shape[0], q_ref.shape[2]
    elements = count // CORES
    for e in range(count):
        for k, ref in enumerate((first_ref, second_ref)):
            halo[pl.ds(south_north(core_ref, k), WIDE), :] = ref[e]
        q = fc_ref[e, :WIDE, panel * width : (panel + 1) * width]
        q = q - stacked(fsn_ref[e, :WIDE, :], right(halo[...]))
        if e:
            q = q - stacked(fu_ref[e, :WIDE, :], right(q_ref[e - 1]))
        q_ref[e] = q
    out_ref[...] = q_ref[count - 1]
    other = (1 - core_ref[0]) * elements
    for e in range(elements):
        away_ref[0, e] = first_ref[other + e]
        away_ref[1, e] = second_ref[other + e]


def through_chips(core_ref, inflow_ref, chips, steps):
    inflow_ref[...] = jnp.zeros_like(inflow_ref)
    for back in range(len(chips), 0, -1):

        @pl.when(core_ref[1] >= back)
        def _():
            if back == len(chips):
                inflow_ref[...] = chips[back - 1][...]
            else:
                passed = stacked(left(steps[back - 1][...]), right(inflow_ref[...]))
                inflow_ref[...] = chips[back - 1][...] + passed


def next_faces(panel, core_ref, faces_ref, resp_ref, *refs):
    first_ref, second_ref, inflow_ref, both = refs[-4:]
    width = inflow_ref.shape[1]
    count = (len(refs) - 3) // 2
    through_chips(core_ref, inflow_ref, refs[:count], refs[count:-4])
    inflow = right(inflow_ref[...])
    first = pl.multiple_of(core_ref[2] * WIDE, WIDE)
    second = pl.multiple_of((1 - core_ref[2]) * WIDE, WIDE)
    for e in range(faces_ref.shape[0]):
        both[...] = faces_ref[e, :, panel * width : (panel + 1) * width] + stacked(resp_ref[e, WIDE:, :], inflow)
        first_ref[e] = both[pl.ds(first, WIDE), :]
        second_ref[e] = both[pl.ds(second, WIDE), :]


def inflow_of_cores(core_ref, q_ref, resp_ref, *refs):
    keep_ref, send_ref = refs[-2:]
    count = (len(refs) - 1) // 2
    through_chips(core_ref, keep_ref, refs[:count], refs[count:-2])
    last = q_ref.shape[0] // CORES - 1

    @pl.when(core_ref[0] == 0)
    def _():
        send_ref[...] = q_ref[last] + stacked(resp_ref[last, :WIDE, :], right(keep_ref[...]))

    @pl.when(core_ref[0] == 1)
    def _():
        send_ref[...] = keep_ref[...]
        keep_ref[...] = q_ref[last] + stacked(resp_ref[last, :WIDE, :], right(send_ref[...]))


def join(core_ref, keep_ref, got_ref, inflow_ref):
    half = keep_ref.shape[1]

    @pl.when(core_ref[0] == 0)
    def _():
        inflow_ref[:, :half] = keep_ref[...]
        inflow_ref[:, half:] = got_ref[...]

    @pl.when(core_ref[0] == 1)
    def _():
        inflow_ref[:, :half] = got_ref[...]
        inflow_ref[:, half:] = keep_ref[...]


def field_without_inflow(panel, core_ref, c_ref, bsn_ref, first_ref, second_ref, got_ref, p_ref, halo):
    elements, width = c_ref.shape[0], first_ref.shape[2]
    half = c_ref.shape[2] // CORES
    for e in range(elements):

        def place(own):
            mine = slice(own * width, (own + 1) * width)
            other = slice((1 - own) * width, (2 - own) * width)
            for k, ref in enumerate((first_ref, second_ref)):
                rows = pl.ds(south_north(core_ref, k), WIDE)
                halo[rows, mine] = ref[own * elements + e]
                halo[rows, other] = got_ref[k, e]

        for k in range(CORES):
            pl.when(core_ref[0] == k)(functools.partial(place, k))
        change = stacked(bsn_ref[e], right(halo[...]))
        for k in range(CORES):
            at = k * half + panel * width
            p_ref[e, :, k * width : (k + 1) * width] = (
                c_ref[e, :, at : at + width] - change[:, k * width : (k + 1) * width]
            )


def whole_field(panel, core_ref, p_ref, bu_ref, keep_ref, got_ref, *refs):
    out_ref, inflow_ref, held, sems = refs[-4:]
    join(core_ref, keep_ref, got_ref, inflow_ref)
    elements, unknowns = held.shape[:2]
    width = keep_ref.shape[1]
    half = out_ref.shape[3] // CORES
    copies = []
    for e in range(elements):
        if e:
            at = 0
            for first, length in face_runs("down"):
                inflow_ref[at : at + length, :] = held[e - 1, first : first + length, :]
                at += length
        value = p_ref[e] - stacked(bu_ref[e], right(inflow_ref[...]))
        held[e] = value[:unknowns]
        for k in range(CORES):
            copy = pltpu.make_async_copy(
                held.at[e, :, pl.ds(k * width, width)],
                out_ref.at[e, :, 0, pl.ds(k * half + panel * width, width)],
                sems.at[e, k],
            )
            copy.start()
            copies.append(copy)
    for copy in copies:
        copy.wait()


def ring(axis, by):
    count = lax.axis_size(axis)
    return [(i, (i + by) % count) for i in range(count)]


def per_device(right_side, start_field, block_inverse, upwind_block, south_block, north_block):
    by_row = lambda x: x.transpose(0, 2, 1, 3)
    rhs, start, inverse, upwind, south, north = map(
        by_row, (right_side, start_field, block_inverse, upwind_block, south_block, north_block)
    )
    elements, unknowns, _, columns = rhs.shape
    depth = -(-unknowns // 128) * 128
    half = columns // CORES
    width = half // PANELS
    count = CORES * elements
    devices, spans = lax.axis_size("sweep"), lax.axis_size("span")
    place = lax.axis_index("sweep")
    odd = lax.axis_index("span") % 2
    where = jnp.stack([place % CORES, place // CORES, odd]).astype(jnp.int32)
    dma = pltpu.SemaphoreType.DMA
    f32, bf16 = jnp.float32, jnp.bfloat16
    core = (SMEM, where)
    face = (elements, FACE, 1, half)

    def held(arrays):
        return [(VMEM, x) for x in arrays]

    def swap(x):
        return lax.ppermute(x, "sweep", [(i, i ^ 1) for i in range(devices)])

    def from_chips(x):
        return [
            lax.ppermute(x, "sweep", ring("sweep", CORES * back))
            for back in range(1, devices // CORES)
        ]

    def along_span(x, second, other_core):
        pairs = []
        for i in range(devices):
            for j in range(spans):
                by = 1 if (j + second) % 2 == 0 else -1
                pairs.append((i * spans + j, (i ^ other_core) * spans + (j + by) % spans))
        return lax.ppermute(x, ("sweep", "span"), pairs)

    runs = start.reshape(elements, NODE**2, VARS * NODE, 1, columns)
    found = call(
        start_faces,
        [(VMEM, (elements, NODE**2, NODE, 1, half), f32)] * 4,
        core, (HBM, runs),
        scratch=[dma((4,))],
    )
    halos = [along_span(found[k].reshape(face), k % 2, k // 2) for k in range(4)]
    raw = [(HBM, x) for x in (inverse, rhs, upwind, south, north)]
    raw_scratch = [
        VMEM((elements, unknowns, unknowns), f32),
        VMEM((elements, unknowns, columns), f32),
        VMEM((elements, 3, unknowns, FACE), f32),
    ]
    fold_scratch = [VMEM((3 * depth, columns + 3 * WIDE), bf16), dma((elements, 5))]
    (own,) = call(
        fold_faces,
        [(VMEM, (CORES, elements, 3 * WIDE, half + 3 * WIDE), f32)],
        *raw,
        scratch=raw_scratch + [VMEM((3 * WIDE, depth), f32)] + fold_scratch,
        us=0,
        limit=MOST,
        after=found,
    )
    cores = lax.all_to_all(
        own, "sweep", 0, 0, axis_index_groups=[[i, i + 1] for i in range(0, devices, CORES)]
    )
    fc, fsn, fu, resp, step = call(
        chip_blocks,
        [
            (VMEM, (count, 3 * WIDE, half), f32),
            (VMEM, (count, 3 * WIDE, 6 * WIDE), bf16),
            (VMEM, (count, 3 * WIDE, 3 * WIDE), bf16),
            (VMEM, (count, 3 * WIDE, 3 * WIDE), bf16),
            (VMEM, (WIDE, WIDE), f32),
        ],
        (VMEM, cores),
        scratch=[VMEM((3 * WIDE, WIDE), f32)],
        us=0,
    )
    steps = from_chips(step)[:-1]
    q, out, halo_stack = call(
        first_traces,
        [
            (VMEM, (count, WIDE, half), f32),
            (VMEM, (WIDE, half), f32),
            (VMEM, (count, 6 * WIDE, half), bf16),
        ],
        core, *held((fc, fsn, fu)), *[(HBM, halos[k]) for k in ORDER],
        scratch=[VMEM((2, 2, elements, FACE, half), f32), dma((4, elements))],
        us=2,
    )
    chips = [from_chips(out)]
    (faces,) = call(
        other_faces,
        [(VMEM, (count, 2 * WIDE, half), f32)],
        *held((fc, fsn, fu, halo_stack, q)),
        us=2,
        after=steps,
    )
    halos, last = [], []
    for p in range(PANELS):
        last = call(
            functools.partial(next_faces, p),
            [(VMEM, (count, WIDE, width), f32)] * 2,
            core, *held((faces, resp, *chips[p], *steps)),
            scratch=[VMEM((WIDE, width), f32), VMEM((2 * WIDE, width), f32)],
            us=1,
            after=last,
        )
        halos.append([along_span(last[k], k, 0) for k in range(2)])
    c, bsn, bu = call(
        fold_rows,
        [
            (VMEM, (elements, depth, columns), f32),
            (VMEM, (elements, depth, 6 * WIDE), bf16),
            (VMEM, (elements, depth, 3 * WIDE), bf16),
        ],
        *raw,
        scratch=raw_scratch + [VMEM((depth, depth), f32)] + fold_scratch,
        us=10,
        after=last,
    )
    field, last = None, [c]
    for p in range(PANELS):
        q, out, away = call(
            functools.partial(last_faces, p),
            [
                (VMEM, (count, WIDE, width), f32),
                (VMEM, (WIDE, width), f32),
                (VMEM, (2, elements, WIDE, width), f32),
            ],
            core, *held((fc, fsn, fu, *halos[p])),
            scratch=[VMEM((2 * WIDE, width), f32)],
            us=1,
            after=last,
        )
        last = [out]
        last_chips = from_chips(out)
        (part,) = call(
            functools.partial(field_without_inflow, p),
            [(VMEM, (elements, depth, CORES * width), f32)],
            core, *held((c, bsn, *halos[p], swap(away))),
            scratch=[VMEM((2 * WIDE, CORES * width), f32)],
            us=1,
        )
        keep, send = call(
            inflow_of_cores,
            [(VMEM, (WIDE, width), f32)] * 2,
            core, *held((q, resp, *last_chips, *steps)),
            after=[part],
        )
        before = [] if field is None else [(HBM, field)]
        (field,) = call(
            functools.partial(whole_field, p),
            [(HBM, rhs.shape, f32)],
            core, *held((part, bu, keep, swap(send))), *before,
            scratch=[
                VMEM((WIDE, CORES * width), f32),
                VMEM((elements, unknowns, CORES * width), f32),
                dma((elements, CORES)),
            ],
            us=1,
            aliases={5: 0} if before else None,
        )
    return by_row(field)


def solution(mesh):
    spec = P("sweep", "span", None, None)
    return jax.shard_map(
        per_device, mesh=mesh, in_specs=(spec,) * 6, out_specs=spec, check_vma=False
    )
```

time: 89.3 us -> 86.8 us (0.972)
  waiting for transfers between devices: 34.6 us -> 21.4 us
  Pallas kernels: 23.2 us -> 32.8 us
    pallas_call x9 -> x11, Pallas kernels: 23.2 us -> 32.8 us  [call(): pl.pallas_call(body, out_shape=[jax.ShapeDtypeStruct(shape, kind) for _,...]
    ppermute x6, waiting for transfers between devices: 20.1 us -> 10.9 us  [along_span(): return lax.ppermute(x, ('sweep', 'span'), pairs)]
    ppermute x6, starting transfers between devices: 11.9 us -> 7.72 us  [along_span(): return lax.ppermute(x, ('sweep', 'span'), pairs)]
    ppermute x6 -> x8, waiting for transfers between devices: 13.6 us -> 9.53 us  [from_chips(): lax.ppermute(x, 'sweep', ring('sweep', CORES * back))]
    ppermute x6 -> x8, starting transfers between devices: 5.35 us -> 8.5 us  [from_chips(): lax.ppermute(x, 'sweep', ring('sweep', CORES * back))]
    ppermute x2, starting transfers between devices: 3.62 us -> 4.86 us  [swap(): return lax.ppermute(x, 'sweep', [(i, i ^ 1) for i in range(devices)])]
    unnamed x10 -> x20, local copies, waits for them, and re-layouts: 1.86 us -> 1.77 us
  transfers between devices with their start and end apart: 14 -> 16, of which waited for: 8 -> 8; matrix products, arithmetic and copies ran while one was open for 0% -> 0% of each run, Pallas kernels for 15% -> 30%
where the time goes in v3:
time: 86.8 us; the launch traced here: 86.3 us
  Pallas kernels  32.8 us (38%)
  waiting for transfers between devices  21.4 us (25%)
  starting transfers between devices  21.1 us (24%)
  blocking collectives  8.84 us (10%)
  local copies, waits for them, and re-layouts  1.77 us (2%)
    pallas_call x11, Pallas kernels, call(): pl.pallas_call(body, out_shape=[jax.ShapeDtypeStruct(shape, kind) for _,...  32.8 us
    ppermute x6, waiting for transfers between devices, along_span(): return lax.ppermute(x, ('sweep', 'span'), pairs)  10.9 us
    ppermute x8, waiting for transfers between devices, from_chips(): lax.ppermute(x, 'sweep', ring('sweep', CORES * back))  9.53 us
    all_to_all x1, blocking collectives, per_device(): lax.all_to_all(own, 'sweep', 0, 0, axis_index_groups=[[i, i + 1] for i in...  8.84 us
    ppermute x8, starting transfers between devices, from_chips(): lax.ppermute(x, 'sweep', ring('sweep', CORES * back))  8.5 us
    ppermute x6, starting transfers between devices, along_span(): return lax.ppermute(x, ('sweep', 'span'), pairs)  7.72 us
    ppermute x2, starting transfers between devices, swap(): return lax.ppermute(x, 'sweep', [(i, i ^ 1) for i in range(devices)])  4.86 us
    unnamed x20, local copies, waits for them, and re-layouts  1.77 us
  transfers between devices with their start and end apart: 16, of which 8 were waited for; matrix products, arithmetic and copies ran while one was open for 0% of the time, Pallas kernels for 30%

profile of v3, /device:TPU:1, one launch (start us, length us, event | category | flops | bytes accessed | tf_op | source)
XLA Modules:
  0.0 86.3 jit_solution(11599711108905658436)
XLA Ops:
  0.0 0.1 pad_add_fusion.refs_0_
  0.1 0.0 copy-start.9
  0.1 1.7 %copy-done.9 = f32[2,1,625,512]{3,1,2,0:T(1,128)S(1)} copy-done((f32[2,1,625,512]{3,1,2,0:T(1,128)S(1)}, f32[2,1,625,512]{3,1,2,0:T(1,128)}, u32[]{:S(2)}) %copy-start.9) | copy-done | bytes 2560024
  1.8 1.0 %start_faces.1 = (f32[2,25,5,1,256]{4,3,2,1,0:T(1,128)S(1)}, f32[2,25,5,1,256]{4,3,2,1,0:T(1,128)S(1)}, f32[2,25,5,1,256]{4,3,2,1,0:T(1,128)S(1)}, f32[2,25,5,1,256]{4,3,2,1,0:T(1,128)S(1)}) custom-call(s32[3]{0:T(128)S(1)} %pad_add_fusion.refs_0_, f32[2,25,25,1,512]{4,3,2,1,0:T(1,128)S(1)} %bitcast.28), custom_call_target="tpu_custom_call" | custom-call | flops 1000000000 | tf_op jit(solution)/shard_map/start_faces/pallas_call | solution.py:68
  2.8 0.0 copy-start.5
  2.8 0.0 copy-start.6
  2.8 0.0 copy-start.7
  2.8 0.0 copy-start.8
  2.8 4.8 %collective-permute-start = (f32[2,125,1,256]{3,2,1,0:T(1,128)S(1)}, f32[2,125,1,256]{3,2,1,0:T(1,128)S(1)}, u32[]{:S(2)}, u32[]{:S(2)}) collective-permute-start(f32[2,125,1,256]{3,2,1,0:T(1,128)S(1)} %bitcast.27), channel_id=1, source_target_pairs={{0,7},{1,6},{2,5},{3,4},{4,3},{5,2},{6,1},{7,0},{8,15},{9,14},{10,... | collective-permute-start | bytes 768008 | tf_op jit(solution)/shard_map/ppermute | solution.py:392
  7.6 0.0 collective-permute-start.2
  7.6 0.2 collective-permute-start.1
  7.8 0.9 %collective-permute-start.3 = (f32[2,125,1,256]{3,2,1,0:T(1,128)S(1)}, f32[2,125,1,256]{3,2,1,0:T(1,128)}, u32[]{:S(2)}, u32[]{:S(2)}) collective-permute-start(f32[2,125,1,256]{3,2,1,0:T(1,128)S(1)} %bitcast.24), channel_id=1, source_target_pairs={{0,1},{1,0},{2,3},{3,2},{4,5},{5,4},{6,7},{7,6},{8,9},{9,8},{10,11... | collective-permute-start | bytes 768008 | tf_op jit(solution)/shard_map/ppermute | solution.py:392
  8.8 0.0 copy-done.5
  8.8 0.0 copy-done.6
  8.8 0.0 copy-done.7
  8.8 0.0 copy-done.8
  8.8 7.9 %fold_faces.1 = f32[2,2,384,640]{3,2,1,0:T(8,128)} custom-call(f32[2,625,1,625]{3,2,1,0:T(1,128)} %bitcast.14, f32[2,625,1,512]{3,2,1,0:T(1,128)} %bitcast.16, f32[2,625,1,125]{3,2,1,0:T(1,128)} %bitcast.18, f32[2,625,1,125]{3,2,1,0:T(1,128)} %bitcast.20, f32[2,625,1,125]{3,2,1,0:T(1,128)} %bitcast.22, f32[2,25,5,1,256]{4,3,2,1,0:T(1,128)} %copy-done.5, ...), custom_call_target="tpu_custom_call" | custom-call | tf_op jit(solution)/shard_map/fold_faces/pallas_call | solution.py:68
  16.7 8.8 %all_to_all.5.refs_0_ = f32[2,2,384,640]{3,2,1,0:T(8,128)S(1)} all-to-all(f32[2,2,384,640]{3,2,1,0:T(8,128)} %fold_faces.1), channel_id=1, replica_groups={{0,4},{8,12},{16,20},{24,28},{1,5},{9,13},{17,21},{25,29},{2,6},{10,14}..., dimensions={0} | all-to-all | bytes 7864320 | tf_op jit(solution)/shard_map/all_to_all | solution.py:418
  25.6 1.1 %chip_blocks.1 = (f32[4,384,256]{2,1,0:T(8,128)S(1)}, bf16[4,384,768]{2,1,0:T(8,128)(2,1)S(1)}, bf16[4,384,384]{2,1,0:T(8,128)(2,1)S(1)}, bf16[4,384,384]{2,1,0:T(8,128)(2,1)S(1)}, f32[128,128]{1,0:T(8,128)S(1)}) custom-call(f32[2,2,384,640]{3,2,1,0:T(8,128)S(1)} %all_to_all.5.refs_0_), custom_call_target="tpu_custom_call" | custom-call | tf_op jit(solution)/shard_map/chip_blocks/pallas_call | solution.py:68
  26.7 1.3 %collective-permute-start.5 = (f32[128,128]{1,0:T(8,128)S(1)}, f32[128,128]{1,0:T(8,128)S(1)}, u32[]{:S(2)}, u32[]{:S(2)}) collective-permute-start(f32[128,128]{1,0:T(8,128)S(1)} %get-tuple-element.36), channel_id=1, source_target_pairs={{0,16},{4,20},{8,24},{12,28},{16,0},{20,4},{24,8},{28,12},{1,17},{... | collective-permute-start | bytes 196616 | tf_op jit(solution)/shard_map/ppermute | solution.py:382
  28.0 0.0 collective-permute-done.refs_4_
  28.0 1.2 %collective-permute-start.4 = (f32[128,128]{1,0:T(8,128)S(1)}, f32[128,128]{1,0:T(8,128)S(1)}, u32[]{:S(2)}, u32[]{:S(2)}) collective-permute-start(f32[128,128]{1,0:T(8,128)S(1)} %get-tuple-element.36), channel_id=1, source_target_pairs={{0,8},{4,12},{8,16},{12,20},{16,24},{20,28},{24,0},{28,4},{1,9},{5... | collective-permute-start | bytes 196616 | tf_op jit(solution)/shard_map/ppermute | solution.py:382
  29.3 0.0 collective-permute-done.2.refs_6_
  29.3 0.0 collective-permute-done.1.refs_5_
  29.3 1.1 %collective-permute-done.3.refs_7_ = f32[2,125,1,256]{3,2,1,0:T(1,128)} collective-permute-done((f32[2,125,1,256]{3,2,1,0:T(1,128)S(1)}, f32[2,125,1,256]{3,2,1,0:T(1,128)}, u32[]{:S(2)}, u32[]{:S(2)}) %collective-permute-start.3) | collective-permute-done | bytes 256032 | tf_op jit(solution)/shard_map/ppermute | solution.py:392
  30.3 3.0 %first_traces.1 = (f32[4,128,256]{2,1,0:T(8,128)S(1)}, f32[128,256]{1,0:T(8,128)S(1)}, bf16[4,768,256]{2,1,0:T(8,128)(2,1)S(1)}) custom-call(s32[3]{0:T(128)S(1)} %pad_add_fusion.refs_0_, f32[4,384,256]{2,1,0:T(8,128)S(1)} %get-tuple-element.31.refs_1_.refs_0_, bf16[4,384,768]{2,1,0:T(8,128)(2,1)S(1)} %get-tuple-element.32.refs_2_.refs_1_, ...), custom_call_target="tpu_custom_call" | custom-call | flops 2000000000 | tf_op jit(solution)/shard_map/first_traces/pallas_call | solution.py:68
  33.4 2.7 %collective-permute-start.8 = (f32[128,256]{1,0:T(8,128)S(1)}, f32[128,256]{1,0:T(8,128)S(1)}, u32[]{:S(2)}, u32[]{:S(2)}) collective-permute-start(f32[128,256]{1,0:T(8,128)S(1)} %get-tuple-element.38), channel_id=1, source_target_pairs={{0,24},{4,28},{8,0},{12,4},{16,8},{20,12},{24,16},{28,20},{1,25},{... | collective-permute-start | bytes 393224 | tf_op jit(solution)/shard_map/ppermute | solution.py:382
  36.1 0.2 collective-permute-start.7
  36.3 0.3 collective-permute-start.6
  36.6 0.0 collective-permute-done.5.refs_6_.refs_7_
  36.6 0.0 collective-permute-done.4.refs_5_.refs_6_
  36.6 0.0 copy-start.2
  36.6 0.0 copy-start.3
  36.6 0.0 copy-start.4
  36.7 0.8 other_faces.1.refs_1_
  37.4 0.0 copy-start
  37.5 1.1 %collective-permute-done.8.refs_5_ = f32[128,256]{1,0:T(8,128)S(1)} collective-permute-done((f32[128,256]{1,0:T(8,128)S(1)}, f32[128,256]{1,0:T(8,128)S(1)}, u32[]{:S(2)}, u32[]{:S(2)}) %collective-permute-start.8) | collective-permute-done | bytes 131104 | tf_op jit(solution)/shard_map/ppermute | solution.py:382
  38.5 2.2 %collective-permute-done.7.refs_4_ = f32[128,256]{1,0:T(8,128)S(1)} collective-permute-done((f32[128,256]{1,0:T(8,128)S(1)}, f32[128,256]{1,0:T(8,128)S(1)}, u32[]{:S(2)}, u32[]{:S(2)}) %collective-permute-start.7) | collective-permute-done | bytes 131104 | tf_op jit(solution)/shard_map/ppermute | solution.py:382
  40.8 1.4 %collective-permute-done.6.refs_3_ = f32[128,256]{1,0:T(8,128)S(1)} collective-permute-done((f32[128,256]{1,0:T(8,128)S(1)}, f32[128,256]{1,0:T(8,128)S(1)}, u32[]{:S(2)}, u32[]{:S(2)}) %collective-permute-start.6) | collective-permute-done | bytes 131104 | tf_op jit(solution)/shard_map/ppermute | solution.py:382
  42.1 1.3 %next_faces.1 = (f32[4,128,256]{2,1,0:T(8,128)S(1)}, f32[4,128,256]{2,1,0:T(8,128)S(1)}) custom-call(s32[3]{0:T(128)S(1)} %pad_add_fusion.refs_0_, f32[4,256,256]{2,1,0:T(8,128)S(1)} %other_faces.1.refs_1_, bf16[4,384,384]{2,1,0:T(8,128)(2,1)S(1)} %get-tuple-element.37.refs_2_, f32[128,256]{1,0:T(8,128)S(1)} %collective-permute-done.6.refs_3_, ...), custom_call_target="tpu_custom_call" | custom-call | flops 1000000000 | tf_op jit(solution)/shard_map/next_faces/pallas_call | solution.py:68
  43.4 1.7 %collective-permute-start.9 = (f32[4,128,256]{2,1,0:T(8,128)S(1)}, f32[4,128,256]{2,1,0:T(8,128)S(1)}, u32[]{:S(2)}, u32[]{:S(2)}) collective-permute-start(f32[4,128,256]{2,1,0:T(8,128)S(1)} %get-tuple-element.39.refs_5_), channel_id=1, source_target_pairs={{0,1},{1,0},{2,3},{3,2},{4,5},{5,4},{6,7},{7,6},{8,9},{9,8},{10,11... | collective-permute-start | bytes 1572872 | tf_op jit(solution)/shard_map/ppermute | solution.py:392
  45.1 0.0 collective-permute-start.10
  45.2 0.0 copy-done.1
  45.2 0.0 copy-done.2
  45.2 0.0 copy-done.3
  45.2 0.0 copy-done.4
  45.2 0.0 copy-done
  45.2 10.8 %fold_rows.1 = (f32[2,640,512]{2,1,0:T(8,128)S(1)}, bf16[2,640,768]{2,1,0:T(8,128)(2,1)S(1)}, bf16[2,640,384]{2,1,0:T(8,128)(2,1)S(1)}) custom-call(f32[2,625,1,625]{3,2,1,0:T(1,128)S(1)} %bitcast.15, f32[2,625,1,512]{3,2,1,0:T(1,128)S(1)} %bitcast.17, f32[2,625,1,125]{3,2,1,0:T(1,128)S(1)} %bitcast.19, f32[2,625,1,125]{3,2,1,0:T(1,128)S(1)} %bitcast.21, ...), custom_call_target="tpu_custom_call" | custom-call | flops 10000000000 | tf_op jit(solution)/shard_map/fold_rows/pallas_call | solution.py:68
  56.0 0.0 collective-permute-done.9.refs_4_.refs_3_
  56.0 9.8 %collective-permute-done.10.refs_5_.refs_4_ = f32[4,128,256]{2,1,0:T(8,128)S(1)} collective-permute-done((f32[4,128,256]{2,1,0:T(8,128)S(1)}, f32[4,128,256]{2,1,0:T(8,128)S(1)}, u32[]{:S(2)}, u32[]{:S(2)}) %collective-permute-start.10) | collective-permute-done | bytes 524320 | tf_op jit(solution)/shard_map/ppermute | solution.py:392
  65.8 1.4 %last_faces.1 = (f32[4,128,256]{2,1,0:T(8,128)S(1)}, f32[128,256]{1,0:T(8,128)S(1)}, f32[2,2,128,256]{3,2,1,0:T(8,128)S(1)}) custom-call(s32[3]{0:T(128)S(1)} %pad_add_fusion.refs_0_, f32[4,384,256]{2,1,0:T(8,128)S(1)} %get-tuple-element.31.refs_1_.refs_0_, bf16[4,384,768]{2,1,0:T(8,128)(2,1)S(1)} %get-tuple-element.32.refs_2_.refs_1_, ...), custom_call_target="tpu_custom_call" | custom-call | flops 1000000000 | tf_op jit(solution)/shard_map/last_faces/pallas_call | solution.py:68
  67.3 3.6 %collective-permute-start.11 = (f32[2,2,128,256]{3,2,1,0:T(8,128)S(1)}, f32[2,2,128,256]{3,2,1,0:T(8,128)S(1)}, u32[]{:S(2)}, u32[]{:S(2)}) collective-permute-start(f32[2,2,128,256]{3,2,1,0:T(8,128)S(1)} %get-tuple-element.43), channel_id=1, source_target_pairs={{0,4},{4,0},{8,12},{12,8},{16,20},{20,16},{24,28},{28,24},{1,5},{5... | collective-permute-start | bytes 1572872 | tf_op jit(solution)/shard_map/ppermute | solution.py:378
  70.9 2.0 %collective-permute-start.14 = (f32[128,256]{1,0:T(8,128)S(1)}, f32[128,256]{1,0:T(8,128)S(1)}, u32[]{:S(2)}, u32[]{:S(2)}) collective-permute-start(f32[128,256]{1,0:T(8,128)S(1)} %get-tuple-element.46), channel_id=1, source_target_pairs={{0,24},{4,28},{8,0},{12,4},{16,8},{20,12},{24,16},{28,20},{1,25},{... | collective-permute-start | bytes 393224 | tf_op jit(solution)/shard_map/ppermute | solution.py:382
  72.9 0.7 collective-permute-start.13
  73.6 0.0 collective-permute-start.12
  73.6 0.0 collective-permute-done.11.refs_5_
  73.6 2.0 %field_without_inflow.1.refs_8_.refs_1_ = f32[2,640,512]{2,1,0:T(8,128)S(1)} custom-call(s32[3]{0:T(128)S(1)} %pad_add_fusion.refs_0_, f32[2,640,512]{2,1,0:T(8,128)S(1)} %get-tuple-element.41.refs_6_.refs_1_, bf16[2,640,768]{2,1,0:T(8,128)(2,1)S(1)} %get-tuple-element.42.refs_2_, f32[4,128,256]{2,1,0:T(8,128)S(1)} %collective-permute-done.9.refs_4_.refs_3_, ...), custom_call_target="tpu_custom_call" | custom-call | flops 1000000000 | tf_op jit(solution)/shard_map/field_without_inflow/pallas_call | solution.py:68
  75.6 0.5 collective-permute-done.14.refs_5_
  76.1 4.3 %collective-permute-done.13.refs_4_ = f32[128,256]{1,0:T(8,128)S(1)} collective-permute-done((f32[128,256]{1,0:T(8,128)S(1)}, f32[128,256]{1,0:T(8,128)S(1)}, u32[]{:S(2)}, u32[]{:S(2)}) %collective-permute-start.13) | collective-permute-done | bytes 131104 | tf_op jit(solution)/shard_map/ppermute | solution.py:382
  80.5 0.0 collective-permute-done.12.refs_3_
  80.5 0.8 inflow_of_cores.1
  81.2 1.2 %collective-permute-start.15 = (f32[128,256]{1,0:T(8,128)S(1)}, f32[128,256]{1,0:T(8,128)S(1)}, u32[]{:S(2)}, u32[]{:S(2)}) collective-permute-start(f32[128,256]{1,0:T(8,128)S(1)} %get-tuple-element.48), channel_id=1, source_target_pairs={{0,4},{4,0},{8,12},{12,8},{16,20},{20,16},{24,28},{28,24},{1,5},{5... | collective-permute-start | bytes 393224 | tf_op jit(solution)/shard_map/ppermute | solution.py:378
  82.5 1.0 %collective-permute-done.15.refs_4_ = f32[128,256]{1,0:T(8,128)S(1)} collective-permute-done((f32[128,256]{1,0:T(8,128)S(1)}, f32[128,256]{1,0:T(8,128)S(1)}, u32[]{:S(2)}, u32[]{:S(2)}) %collective-permute-start.15) | collective-permute-done | bytes 131104 | tf_op jit(solution)/shard_map/ppermute | solution.py:378
  83.5 2.7 %whole_field.1 = f32[2,625,1,512]{3,2,1,0:T(1,128)} custom-call(s32[3]{0:T(128)S(1)} %pad_add_fusion.refs_0_, f32[2,640,512]{2,1,0:T(8,128)S(1)} %field_without_inflow.1.refs_8_.refs_1_, bf16[2,640,384]{2,1,0:T(8,128)(2,1)S(1)} %get-tuple-element.44.refs_2_, f32[128,256]{1,0:T(8,128)S(1)} %get-tuple-element.47.refs_3_, ...), custom_call_target="tpu_custom_call" | custom-call | flops 1000000000 | tf_op jit(solution)/shard_map/whole_field/pallas_call | solution.py:68
  (1 shorter events, 0.0 us)
Async XLA Ops:
  0.1 1.7 %copy-start.9 = (f32[2,1,625,512]{3,1,2,0:T(1,128)S(1)}, f32[2,1,625,512]{3,1,2,0:T(1,128)}, u32[]{:S(2)}) copy-start(f32[2,1,625,512]{3,1,2,0:T(1,128)} %param.7) | copy-start | bytes 7680004
  2.8 6.0 %copy-start.5 = (f32[2,25,5,1,256]{4,3,2,1,0:T(1,128)}, f32[2,25,5,1,256]{4,3,2,1,0:T(1,128)S(1)}, u32[]{:S(2)}) copy-start(f32[2,25,5,1,256]{4,3,2,1,0:T(1,128)S(1)} %get-tuple-element.27.refs_5_) | copy-start | bytes 768004
  2.8 6.0 %copy-start.6 = (f32[2,25,5,1,256]{4,3,2,1,0:T(1,128)}, f32[2,25,5,1,256]{4,3,2,1,0:T(1,128)S(1)}, u32[]{:S(2)}) copy-start(f32[2,25,5,1,256]{4,3,2,1,0:T(1,128)S(1)} %get-tuple-element.28.refs_6_) | copy-start | bytes 768004
  2.8 6.0 %copy-start.7 = (f32[2,25,5,1,256]{4,3,2,1,0:T(1,128)}, f32[2,25,5,1,256]{4,3,2,1,0:T(1,128)S(1)}, u32[]{:S(2)}) copy-start(f32[2,25,5,1,256]{4,3,2,1,0:T(1,128)S(1)} %get-tuple-element.29.refs_7_) | copy-start | bytes 768004
  2.8 6.0 %copy-start.8 = (f32[2,25,5,1,256]{4,3,2,1,0:T(1,128)}, f32[2,25,5,1,256]{4,3,2,1,0:T(1,128)S(1)}, u32[]{:S(2)}) copy-start(f32[2,25,5,1,256]{4,3,2,1,0:T(1,128)S(1)} %get-tuple-element.30.refs_8_) | copy-start | bytes 768004
  2.8 25.2 %collective-permute-start = (f32[2,125,1,256]{3,2,1,0:T(1,128)S(1)}, f32[2,125,1,256]{3,2,1,0:T(1,128)S(1)}, u32[]{:S(2)}, u32[]{:S(2)}) collective-permute-start(f32[2,125,1,256]{3,2,1,0:T(1,128)S(1)} %bitcast.27), channel_id=1, source_target_pairs={{0,7},{1,6},{2,5},{3,4},{4,3},{5,2},{6,1},{7,0},{8,15},{9,14},{10,... | collective-permute-start | bytes 768008 | tf_op jit(solution)/shard_map/ppermute | solution.py:392
  7.6 21.7 %collective-permute-start.2 = (f32[2,125,1,256]{3,2,1,0:T(1,128)S(1)}, f32[2,125,1,256]{3,2,1,0:T(1,128)S(1)}, u32[]{:S(2)}, u32[]{:S(2)}) collective-permute-start(f32[2,125,1,256]{3,2,1,0:T(1,128)S(1)} %bitcast.26), channel_id=1, source_target_pairs={{0,5},{1,4},{2,7},{3,6},{4,1},{5,0},{6,3},{7,2},{8,13},{9,12},{10,... | collective-permute-start | bytes 768008 | tf_op jit(solution)/shard_map/ppermute | solution.py:392
  7.6 21.7 %collective-permute-start.1 = (f32[2,125,1,256]{3,2,1,0:T(1,128)S(1)}, f32[2,125,1,256]{3,2,1,0:T(1,128)S(1)}, u32[]{:S(2)}, u32[]{:S(2)}) collective-permute-start(f32[2,125,1,256]{3,2,1,0:T(1,128)S(1)} %bitcast.25), channel_id=1, source_target_pairs={{0,3},{1,2},{2,1},{3,0},{4,7},{5,6},{6,5},{7,4},{8,11},{9,10},{10,... | collective-permute-start | bytes 768008 | tf_op jit(solution)/shard_map/ppermute | solution.py:392
  7.8 22.5 %collective-permute-start.3 = (f32[2,125,1,256]{3,2,1,0:T(1,128)S(1)}, f32[2,125,1,256]{3,2,1,0:T(1,128)}, u32[]{:S(2)}, u32[]{:S(2)}) collective-permute-start(f32[2,125,1,256]{3,2,1,0:T(1,128)S(1)} %bitcast.24), channel_id=1, source_target_pairs={{0,1},{1,0},{2,3},{3,2},{4,5},{5,4},{6,7},{7,6},{8,9},{9,8},{10,11... | collective-permute-start | bytes 768008 | tf_op jit(solution)/shard_map/ppermute | solution.py:392
  26.7 9.9 %collective-permute-start.5 = (f32[128,128]{1,0:T(8,128)S(1)}, f32[128,128]{1,0:T(8,128)S(1)}, u32[]{:S(2)}, u32[]{:S(2)}) collective-permute-start(f32[128,128]{1,0:T(8,128)S(1)} %get-tuple-element.36), channel_id=1, source_target_pairs={{0,16},{4,20},{8,24},{12,28},{16,0},{20,4},{24,8},{28,12},{1,17},{... | collective-permute-start | bytes 196616 | tf_op jit(solution)/shard_map/ppermute | solution.py:382
  28.0 8.6 %collective-permute-start.4 = (f32[128,128]{1,0:T(8,128)S(1)}, f32[128,128]{1,0:T(8,128)S(1)}, u32[]{:S(2)}, u32[]{:S(2)}) collective-permute-start(f32[128,128]{1,0:T(8,128)S(1)} %get-tuple-element.36), channel_id=1, source_target_pairs={{0,8},{4,12},{8,16},{12,20},{16,24},{20,28},{24,0},{28,4},{1,9},{5... | collective-permute-start | bytes 196616 | tf_op jit(solution)/shard_map/ppermute | solution.py:382
  33.4 5.2 %collective-permute-start.8 = (f32[128,256]{1,0:T(8,128)S(1)}, f32[128,256]{1,0:T(8,128)S(1)}, u32[]{:S(2)}, u32[]{:S(2)}) collective-permute-start(f32[128,256]{1,0:T(8,128)S(1)} %get-tuple-element.38), channel_id=1, source_target_pairs={{0,24},{4,28},{8,0},{12,4},{16,8},{20,12},{24,16},{28,20},{1,25},{... | collective-permute-start | bytes 393224 | tf_op jit(solution)/shard_map/ppermute | solution.py:382
  36.1 4.7 %collective-permute-start.7 = (f32[128,256]{1,0:T(8,128)S(1)}, f32[128,256]{1,0:T(8,128)S(1)}, u32[]{:S(2)}, u32[]{:S(2)}) collective-permute-start(f32[128,256]{1,0:T(8,128)S(1)} %get-tuple-element.38), channel_id=1, source_target_pairs={{0,16},{4,20},{8,24},{12,28},{16,0},{20,4},{24,8},{28,12},{1,17},{... | collective-permute-start | bytes 393224 | tf_op jit(solution)/shard_map/ppermute | solution.py:382
  36.3 5.8 %collective-permute-start.6 = (f32[128,256]{1,0:T(8,128)S(1)}, f32[128,256]{1,0:T(8,128)S(1)}, u32[]{:S(2)}, u32[]{:S(2)}) collective-permute-start(f32[128,256]{1,0:T(8,128)S(1)} %get-tuple-element.38), channel_id=1, source_target_pairs={{0,8},{4,12},{8,16},{12,20},{16,24},{20,28},{24,0},{28,4},{1,9},{5... | collective-permute-start | bytes 393224 | tf_op jit(solution)/shard_map/ppermute | solution.py:382
  36.6 8.5 %copy-start.1 = (f32[2,1,625,512]{3,1,2,0:T(1,128)S(1)}, f32[2,1,625,512]{3,1,2,0:T(1,128)}, u32[]{:S(2)}) copy-start(f32[2,1,625,512]{3,1,2,0:T(1,128)} %param.6) | copy-start | bytes 7680004
  36.6 8.5 %copy-start.2 = (f32[2,1,625,125]{3,1,2,0:T(1,128)S(1)}, f32[2,1,625,125]{3,1,2,0:T(1,128)}, u32[]{:S(2)}) copy-start(f32[2,1,625,125]{3,1,2,0:T(1,128)} %param.9) | copy-start | bytes 1875004
  36.6 8.5 %copy-start.3 = (f32[2,1,625,125]{3,1,2,0:T(1,128)S(1)}, f32[2,1,625,125]{3,1,2,0:T(1,128)}, u32[]{:S(2)}) copy-start(f32[2,1,625,125]{3,1,2,0:T(1,128)} %param.10) | copy-start | bytes 1875004
  36.6 8.5 %copy-start.4 = (f32[2,1,625,125]{3,1,2,0:T(1,128)S(1)}, f32[2,1,625,125]{3,1,2,0:T(1,128)}, u32[]{:S(2)}) copy-start(f32[2,1,625,125]{3,1,2,0:T(1,128)} %param.11) | copy-start | bytes 1875004
  37.4 7.7 %copy-start = (f32[2,1,625,625]{3,1,2,0:T(1,128)S(1)}, f32[2,1,625,625]{3,1,2,0:T(1,128)}, u32[]{:S(2)}) copy-start(f32[2,1,625,625]{3,1,2,0:T(1,128)} %param.8) | copy-start | bytes 9375004
  43.4 12.6 %collective-permute-start.9 = (f32[4,128,256]{2,1,0:T(8,128)S(1)}, f32[4,128,256]{2,1,0:T(8,128)S(1)}, u32[]{:S(2)}, u32[]{:S(2)}) collective-permute-start(f32[4,128,256]{2,1,0:T(8,128)S(1)} %get-tuple-element.39.refs_5_), channel_id=1, source_target_pairs={{0,1},{1,0},{2,3},{3,2},{4,5},{5,4},{6,7},{7,6},{8,9},{9,8},{10,11... | collective-permute-start | bytes 1572872 | tf_op jit(solution)/shard_map/ppermute | solution.py:392
  45.1 20.7 %collective-permute-start.10 = (f32[4,128,256]{2,1,0:T(8,128)S(1)}, f32[4,128,256]{2,1,0:T(8,128)S(1)}, u32[]{:S(2)}, u32[]{:S(2)}) collective-permute-start(f32[4,128,256]{2,1,0:T(8,128)S(1)} %get-tuple-element.40.refs_6_), channel_id=1, source_target_pairs={{0,3},{1,2},{2,1},{3,0},{4,7},{5,6},{6,5},{7,4},{8,11},{9,10},{10,... | collective-permute-start | bytes 1572872 | tf_op jit(solution)/shard_map/ppermute | solution.py:392
  67.3 6.3 %collective-permute-start.11 = (f32[2,2,128,256]{3,2,1,0:T(8,128)S(1)}, f32[2,2,128,256]{3,2,1,0:T(8,128)S(1)}, u32[]{:S(2)}, u32[]{:S(2)}) collective-permute-start(f32[2,2,128,256]{3,2,1,0:T(8,128)S(1)} %get-tuple-element.43), channel_id=1, source_target_pairs={{0,4},{4,0},{8,12},{12,8},{16,20},{20,16},{24,28},{28,24},{1,5},{5... | collective-permute-start | bytes 1572872 | tf_op jit(solution)/shard_map/ppermute | solution.py:378
  70.9 5.2 %collective-permute-start.14 = (f32[128,256]{1,0:T(8,128)S(1)}, f32[128,256]{1,0:T(8,128)S(1)}, u32[]{:S(2)}, u32[]{:S(2)}) collective-permute-start(f32[128,256]{1,0:T(8,128)S(1)} %get-tuple-element.46), channel_id=1, source_target_pairs={{0,24},{4,28},{8,0},{12,4},{16,8},{20,12},{24,16},{28,20},{1,25},{... | collective-permute-start | bytes 393224 | tf_op jit(solution)/shard_map/ppermute | solution.py:382
  72.9 7.5 %collective-permute-start.13 = (f32[128,256]{1,0:T(8,128)S(1)}, f32[128,256]{1,0:T(8,128)S(1)}, u32[]{:S(2)}, u32[]{:S(2)}) collective-permute-start(f32[128,256]{1,0:T(8,128)S(1)} %get-tuple-element.46), channel_id=1, source_target_pairs={{0,16},{4,20},{8,24},{12,28},{16,0},{20,4},{24,8},{28,12},{1,17},{... | collective-permute-start | bytes 393224 | tf_op jit(solution)/shard_map/ppermute | solution.py:382
  73.6 6.9 %collective-permute-start.12 = (f32[128,256]{1,0:T(8,128)S(1)}, f32[128,256]{1,0:T(8,128)S(1)}, u32[]{:S(2)}, u32[]{:S(2)}) collective-permute-start(f32[128,256]{1,0:T(8,128)S(1)} %get-tuple-element.46), channel_id=1, source_target_pairs={{0,8},{4,12},{8,16},{12,20},{16,24},{20,28},{24,0},{28,4},{1,9},{5... | collective-permute-start | bytes 393224 | tf_op jit(solution)/shard_map/ppermute | solution.py:382
  81.2 2.2 %collective-permute-start.15 = (f32[128,256]{1,0:T(8,128)S(1)}, f32[128,256]{1,0:T(8,128)S(1)}, u32[]{:S(2)}, u32[]{:S(2)}) collective-permute-start(f32[128,256]{1,0:T(8,128)S(1)} %get-tuple-element.48), channel_id=1, source_target_pairs={{0,4},{4,0},{8,12},{12,8},{16,20},{20,16},{24,28},{28,24},{1,5},{5... | collective-permute-start | bytes 393224 | tf_op jit(solution)/shard_map/ppermute | solution.py:378

commit v4 on v3

v4 whole, which is shorter than its diff:
```python
import functools

import jax
import jax.numpy as jnp
from jax import lax
from jax.experimental import pallas as pl
from jax.experimental.pallas import tpu as pltpu
from jax.sharding import PartitionSpec as P

VARS = 5
NODE = 5
FACE = VARS * NODE**2
WIDE = 128
SWEEPS = 2
CORES = 2
ORDER = (3, 1, 2, 0)
LIMIT = 24 * 1024 * 1024
MOST = 60 * 1024 * 1024
ANY = pl.ANY
HBM = pltpu.HBM
VMEM = pltpu.VMEM
SMEM = pltpu.SMEM


def face_runs(kind):
    if kind == "down":
        return [(var * NODE**3 + (NODE - 1) * NODE**2, NODE**2) for var in range(VARS)]
    b = NODE - 1 if kind == "high" else 0
    return [
        (var * NODE**3 + a * NODE**2 + b * NODE, NODE)
        for var in range(VARS)
        for a in range(NODE)
    ]


def split(x):
    top = x.astype(jnp.bfloat16)
    return top, (x - top.astype(jnp.float32)).astype(jnp.bfloat16)


def left(x):
    high, low = split(x)
    return jnp.concatenate([high, high, low], axis=1)


def right(x):
    high, low = split(x)
    return jnp.concatenate([high, low, high], axis=0)


def stacked(a, b):
    return jnp.dot(a, b, preferred_element_type=jnp.float32)


def padded(x, rows):
    short = rows - x.shape[0]
    return jnp.concatenate([x, jnp.zeros((short, x.shape[1]), x.dtype)], axis=0) if short else x


def call(kernel, outs, *args, scratch=(), us=1, after=(), limit=LIMIT, aliases=None):
    args = list(args) + [(ANY, x) for x in after]

    def body(*refs):
        given = len(args) - len(after)
        kernel(*refs[:given], *refs[len(args) :])

    return pl.pallas_call(
        body,
        out_shape=[jax.ShapeDtypeStruct(shape, kind) for _, shape, kind in outs],
        in_specs=[pl.BlockSpec(memory_space=space) for space, _ in args],
        out_specs=[pl.BlockSpec(memory_space=space) for space, _, _ in outs],
        scratch_shapes=list(scratch),
        input_output_aliases=aliases or {},
        compiler_params=pltpu.CompilerParams(vmem_limit_bytes=limit),
        cost_estimate=pl.CostEstimate(flops=int(us * 10**9), bytes_accessed=0, transcendentals=0),
        name=getattr(kernel, "func", kernel).__name__,
    )(*[array for _, array in args])


def start_faces(core_ref, field_ref, *refs):
    outs, sems = refs[:-1], refs[-1]
    half = outs[0].shape[-1]
    parts = []
    for k, out in enumerate(outs):
        own = core_ref[0] if k < 2 else 1 - core_ref[0]
        low = core_ref[2] if k % 2 == 0 else 1 - core_ref[2]
        part = pltpu.make_async_copy(
            field_ref.at[
                :, :, pl.ds((1 - low) * (NODE - 1) * NODE, NODE), :,
                pl.ds(pl.multiple_of(own * half, half), half),
            ],
            out,
            sems.at[k],
        )
        part.start()
        parts.append(part)
    for part in parts:
        part.wait()


def load_rows(pairs, sems):
    copies = []
    for k, (source, held) in enumerate(pairs):
        copies.append(pltpu.make_async_copy(source, held, sems.at[k]))
        copies[-1].start()
    return copies


def load_blocks(inv_ref, rhs_ref, up_ref, south_ref, north_ref, inv, rhs, blocks, sems):
    return [
        load_rows(
            [
                (inv_ref.at[e, :, 0, :], inv.at[e]),
                (rhs_ref.at[e, :, 0, :], rhs.at[e]),
                (south_ref.at[e, :, 0, :], blocks.at[e, 0]),
                (north_ref.at[e, :, 0, :], blocks.at[e, 1]),
                (up_ref.at[e, :, 0, :], blocks.at[e, 2]),
            ],
            sems.at[e],
        )
        for e in range(inv_ref.shape[0])
    ]


def fill_columns(e, depth, rhs, blocks, columns):
    wide = rhs.shape[2]
    columns[:, :wide] = right(padded(rhs[e], depth))
    for k in range(3):
        at = wide + k * WIDE
        block = right(padded(blocks[e, k], depth))
        columns[:, at : at + FACE] = block


def fold_faces(inv_ref, rhs_ref, up_ref, south_ref, north_ref, faces_ref,
               inv, rhs, blocks, rows, columns, sems):
    elements, depth, wide = inv.shape[0], rows.shape[1], rhs.shape[2]
    half = wide // CORES
    copies = load_blocks(inv_ref, rhs_ref, up_ref, south_ref, north_ref, inv, rhs, blocks, sems)
    rows[...] = jnp.zeros_like(rows)
    columns[...] = jnp.zeros_like(columns)
    for e in range(elements):
        copies[e][0].wait()
        for f, kind in enumerate(("down", "high", "low")):
            at = f * WIDE
            for first, length in face_runs(kind):
                rows[at : at + length, : inv.shape[2]] = inv[e, first : first + length, :]
                at += length
        for copy in copies[e][1:]:
            copy.wait()
        fill_columns(e, depth, rhs, blocks, columns)
        product = stacked(left(rows[...]), columns[...])
        for k in range(CORES):
            faces_ref[k, e, :, :half] = product[:, k * half : (k + 1) * half]
            faces_ref[k, e, :, half:] = product[:, wide:]


def fold_element(e, raw, outs, inv, rhs, blocks, rows, columns, sems):
    inv_ref, rhs_ref, up_ref, south_ref, north_ref = raw
    unknowns = inv.shape[1]
    depth, wide = rows.shape[1], rhs.shape[2]
    copies = load_rows(
        [
            (inv_ref.at[e, :, 0, :], inv.at[0]),
            (rhs_ref.at[e, :, 0, :], rhs.at[0]),
            (south_ref.at[e, :, 0, :], blocks.at[0, 0]),
            (north_ref.at[e, :, 0, :], blocks.at[0, 1]),
            (up_ref.at[e, :, 0, :], blocks.at[0, 2]),
        ],
        sems,
    )
    rows[...] = jnp.zeros_like(rows)
    columns[...] = jnp.zeros_like(columns)
    for copy in copies:
        copy.wait()
    rows[:unknowns, :unknowns] = inv[0]
    fill_columns(0, depth, rhs, blocks, columns)
    product = stacked(left(rows[...]), columns[...])
    c_ref, bsn_ref, bu_ref = outs
    c_ref[...] = product[:, :wide]
    bsn_ref[...] = left(product[:, wide : wide + 2 * WIDE])
    bu_ref[...] = left(product[:, wide + 2 * WIDE :])


def fold_rest(core_ref, *refs):
    raw, scratch = refs[:5], refs[-6:]
    outs = refs[5:-6]
    for e in range(len(outs) // 3 - 1, -1, -1):
        one = functools.partial(fold_element, e, raw, outs[3 * e : 3 * e + 3], *scratch)
        if e:
            one()
        else:
            pl.when(core_ref[0] == 1)(one)


def chip_blocks(faces_ref, fc_ref, fsn_ref, fu_ref, resp_ref, step_ref, const_ref, high_ref, low_ref, held):
    elements, half = faces_ref.shape[1], fc_ref.shape[2]
    count = CORES * elements
    for e in range(count):
        source = faces_ref.at[e // elements, e % elements]
        fc_ref[e] = source[:, :half]
        fsn_ref[e] = left(source[:, half : half + 2 * WIDE])
        own = source[:, half + 2 * WIDE :]
        fu_ref[e] = left(own)
        held[...] = -stacked(fu_ref[e], right(held[:WIDE, :])) if e else -own
        resp_ref[e] = left(held[...])
    step_ref[...] = held[:WIDE, :]
    high_ref[WIDE:, elements * 2 * WIDE :] = jnp.zeros_like(high_ref[WIDE:, elements * 2 * WIDE :])
    low_ref[WIDE:, elements * 2 * WIDE :] = jnp.zeros_like(low_ref[WIDE:, elements * 2 * WIDE :])
    for rows, last in ((slice(0, WIDE), count - 1), (slice(WIDE, 2 * WIDE), elements - 1)):
        passed = None
        for e in range(last, -1, -1):
            source = faces_ref.at[e // elements, e % elements]
            block = source[:WIDE, :]
            value = block if passed is None else stacked(left(passed), right(block))
            const = value[:, :half] if passed is None else const + value[:, :half]
            at = slice(e * 2 * WIDE, (e + 1) * 2 * WIDE)
            high_ref[rows, at], low_ref[rows, at] = split(value[:, half : half + 2 * WIDE])
            passed = -value[:, half + 2 * WIDE :]
        const_ref[rows, :] = const


def south_north(core_ref, k):
    return pl.multiple_of(((1 - core_ref[2]) if k == 0 else core_ref[2]) * WIDE, WIDE)


def traces(const, high, low, halo_high, halo_low):
    dot = functools.partial(jnp.dot, preferred_element_type=jnp.float32)
    return const - (dot(high, halo_high) + (dot(high, halo_low) + dot(low, halo_high)))


def first_traces(core_ref, const_ref, high_ref, low_ref, *refs):
    halos, raw, (out_ref, halo_high, halo_low), outs = refs[:4], refs[4:9], refs[9:12], refs[12:15]
    held, sems, scratch = refs[15], refs[16], refs[17:]
    elements = held.shape[1]
    copies = load_rows([(halo.at[:, :, 0, :], held.at[k]) for k, halo in enumerate(halos)], sems)
    for k, kind in enumerate(ORDER):
        copies[k].wait()
        owner = core_ref[0] if kind < 2 else 1 - core_ref[0]
        for e in range(elements):
            row = 2 * WIDE * (owner * elements + e) + south_north(core_ref, kind % 2)
            at = pl.ds(pl.multiple_of(row, WIDE), WIDE)
            halo_high[at, :], halo_low[at, :] = split(padded(held[k, e], WIDE))
    out_ref[...] = traces(
        const_ref[:WIDE, :], high_ref[:WIDE, :], low_ref[:WIDE, :], halo_high[...], halo_low[...]
    )
    pl.when(core_ref[0] == 0)(functools.partial(fold_element, 0, raw, outs, *scratch))


def other_faces(fc_ref, fsn_ref, fu_ref, halo_high, halo_low, faces_ref):
    trace = None
    for e in range(fc_ref.shape[0]):
        at = slice(2 * e * WIDE, 2 * (e + 1) * WIDE)
        high = halo_high[at, :]
        faces = fc_ref[e] - stacked(fsn_ref[e], jnp.concatenate([high, halo_low[at, :], high], axis=0))
        if e:
            faces = faces - stacked(fu_ref[e], right(trace))
        trace = faces[:WIDE]
        faces_ref[e] = faces[WIDE:]


def last_traces(core_ref, const_ref, high_ref, low_ref, second_ref, first_ref, out_ref, lead_ref, away_ref,
                halo_high, halo_low):
    count = first_ref.shape[0]
    elements = count // CORES
    for e in range(count):
        for k, ref in enumerate((first_ref, second_ref)):
            at = pl.ds(pl.multiple_of(south_north(core_ref, k) + 2 * e * WIDE, WIDE), WIDE)
            halo_high[at, :], halo_low[at, :] = split(ref[e])
    both = traces(const_ref[...], high_ref[...], low_ref[...], halo_high[...], halo_low[...])
    out_ref[...] = both[:WIDE]
    lead_ref[...] = both[WIDE:]
    other = (1 - core_ref[0]) * elements
    for e in range(elements):
        away_ref[0, e] = first_ref[other + e]
        away_ref[1, e] = second_ref[other + e]


def through_chips(core_ref, inflow_ref, chips, steps):
    inflow_ref[...] = jnp.zeros_like(inflow_ref)
    for back in range(len(chips), 0, -1):

        @pl.when(core_ref[1] >= back)
        def _():
            if back == len(chips):
                inflow_ref[...] = chips[back - 1][...]
            else:
                passed = stacked(left(steps[back - 1][...]), right(inflow_ref[...]))
                inflow_ref[...] = chips[back - 1][...] + passed


def next_faces(core_ref, faces_ref, resp_ref, *refs):
    first_ref, second_ref, inflow_ref, both = refs[-4:]
    count = (len(refs) - 3) // 2
    through_chips(core_ref, inflow_ref, refs[:count], refs[count:-4])
    inflow = right(inflow_ref[...])
    first = pl.multiple_of(core_ref[2] * WIDE, WIDE)
    second = pl.multiple_of((1 - core_ref[2]) * WIDE, WIDE)
    for e in range(faces_ref.shape[0]):
        both[e] = faces_ref[e] + stacked(resp_ref[e, WIDE:, :], inflow)
    for e in range(faces_ref.shape[0]):
        first_ref[e] = both[e, pl.ds(first, WIDE), :]
        second_ref[e] = both[e, pl.ds(second, WIDE), :]


def inflow_of_cores(core_ref, lead_ref, resp_ref, *refs):
    keep_ref, send_ref = refs[-2:]
    count = (len(refs) - 1) // 2
    through_chips(core_ref, keep_ref, refs[:count], refs[count:-2])
    last = resp_ref.shape[0] // CORES - 1

    @pl.when(core_ref[0] == 0)
    def _():
        send_ref[...] = lead_ref[...] + stacked(resp_ref[last, :WIDE, :], right(keep_ref[...]))

    @pl.when(core_ref[0] == 1)
    def _():
        send_ref[...] = keep_ref[...]
        keep_ref[...] = lead_ref[...] + stacked(resp_ref[last, :WIDE, :], right(send_ref[...]))


def join(core_ref, keep_ref, got_ref, inflow_ref):
    half = keep_ref.shape[1]

    @pl.when(core_ref[0] == 0)
    def _():
        inflow_ref[:, :half] = keep_ref[...]
        inflow_ref[:, half:] = got_ref[...]

    @pl.when(core_ref[0] == 1)
    def _():
        inflow_ref[:, :half] = got_ref[...]
        inflow_ref[:, half:] = keep_ref[...]


def field_without_inflow(other, core_ref, *refs):
    first_ref, second_ref, p_ref, halo = refs[-4:]
    elements, half = p_ref.shape[0], p_ref.shape[2]
    c_refs, bsn_refs = refs[: elements + 1], refs[elements + 1 : 2 * elements + 2]
    own = 0 if other else core_ref[0] * elements
    at = pl.ds(pl.multiple_of((1 - core_ref[0] if other else core_ref[0]) * half, half), half)
    for e in range(elements):
        for k, ref in enumerate((first_ref, second_ref)):
            halo[pl.ds(south_north(core_ref, k), WIDE), :] = ref[own + e]
        halos = right(halo[...])

        def place(c_ref, bsn_ref):
            p_ref[e] = c_ref[:, at] - stacked(bsn_ref[...], halos)

        by_core(core_ref, e, place, c_refs, bsn_refs)


def by_core(core_ref, e, use, *stacks):
    if e:
        use(*[refs[e + 1] for refs in stacks])
    else:
        for k in range(CORES):
            pl.when(core_ref[0] == k)(functools.partial(use, *[refs[k] for refs in stacks]))


def whole_field(core_ref, own_ref, other_ref, keep_ref, got_ref, *refs):
    bu_refs, (out_ref, inflow_ref, held, sems) = refs[:-4], refs[-4:]
    join(core_ref, keep_ref, got_ref, inflow_ref)
    elements, unknowns = held.shape[:2]
    half = keep_ref.shape[1]
    copies = []
    for e in range(elements):
        if e:
            at = 0
            for first, length in face_runs("down"):
                inflow_ref[at : at + length, :] = held[e - 1, first : first + length, :]
                at += length
        inflow = right(inflow_ref[...])

        def place(own, bu_ref):
            change = stacked(bu_ref[...], inflow)[:unknowns]
            for k in range(CORES):
                part = own_ref if k == own else other_ref
                at = slice(k * half, (k + 1) * half)
                held[e, :, at] = part[e, :unknowns, :] - change[:, at]

        for k in range(CORES):
            pl.when(core_ref[0] == k)(functools.partial(place, k, bu_refs[e + 1 if e else k]))
        copy = pltpu.make_async_copy(held.at[e], out_ref.at[e, :, 0, :], sems.at[e])
        copy.start()
        copies.append(copy)
    for copy in copies:
        copy.wait()


def ring(axis, by):
    count = lax.axis_size(axis)
    return [(i, (i + by) % count) for i in range(count)]


def per_device(right_side, start_field, block_inverse, upwind_block, south_block, north_block):
    by_row = lambda x: x.transpose(0, 2, 1, 3)
    rhs, start, inverse, upwind, south, north = map(
        by_row, (right_side, start_field, block_inverse, upwind_block, south_block, north_block)
    )
    elements, unknowns, _, columns = rhs.shape
    depth = -(-unknowns // 128) * 128
    half = columns // CORES
    count = CORES * elements
    devices, spans = lax.axis_size("sweep"), lax.axis_size("span")
    place = lax.axis_index("sweep")
    odd = lax.axis_index("span") % 2
    where = jnp.stack([place % CORES, place // CORES, odd]).astype(jnp.int32)
    dma = pltpu.SemaphoreType.DMA
    f32, bf16 = jnp.float32, jnp.bfloat16
    core = (SMEM, where)
    face = (elements, FACE, 1, half)

    def held(arrays):
        return [(VMEM, x) for x in arrays]

    def swap(x):
        return lax.ppermute(x, "sweep", [(i, i ^ 1) for i in range(devices)])

    def from_chips(x):
        return [
            lax.ppermute(x, "sweep", ring("sweep", CORES * back))
            for back in range(1, devices // CORES)
        ]

    def along_span(x, second, other_core):
        pairs = []
        for i in range(devices):
            for j in range(spans):
                by = 1 if (j + second) % 2 == 0 else -1
                pairs.append((i * spans + j, (i ^ other_core) * spans + (j + by) % spans))
        return lax.ppermute(x, ("sweep", "span"), pairs)

    runs = start.reshape(elements, NODE**2, VARS * NODE, 1, columns)
    found = call(
        start_faces,
        [(VMEM, (elements, NODE**2, NODE, 1, half), f32)] * 4,
        core, (HBM, runs),
        scratch=[dma((4,))],
    )
    halos = [along_span(found[k].reshape(face), k % 2, k // 2) for k in range(4)]
    raw = [(HBM, x) for x in (inverse, rhs, upwind, south, north)]
    raw_scratch = [
        VMEM((elements, unknowns, unknowns), f32),
        VMEM((elements, unknowns, columns), f32),
        VMEM((elements, 3, unknowns, FACE), f32),
    ]
    fold_scratch = [VMEM((3 * depth, columns + 3 * WIDE), bf16), dma((elements, 5))]
    (own,) = call(
        fold_faces,
        [(VMEM, (CORES, elements, 3 * WIDE, half + 3 * WIDE), f32)],
        *raw,
        scratch=raw_scratch + [VMEM((3 * WIDE, depth), f32)] + fold_scratch,
        us=0,
        limit=MOST,
        after=found,
    )
    cores = lax.all_to_all(
        own, "sweep", 0, 0, axis_index_groups=[[i, i + 1] for i in range(0, devices, CORES)]
    )
    fc, fsn, fu, resp, step, *trace_blocks = call(
        chip_blocks,
        [
            (VMEM, (count, 3 * WIDE, half), f32),
            (VMEM, (count, 3 * WIDE, 6 * WIDE), bf16),
            (VMEM, (count, 3 * WIDE, 3 * WIDE), bf16),
            (VMEM, (count, 3 * WIDE, 3 * WIDE), bf16),
            (VMEM, (WIDE, WIDE), f32),
            (VMEM, (2 * WIDE, half), f32),
        ]
        + [(VMEM, (2 * WIDE, 2 * count * WIDE), bf16)] * 2,
        (VMEM, cores),
        scratch=[VMEM((3 * WIDE, WIDE), f32)],
        us=0,
    )
    steps = from_chips(step)[:-1]
    halo_split = (2 * count * WIDE, half)
    folded = [
        (VMEM, (depth, columns), f32),
        (VMEM, (depth, 6 * WIDE), bf16),
        (VMEM, (depth, 3 * WIDE), bf16),
    ]
    one_scratch = [VMEM((1,) + x.shape[1:], f32) for x in raw_scratch]
    one_scratch += [VMEM((depth, depth), f32), VMEM((3 * depth, columns + 3 * WIDE), bf16), dma((5,))]
    out, *halo_parts = call(
        first_traces,
        [(VMEM, (WIDE, half), f32)] + [(VMEM, halo_split, bf16)] * 2 + folded,
        core, *held(trace_blocks), *[(HBM, halos[k]) for k in ORDER], *raw,
        scratch=[VMEM((4, elements, FACE, half), f32), dma((4,))] + one_scratch,
        us=2,
    )
    halo_parts, early = halo_parts[:2], halo_parts[2:]
    chips = from_chips(out)
    (faces,) = call(
        other_faces,
        [(VMEM, (count, 2 * WIDE, half), f32)],
        *held((fc, fsn, fu, *halo_parts)),
        us=2,
        after=steps,
    )
    last = call(
        next_faces,
        [(VMEM, (count, WIDE, half), f32)] * 2,
        core, *held((faces, resp, *chips, *steps)),
        scratch=[VMEM((WIDE, half), f32), VMEM((count, 2 * WIDE, half), f32)],
        us=1,
    )
    halos = [along_span(last[k], k, 0) for k in (1, 0)][::-1]
    late = call(
        fold_rest,
        folded * elements,
        core, *raw,
        scratch=one_scratch,
        us=10,
        after=last,
    )
    c, bsn, bu = [held([early[k], *late[k::3]]) for k in range(3)]
    out, lead, away = call(
        last_traces,
        [
            (VMEM, (WIDE, half), f32),
            (VMEM, (WIDE, half), f32),
            (VMEM, (2, elements, WIDE, half), f32),
        ],
        core, *held((*trace_blocks, *halos[::-1])),
        scratch=[VMEM(halo_split, bf16)] * 2,
        us=1,
        after=late[:1],
    )
    chips = from_chips(out)
    got = swap(away)
    parts = [
        call(
            functools.partial(field_without_inflow, other),
            [(VMEM, (elements, depth, half), f32)],
            core, *c, *bsn, *held(source),
            scratch=[VMEM((2 * WIDE, half), f32)],
            us=0 if other == 0 else 0,
            after=[out],
        )[0]
        for other, source in enumerate((halos, (got[0], got[1])))
    ]
    keep, send = call(
        inflow_of_cores,
        [(VMEM, (WIDE, half), f32)] * 2,
        core, *held((lead, resp, *chips, *steps)),
        us=20,
    )
    (field,) = call(
        whole_field,
        [(HBM, rhs.shape, f32)],
        core, *held((*parts, keep, swap(send))), *bu,
        scratch=[
            VMEM((WIDE, columns), f32),
            VMEM((elements, unknowns, columns), f32),
            dma((elements,)),
        ],
        us=1,
    )
    return by_row(field)


def solution(mesh):
    spec = P("sweep", "span", None, None)
    return jax.shard_map(
        per_device, mesh=mesh, in_specs=(spec,) * 6, out_specs=spec, check_vma=False
    )
```

time: 86.8 us -> 82.9 us (0.955)
  waiting for transfers between devices: 21.4 us -> 10.3 us
  starting transfers between devices: 21.1 us -> 27.1 us
  Pallas kernels: 32.8 us -> 34.5 us
    ppermute x8, waiting for transfers between devices: 9.53 us -> 1.35 us  [from_chips(): lax.ppermute(x, 'sweep', ring('sweep', CORES * back))]
    ppermute x8, starting transfers between devices: 8.5 us -> 11.1 us  [from_chips(): lax.ppermute(x, 'sweep', ring('sweep', CORES * back))]
    ppermute x6, starting transfers between devices: 7.72 us -> 9.95 us  [along_span(): return lax.ppermute(x, ('sweep', 'span'), pairs)]
    ppermute x6, waiting for transfers between devices: 10.9 us -> 8.97 us  [along_span(): return lax.ppermute(x, ('sweep', 'span'), pairs)]
    pallas_call x11 -> x12, Pallas kernels: 32.8 us -> 34.5 us  [call(): pl.pallas_call(body, out_shape=[jax.ShapeDtypeStruct(shape, kind) for _,...]
    ppermute x2, starting transfers between devices: 4.86 us -> 6.07 us  [swap(): return lax.ppermute(x, 'sweep', [(i, i ^ 1) for i in range(devices)])]
    ppermute x2, waiting for transfers between devices: 0.99 us -> 0.01 us  [swap(): return lax.ppermute(x, 'sweep', [(i, i ^ 1) for i in range(devices)])]
  transfers between devices with their start and end apart: 16 -> 16, of which waited for: 8 -> 4; matrix products, arithmetic and copies ran while one was open for 0% -> 0% of each run, Pallas kernels for 30% -> 34%
where the time goes in v4:
time: 82.9 us; the launch traced here: 82.7 us
  Pallas kernels  34.5 us (42%)
  starting transfers between devices  27.1 us (33%)
  waiting for transfers between devices  10.3 us (12%)
  blocking collectives  8.47 us (10%)
  local copies, waits for them, and re-layouts  1.8 us (2%)
    pallas_call x12, Pallas kernels, call(): pl.pallas_call(body, out_shape=[jax.ShapeDtypeStruct(shape, kind) for _,...  34.5 us
    ppermute x8, starting transfers between devices, from_chips(): lax.ppermute(x, 'sweep', ring('sweep', CORES * back))  11.1 us
    ppermute x6, starting transfers between devices, along_span(): return lax.ppermute(x, ('sweep', 'span'), pairs)  9.95 us
    ppermute x6, waiting for transfers between devices, along_span(): return lax.ppermute(x, ('sweep', 'span'), pairs)  8.97 us
    all_to_all x1, blocking collectives, per_device(): lax.all_to_all(own, 'sweep', 0, 0, axis_index_groups=[[i, i + 1] for i in...  8.47 us
    ppermute x2, starting transfers between devices, swap(): return lax.ppermute(x, 'sweep', [(i, i ^ 1) for i in range(devices)])  6.07 us
    unnamed x20, local copies, waits for them, and re-layouts  1.77 us
  transfers between devices with their start and end apart: 16, of which 4 were waited for; matrix products, arithmetic and copies ran while one was open for 0% of the time, Pallas kernels for 34%

profile of v4, /device:TPU:1, one launch (start us, length us, event | category | flops | bytes accessed | tf_op | source)
XLA Modules:
  0.0 82.7 jit_solution(4289038083018551339)
XLA Ops:
  0.0 0.1 pad_add_fusion.refs_0_
  0.1 0.0 copy-start.9
  0.1 1.7 %copy-done.9 = f32[2,1,625,512]{3,1,2,0:T(1,128)S(1)} copy-done((f32[2,1,625,512]{3,1,2,0:T(1,128)S(1)}, f32[2,1,625,512]{3,1,2,0:T(1,128)}, u32[]{:S(2)}) %copy-start.9) | copy-done | bytes 2560024
  1.8 1.0 %start_faces.1 = (f32[2,25,5,1,256]{4,3,2,1,0:T(1,128)S(1)}, f32[2,25,5,1,256]{4,3,2,1,0:T(1,128)S(1)}, f32[2,25,5,1,256]{4,3,2,1,0:T(1,128)S(1)}, f32[2,25,5,1,256]{4,3,2,1,0:T(1,128)S(1)}) custom-call(s32[3]{0:T(128)S(1)} %pad_add_fusion.refs_0_, f32[2,25,25,1,512]{4,3,2,1,0:T(1,128)S(1)} %bitcast.37), custom_call_target="tpu_custom_call" | custom-call | flops 1000000000 | tf_op jit(solution)/shard_map/start_faces/pallas_call | solution.py:67
  2.8 0.0 copy-start.5
  2.8 0.0 copy-start.6
  2.8 0.0 copy-start.7
  2.8 0.0 copy-start.8
  2.8 4.8 %collective-permute-start = (f32[2,125,1,256]{3,2,1,0:T(1,128)S(1)}, f32[2,125,1,256]{3,2,1,0:T(1,128)S(1)}, u32[]{:S(2)}, u32[]{:S(2)}) collective-permute-start(f32[2,125,1,256]{3,2,1,0:T(1,128)S(1)} %bitcast.36), channel_id=1, source_target_pairs={{0,7},{1,6},{2,5},{3,4},{4,3},{5,2},{6,1},{7,0},{8,15},{9,14},{10,... | collective-permute-start | bytes 768008 | tf_op jit(solution)/shard_map/ppermute | solution.py:431
  7.6 0.0 collective-permute-start.1
  7.6 0.0 collective-permute-start.2
  7.6 1.8 %collective-permute-start.3 = (f32[2,125,1,256]{3,2,1,0:T(1,128)S(1)}, f32[2,125,1,256]{3,2,1,0:T(1,128)S(1)}, u32[]{:S(2)}, u32[]{:S(2)}) collective-permute-start(f32[2,125,1,256]{3,2,1,0:T(1,128)S(1)} %bitcast.33), channel_id=1, source_target_pairs={{0,1},{1,0},{2,3},{3,2},{4,5},{5,4},{6,7},{7,6},{8,9},{9,8},{10,11... | collective-permute-start | bytes 768008 | tf_op jit(solution)/shard_map/ppermute | solution.py:431
  9.4 0.0 copy-done.5
  9.4 0.0 copy-done.6
  9.4 0.0 copy-done.7
  9.4 0.0 copy-done.8
  9.4 7.9 %fold_faces.1 = f32[2,2,384,640]{3,2,1,0:T(8,128)} custom-call(f32[2,625,1,625]{3,2,1,0:T(1,128)} %bitcast.18, f32[2,625,1,512]{3,2,1,0:T(1,128)} %bitcast.21, f32[2,625,1,125]{3,2,1,0:T(1,128)} %bitcast.24, f32[2,625,1,125]{3,2,1,0:T(1,128)} %bitcast.27, f32[2,625,1,125]{3,2,1,0:T(1,128)} %bitcast.30, f32[2,25,5,1,256]{4,3,2,1,0:T(1,128)} %copy-done.5, ...), custom_call_target="tpu_custom_call" | custom-call | tf_op jit(solution)/shard_map/fold_faces/pallas_call | solution.py:67
  17.4 0.0 copy-start.1
  17.4 0.0 copy-start.3
  17.4 0.0 copy-start.4
  17.4 8.5 %all_to_all.5.refs_0_ = f32[2,2,384,640]{3,2,1,0:T(8,128)S(1)} all-to-all(f32[2,2,384,640]{3,2,1,0:T(8,128)} %fold_faces.1), channel_id=1, replica_groups={{0,4},{8,12},{16,20},{24,28},{1,5},{9,13},{17,21},{25,29},{2,6},{10,14}..., dimensions={0} | all-to-all | bytes 7864320 | tf_op jit(solution)/shard_map/all_to_all | solution.py:457
  25.9 1.7 %chip_blocks.1 = (f32[4,384,256]{2,1,0:T(8,128)S(1)}, bf16[4,384,768]{2,1,0:T(8,128)(2,1)S(1)}, bf16[4,384,384]{2,1,0:T(8,128)(2,1)S(1)}, bf16[4,384,384]{2,1,0:...) custom-call(f32[2,2,384,640]{3,2,1,0:T(8,128)S(1)} %all_to_all.5.refs_0_), custom_call_target="tpu_custom_call" | custom-call | tf_op jit(solution)/shard_map/chip_blocks/pallas_call | solution.py:67
  27.6 1.3 %collective-permute-start.4 = (f32[128,128]{1,0:T(8,128)S(1)}, f32[128,128]{1,0:T(8,128)S(1)}, u32[]{:S(2)}, u32[]{:S(2)}) collective-permute-start(f32[128,128]{1,0:T(8,128)S(1)} %get-tuple-element.49), channel_id=1, source_target_pairs={{0,8},{4,12},{8,16},{12,20},{16,24},{20,28},{24,0},{28,4},{1,9},{5... | collective-permute-start | bytes 196616 | tf_op jit(solution)/shard_map/ppermute | solution.py:421
  28.8 0.0 collective-permute-done.refs_4_
  28.8 1.3 %collective-permute-start.5 = (f32[128,128]{1,0:T(8,128)S(1)}, f32[128,128]{1,0:T(8,128)S(1)}, u32[]{:S(2)}, u32[]{:S(2)}) collective-permute-start(f32[128,128]{1,0:T(8,128)S(1)} %get-tuple-element.49), channel_id=1, source_target_pairs={{0,16},{4,20},{8,24},{12,28},{16,0},{20,4},{24,8},{28,12},{1,17},{... | collective-permute-start | bytes 196616 | tf_op jit(solution)/shard_map/ppermute | solution.py:421
  30.1 0.0 collective-permute-done.1.refs_5_
  30.1 0.0 collective-permute-done.2.refs_6_
  30.1 0.2 collective-permute-done.3.refs_7_
  30.3 0.0 copy-done.1
  30.3 0.0 copy-done.3
  30.3 0.0 copy-done.4
  30.3 0.0 copy-done
  30.3 0.0 copy-done.2
  30.3 2.0 %first_traces.1 = (f32[128,256]{1,0:T(8,128)S(1)}, bf16[1024,256]{1,0:T(8,128)(2,1)S(1)}, bf16[1024,256]{1,0:T(8,128)(2,1)S(1)}, f32[640,512]{1,0:T(8,128)S(1)},...) custom-call(s32[3]{0:T(128)S(1)} %pad_add_fusion.refs_0_, f32[256,256]{1,0:T(8,128)S(1)} %get-tuple-element.40.refs_1_, ...), custom_call_target="tpu_custom_call" | custom-call | flops 2000000000 | tf_op jit(solution)/shard_map/first_traces/pallas_call | solution.py:67
  32.3 1.8 %collective-permute-start.6 = (f32[128,256]{1,0:T(8,128)S(1)}, f32[128,256]{1,0:T(8,128)S(1)}, u32[]{:S(2)}, u32[]{:S(2)}) collective-permute-start(f32[128,256]{1,0:T(8,128)S(1)} %get-tuple-element.51), channel_id=1, source_target_pairs={{0,8},{4,12},{8,16},{12,20},{16,24},{20,28},{24,0},{28,4},{1,9},{5... | collective-permute-start | bytes 393224 | tf_op jit(solution)/shard_map/ppermute | solution.py:421
  34.1 1.2 %collective-permute-start.7 = (f32[128,256]{1,0:T(8,128)S(1)}, f32[128,256]{1,0:T(8,128)S(1)}, u32[]{:S(2)}, u32[]{:S(2)}) collective-permute-start(f32[128,256]{1,0:T(8,128)S(1)} %get-tuple-element.51), channel_id=1, source_target_pairs={{0,16},{4,20},{8,24},{12,28},{16,0},{20,4},{24,8},{28,12},{1,17},{... | collective-permute-start | bytes 393224 | tf_op jit(solution)/shard_map/ppermute | solution.py:421
  35.3 1.2 %collective-permute-start.8 = (f32[128,256]{1,0:T(8,128)S(1)}, f32[128,256]{1,0:T(8,128)S(1)}, u32[]{:S(2)}, u32[]{:S(2)}) collective-permute-start(f32[128,256]{1,0:T(8,128)S(1)} %get-tuple-element.51), channel_id=1, source_target_pairs={{0,24},{4,28},{8,0},{12,4},{16,8},{20,12},{24,16},{28,20},{1,25},{... | collective-permute-start | bytes 393224 | tf_op jit(solution)/shard_map/ppermute | solution.py:421
  36.5 0.0 collective-permute-done.4.refs_5_.refs_6_
  36.5 0.0 collective-permute-done.5.refs_6_.refs_7_
  36.5 1.3 %other_faces.1.refs_1_ = f32[4,256,256]{2,1,0:T(8,128)S(1)} custom-call(f32[4,384,256]{2,1,0:T(8,128)S(1)} %get-tuple-element.44.refs_0_, bf16[4,384,768]{2,1,0:T(8,128)(2,1)S(1)} %get-tuple-element.45.refs_1_, bf16[4,384,384]{2,1,0:T(8,128)(2,1)S(1)} %get-tuple-element.46.refs_2_, bf16[1024,256]{1,0:T(8,128)(2,1)S(1)} %get-tuple-element.47.refs_3_, ...), custom_call_target="tpu_custom_call" | custom-call | flops 2000000000 | tf_op jit(solution)/shard_map/other_faces/pallas_call | solution.py:67
  37.8 0.0 collective-permute-done.6.refs_3_
  37.8 1.0 %collective-permute-done.7.refs_4_ = f32[128,256]{1,0:T(8,128)S(1)} collective-permute-done((f32[128,256]{1,0:T(8,128)S(1)}, f32[128,256]{1,0:T(8,128)S(1)}, u32[]{:S(2)}, u32[]{:S(2)}) %collective-permute-start.7) | collective-permute-done | bytes 131104 | tf_op jit(solution)/shard_map/ppermute | solution.py:421
  38.8 0.3 collective-permute-done.8.refs_5_
  39.2 1.1 %next_faces.1 = (f32[4,128,256]{2,1,0:T(8,128)S(1)}, f32[4,128,256]{2,1,0:T(8,128)S(1)}) custom-call(s32[3]{0:T(128)S(1)} %pad_add_fusion.refs_0_, f32[4,256,256]{2,1,0:T(8,128)S(1)} %other_faces.1.refs_1_, bf16[4,384,384]{2,1,0:T(8,128)(2,1)S(1)} %get-tuple-element.50.refs_2_, f32[128,256]{1,0:T(8,128)S(1)} %collective-permute-done.6.refs_3_, ...), custom_call_target="tpu_custom_call" | custom-call | flops 1000000000 | tf_op jit(solution)/shard_map/next_faces/pallas_call | solution.py:67
  40.2 3.3 %collective-permute-start.10 = (f32[4,128,256]{2,1,0:T(8,128)S(1)}, f32[4,128,256]{2,1,0:T(8,128)S(1)}, u32[]{:S(2)}, u32[]{:S(2)}) collective-permute-start(f32[4,128,256]{2,1,0:T(8,128)S(1)} %get-tuple-element.53.refs_7_), channel_id=1, source_target_pairs={{0,3},{1,2},{2,1},{3,0},{4,7},{5,6},{6,5},{7,4},{8,11},{9,10},{10,... | collective-permute-start | bytes 1572872 | tf_op jit(solution)/shard_map/ppermute | solution.py:431
  43.6 0.0 collective-permute-start.9
  43.6 11.7 %fold_rest.1 = (f32[640,512]{1,0:T(8,128)S(1)}, bf16[640,768]{1,0:T(8,128)(2,1)S(1)}, bf16[640,384]{1,0:T(8,128)(2,1)S(1)}, f32[640,512]{1,0:T(8,128)S(1)}, bf16...) custom-call(s32[3]{0:T(128)S(1)} %pad_add_fusion.refs_0_, f32[2,625,1,625]{3,2,1,0:T(1,128)S(1)} %bitcast.20, ...), custom_call_target="tpu_custom_call" | custom-call | flops 10000000000 | tf_op jit(solution)/shard_map/fold_rest/pallas_call | solution.py:67
  55.3 0.0 collective-permute-done.10.refs_4_.refs_8_
  55.4 8.7 %collective-permute-done.9.refs_5_.refs_7_ = f32[4,128,256]{2,1,0:T(8,128)S(1)} collective-permute-done((f32[4,128,256]{2,1,0:T(8,128)S(1)}, f32[4,128,256]{2,1,0:T(8,128)S(1)}, u32[]{:S(2)}, u32[]{:S(2)}) %collective-permute-start.9) | collective-permute-done | bytes 524320 | tf_op jit(solution)/shard_map/ppermute | solution.py:431
  64.1 1.3 %last_traces.1 = (f32[128,256]{1,0:T(8,128)S(1)}, f32[128,256]{1,0:T(8,128)S(1)}, f32[2,2,128,256]{3,2,1,0:T(8,128)S(1)}) custom-call(s32[3]{0:T(128)S(1)} %pad_add_fusion.refs_0_, f32[256,256]{1,0:T(8,128)S(1)} %get-tuple-element.40.refs_1_, bf16[256,1024]{1,0:T(8,128)(2,1)S(1)} %get-tuple-element.41.refs_2_, ...), custom_call_target="tpu_custom_call" | custom-call | flops 1000000000 | tf_op jit(solution)/shard_map/last_traces/pallas_call | solution.py:67
  65.4 1.9 %collective-permute-start.12 = (f32[128,256]{1,0:T(8,128)S(1)}, f32[128,256]{1,0:T(8,128)S(1)}, u32[]{:S(2)}, u32[]{:S(2)}) collective-permute-start(f32[128,256]{1,0:T(8,128)S(1)} %get-tuple-element.59.refs_9_), channel_id=1, source_target_pairs={{0,8},{4,12},{8,16},{12,20},{16,24},{20,28},{24,0},{28,4},{1,9},{5... | collective-permute-start | bytes 393224 | tf_op jit(solution)/shard_map/ppermute | solution.py:421
  67.3 0.9 %collective-permute-start.13 = (f32[128,256]{1,0:T(8,128)S(1)}, f32[128,256]{1,0:T(8,128)S(1)}, u32[]{:S(2)}, u32[]{:S(2)}) collective-permute-start(f32[128,256]{1,0:T(8,128)S(1)} %get-tuple-element.59.refs_9_), channel_id=1, source_target_pairs={{0,16},{4,20},{8,24},{12,28},{16,0},{20,4},{24,8},{28,12},{1,17},{... | collective-permute-start | bytes 393224 | tf_op jit(solution)/shard_map/ppermute | solution.py:421
  68.1 1.7 %collective-permute-start.14 = (f32[128,256]{1,0:T(8,128)S(1)}, f32[128,256]{1,0:T(8,128)S(1)}, u32[]{:S(2)}, u32[]{:S(2)}) collective-permute-start(f32[128,256]{1,0:T(8,128)S(1)} %get-tuple-element.59.refs_9_), channel_id=1, source_target_pairs={{0,24},{4,28},{8,0},{12,4},{16,8},{20,12},{24,16},{28,20},{1,25},{... | collective-permute-start | bytes 393224 | tf_op jit(solution)/shard_map/ppermute | solution.py:421
  69.8 4.0 %collective-permute-start.11 = (f32[2,2,128,256]{3,2,1,0:T(8,128)S(1)}, f32[2,2,128,256]{3,2,1,0:T(8,128)S(1)}, u32[]{:S(2)}, u32[]{:S(2)}) collective-permute-start(f32[2,2,128,256]{3,2,1,0:T(8,128)S(1)} %get-tuple-element.60), channel_id=1, source_target_pairs={{0,4},{4,0},{8,12},{12,8},{16,20},{20,16},{24,28},{28,24},{1,5},{5... | collective-permute-start | bytes 1572872 | tf_op jit(solution)/shard_map/ppermute | solution.py:417
  73.8 1.5 %field_without_inflow.2.refs_1_ = f32[2,640,256]{2,1,0:T(8,128)S(1)} custom-call(s32[3]{0:T(128)S(1)} %pad_add_fusion.refs_0_, f32[640,512]{1,0:T(8,128)S(1)} %get-tuple-element.43.refs_1_, f32[640,512]{1,0:T(8,128)S(1)} %get-tuple-element.54.refs_6_.refs_2_, f32[640,512]{1,0:T(8,128)S(1)} %get-tuple-element.55.refs_3_, ...), custom_call_target="tpu_custom_call" | custom-call | tf_op jit(solution)/shard_map/field_without_inflow/pallas_call | solution.py:67
  75.3 0.0 collective-permute-done.12.refs_3_
  75.3 0.0 collective-permute-done.13.refs_4_
  75.3 0.0 collective-permute-done.14.refs_5_
  75.3 0.8 inflow_of_cores.1
  76.1 2.1 %collective-permute-start.15 = (f32[128,256]{1,0:T(8,128)S(1)}, f32[128,256]{1,0:T(8,128)S(1)}, u32[]{:S(2)}, u32[]{:S(2)}) collective-permute-start(f32[128,256]{1,0:T(8,128)S(1)} %get-tuple-element.63), channel_id=1, source_target_pairs={{0,4},{4,0},{8,12},{12,8},{16,20},{20,16},{24,28},{28,24},{1,5},{5... | collective-permute-start | bytes 393224 | tf_op jit(solution)/shard_map/ppermute | solution.py:417
  78.2 0.0 collective-permute-done.11
  78.2 1.5 %field_without_inflow.3.refs_2_ = f32[2,640,256]{2,1,0:T(8,128)S(1)} custom-call(s32[3]{0:T(128)S(1)} %pad_add_fusion.refs_0_, f32[640,512]{1,0:T(8,128)S(1)} %get-tuple-element.43.refs_1_, f32[640,512]{1,0:T(8,128)S(1)} %get-tuple-element.54.refs_6_.refs_2_, f32[640,512]{1,0:T(8,128)S(1)} %get-tuple-element.55.refs_3_, ...), custom_call_target="tpu_custom_call" | custom-call | tf_op jit(solution)/shard_map/field_without_inflow/pallas_call | solution.py:67
  79.8 0.0 collective-permute-done.15.refs_4_
  79.8 2.7 %whole_field.1 = f32[2,625,1,512]{3,2,1,0:T(1,128)} custom-call(s32[3]{0:T(128)S(1)} %pad_add_fusion.refs_0_, f32[2,640,256]{2,1,0:T(8,128)S(1)} %field_without_inflow.2.refs_1_, f32[2,640,256]{2,1,0:T(8,128)S(1)} %field_without_inflow.3.refs_2_, f32[128,256]{1,0:T(8,128)S(1)} %get-tuple-element.62.refs_3_, f32[128,256]{1,0:T(8,128)S(1)} %collective-permute-done.15.refs_4_, ...), custom_call_target="tpu_custom_call" | custom-call | flops 1000000000 | tf_op jit(solution)/shard_map/whole_field/pallas_call | solution.py:67
  (3 shorter events, 0.0 us)
Async XLA Ops:
  0.1 1.7 %copy-start.9 = (f32[2,1,625,512]{3,1,2,0:T(1,128)S(1)}, f32[2,1,625,512]{3,1,2,0:T(1,128)}, u32[]{:S(2)}) copy-start(f32[2,1,625,512]{3,1,2,0:T(1,128)} %param.7) | copy-start | bytes 7680004
  2.8 6.6 %copy-start.5 = (f32[2,25,5,1,256]{4,3,2,1,0:T(1,128)}, f32[2,25,5,1,256]{4,3,2,1,0:T(1,128)S(1)}, u32[]{:S(2)}) copy-start(f32[2,25,5,1,256]{4,3,2,1,0:T(1,128)S(1)} %get-tuple-element.36.refs_5_) | copy-start | bytes 768004
  2.8 6.6 %copy-start.6 = (f32[2,25,5,1,256]{4,3,2,1,0:T(1,128)}, f32[2,25,5,1,256]{4,3,2,1,0:T(1,128)S(1)}, u32[]{:S(2)}) copy-start(f32[2,25,5,1,256]{4,3,2,1,0:T(1,128)S(1)} %get-tuple-element.38.refs_7_) | copy-start | bytes 768004
  2.8 6.6 %copy-start.7 = (f32[2,25,5,1,256]{4,3,2,1,0:T(1,128)}, f32[2,25,5,1,256]{4,3,2,1,0:T(1,128)S(1)}, u32[]{:S(2)}) copy-start(f32[2,25,5,1,256]{4,3,2,1,0:T(1,128)S(1)} %get-tuple-element.37.refs_6_) | copy-start | bytes 768004
  2.8 6.6 %copy-start.8 = (f32[2,25,5,1,256]{4,3,2,1,0:T(1,128)}, f32[2,25,5,1,256]{4,3,2,1,0:T(1,128)S(1)}, u32[]{:S(2)}) copy-start(f32[2,25,5,1,256]{4,3,2,1,0:T(1,128)S(1)} %get-tuple-element.39.refs_8_) | copy-start | bytes 768004
  2.8 26.0 %collective-permute-start = (f32[2,125,1,256]{3,2,1,0:T(1,128)S(1)}, f32[2,125,1,256]{3,2,1,0:T(1,128)S(1)}, u32[]{:S(2)}, u32[]{:S(2)}) collective-permute-start(f32[2,125,1,256]{3,2,1,0:T(1,128)S(1)} %bitcast.36), channel_id=1, source_target_pairs={{0,7},{1,6},{2,5},{3,4},{4,3},{5,2},{6,1},{7,0},{8,15},{9,14},{10,... | collective-permute-start | bytes 768008 | tf_op jit(solution)/shard_map/ppermute | solution.py:431
  7.6 22.5 %collective-permute-start.1 = (f32[2,125,1,256]{3,2,1,0:T(1,128)S(1)}, f32[2,125,1,256]{3,2,1,0:T(1,128)S(1)}, u32[]{:S(2)}, u32[]{:S(2)}) collective-permute-start(f32[2,125,1,256]{3,2,1,0:T(1,128)S(1)} %bitcast.35), channel_id=1, source_target_pairs={{0,3},{1,2},{2,1},{3,0},{4,7},{5,6},{6,5},{7,4},{8,11},{9,10},{10,... | collective-permute-start | bytes 768008 | tf_op jit(solution)/shard_map/ppermute | solution.py:431
  7.6 22.5 %collective-permute-start.2 = (f32[2,125,1,256]{3,2,1,0:T(1,128)S(1)}, f32[2,125,1,256]{3,2,1,0:T(1,128)S(1)}, u32[]{:S(2)}, u32[]{:S(2)}) collective-permute-start(f32[2,125,1,256]{3,2,1,0:T(1,128)S(1)} %bitcast.34), channel_id=1, source_target_pairs={{0,5},{1,4},{2,7},{3,6},{4,1},{5,0},{6,3},{7,2},{8,13},{9,12},{10,... | collective-permute-start | bytes 768008 | tf_op jit(solution)/shard_map/ppermute | solution.py:431
  7.6 22.7 %collective-permute-start.3 = (f32[2,125,1,256]{3,2,1,0:T(1,128)S(1)}, f32[2,125,1,256]{3,2,1,0:T(1,128)S(1)}, u32[]{:S(2)}, u32[]{:S(2)}) collective-permute-start(f32[2,125,1,256]{3,2,1,0:T(1,128)S(1)} %bitcast.33), channel_id=1, source_target_pairs={{0,1},{1,0},{2,3},{3,2},{4,5},{5,4},{6,7},{7,6},{8,9},{9,8},{10,11... | collective-permute-start | bytes 768008 | tf_op jit(solution)/shard_map/ppermute | solution.py:431
  17.4 12.9 %copy-start.1 = (f32[2,1,625,512]{3,1,2,0:T(1,128)S(1)}, f32[2,1,625,512]{3,1,2,0:T(1,128)}, u32[]{:S(2)}) copy-start(f32[2,1,625,512]{3,1,2,0:T(1,128)} %param.6) | copy-start | bytes 7680004
  17.4 12.9 %copy-start.3 = (f32[2,1,625,125]{3,1,2,0:T(1,128)S(1)}, f32[2,1,625,125]{3,1,2,0:T(1,128)}, u32[]{:S(2)}) copy-start(f32[2,1,625,125]{3,1,2,0:T(1,128)} %param.10) | copy-start | bytes 1875004
  17.4 12.9 %copy-start.4 = (f32[2,1,625,125]{3,1,2,0:T(1,128)S(1)}, f32[2,1,625,125]{3,1,2,0:T(1,128)}, u32[]{:S(2)}) copy-start(f32[2,1,625,125]{3,1,2,0:T(1,128)} %param.11) | copy-start | bytes 1875004
  25.9 4.4 %copy-start = (f32[2,1,625,625]{3,1,2,0:T(1,128)S(1)}, f32[2,1,625,625]{3,1,2,0:T(1,128)}, u32[]{:S(2)}) copy-start(f32[2,1,625,625]{3,1,2,0:T(1,128)} %param.8) | copy-start | bytes 9375004
  25.9 4.4 %copy-start.2 = (f32[2,1,625,125]{3,1,2,0:T(1,128)S(1)}, f32[2,1,625,125]{3,1,2,0:T(1,128)}, u32[]{:S(2)}) copy-start(f32[2,1,625,125]{3,1,2,0:T(1,128)} %param.9) | copy-start | bytes 1875004
  27.6 8.9 %collective-permute-start.4 = (f32[128,128]{1,0:T(8,128)S(1)}, f32[128,128]{1,0:T(8,128)S(1)}, u32[]{:S(2)}, u32[]{:S(2)}) collective-permute-start(f32[128,128]{1,0:T(8,128)S(1)} %get-tuple-element.49), channel_id=1, source_target_pairs={{0,8},{4,12},{8,16},{12,20},{16,24},{20,28},{24,0},{28,4},{1,9},{5... | collective-permute-start | bytes 196616 | tf_op jit(solution)/shard_map/ppermute | solution.py:421
  28.8 7.7 %collective-permute-start.5 = (f32[128,128]{1,0:T(8,128)S(1)}, f32[128,128]{1,0:T(8,128)S(1)}, u32[]{:S(2)}, u32[]{:S(2)}) collective-permute-start(f32[128,128]{1,0:T(8,128)S(1)} %get-tuple-element.49), channel_id=1, source_target_pairs={{0,16},{4,20},{8,24},{12,28},{16,0},{20,4},{24,8},{28,12},{1,17},{... | collective-permute-start | bytes 196616 | tf_op jit(solution)/shard_map/ppermute | solution.py:421
  32.3 5.5 %collective-permute-start.6 = (f32[128,256]{1,0:T(8,128)S(1)}, f32[128,256]{1,0:T(8,128)S(1)}, u32[]{:S(2)}, u32[]{:S(2)}) collective-permute-start(f32[128,256]{1,0:T(8,128)S(1)} %get-tuple-element.51), channel_id=1, source_target_pairs={{0,8},{4,12},{8,16},{12,20},{16,24},{20,28},{24,0},{28,4},{1,9},{5... | collective-permute-start | bytes 393224 | tf_op jit(solution)/shard_map/ppermute | solution.py:421
  34.1 4.7 %collective-permute-start.7 = (f32[128,256]{1,0:T(8,128)S(1)}, f32[128,256]{1,0:T(8,128)S(1)}, u32[]{:S(2)}, u32[]{:S(2)}) collective-permute-start(f32[128,256]{1,0:T(8,128)S(1)} %get-tuple-element.51), channel_id=1, source_target_pairs={{0,16},{4,20},{8,24},{12,28},{16,0},{20,4},{24,8},{28,12},{1,17},{... | collective-permute-start | bytes 393224 | tf_op jit(solution)/shard_map/ppermute | solution.py:421
  35.3 3.8 %collective-permute-start.8 = (f32[128,256]{1,0:T(8,128)S(1)}, f32[128,256]{1,0:T(8,128)S(1)}, u32[]{:S(2)}, u32[]{:S(2)}) collective-permute-start(f32[128,256]{1,0:T(8,128)S(1)} %get-tuple-element.51), channel_id=1, source_target_pairs={{0,24},{4,28},{8,0},{12,4},{16,8},{20,12},{24,16},{28,20},{1,25},{... | collective-permute-start | bytes 393224 | tf_op jit(solution)/shard_map/ppermute | solution.py:421
  40.2 15.1 %collective-permute-start.10 = (f32[4,128,256]{2,1,0:T(8,128)S(1)}, f32[4,128,256]{2,1,0:T(8,128)S(1)}, u32[]{:S(2)}, u32[]{:S(2)}) collective-permute-start(f32[4,128,256]{2,1,0:T(8,128)S(1)} %get-tuple-element.53.refs_7_), channel_id=1, source_target_pairs={{0,3},{1,2},{2,1},{3,0},{4,7},{5,6},{6,5},{7,4},{8,11},{9,10},{10,... | collective-permute-start | bytes 1572872 | tf_op jit(solution)/shard_map/ppermute | solution.py:431
  43.6 20.5 %collective-permute-start.9 = (f32[4,128,256]{2,1,0:T(8,128)S(1)}, f32[4,128,256]{2,1,0:T(8,128)S(1)}, u32[]{:S(2)}, u32[]{:S(2)}) collective-permute-start(f32[4,128,256]{2,1,0:T(8,128)S(1)} %get-tuple-element.52.refs_6_), channel_id=1, source_target_pairs={{0,1},{1,0},{2,3},{3,2},{4,5},{5,4},{6,7},{7,6},{8,9},{9,8},{10,11... | collective-permute-start | bytes 1572872 | tf_op jit(solution)/shard_map/ppermute | solution.py:431
  65.4 9.9 %collective-permute-start.12 = (f32[128,256]{1,0:T(8,128)S(1)}, f32[128,256]{1,0:T(8,128)S(1)}, u32[]{:S(2)}, u32[]{:S(2)}) collective-permute-start(f32[128,256]{1,0:T(8,128)S(1)} %get-tuple-element.59.refs_9_), channel_id=1, source_target_pairs={{0,8},{4,12},{8,16},{12,20},{16,24},{20,28},{24,0},{28,4},{1,9},{5... | collective-permute-start | bytes 393224 | tf_op jit(solution)/shard_map/ppermute | solution.py:421
  67.3 8.0 %collective-permute-start.13 = (f32[128,256]{1,0:T(8,128)S(1)}, f32[128,256]{1,0:T(8,128)S(1)}, u32[]{:S(2)}, u32[]{:S(2)}) collective-permute-start(f32[128,256]{1,0:T(8,128)S(1)} %get-tuple-element.59.refs_9_), channel_id=1, source_target_pairs={{0,16},{4,20},{8,24},{12,28},{16,0},{20,4},{24,8},{28,12},{1,17},{... | collective-permute-start | bytes 393224 | tf_op jit(solution)/shard_map/ppermute | solution.py:421
  68.1 7.2 %collective-permute-start.14 = (f32[128,256]{1,0:T(8,128)S(1)}, f32[128,256]{1,0:T(8,128)S(1)}, u32[]{:S(2)}, u32[]{:S(2)}) collective-permute-start(f32[128,256]{1,0:T(8,128)S(1)} %get-tuple-element.59.refs_9_), channel_id=1, source_target_pairs={{0,24},{4,28},{8,0},{12,4},{16,8},{20,12},{24,16},{28,20},{1,25},{... | collective-permute-start | bytes 393224 | tf_op jit(solution)/shard_map/ppermute | solution.py:421
  69.8 8.4 %collective-permute-start.11 = (f32[2,2,128,256]{3,2,1,0:T(8,128)S(1)}, f32[2,2,128,256]{3,2,1,0:T(8,128)S(1)}, u32[]{:S(2)}, u32[]{:S(2)}) collective-permute-start(f32[2,2,128,256]{3,2,1,0:T(8,128)S(1)} %get-tuple-element.60), channel_id=1, source_target_pairs={{0,4},{4,0},{8,12},{12,8},{16,20},{20,16},{24,28},{28,24},{1,5},{5... | collective-permute-start | bytes 1572872 | tf_op jit(solution)/shard_map/ppermute | solution.py:417
  76.1 3.6 %collective-permute-start.15 = (f32[128,256]{1,0:T(8,128)S(1)}, f32[128,256]{1,0:T(8,128)S(1)}, u32[]{:S(2)}, u32[]{:S(2)}) collective-permute-start(f32[128,256]{1,0:T(8,128)S(1)} %get-tuple-element.63), channel_id=1, source_target_pairs={{0,4},{4,0},{8,12},{12,8},{16,20},{20,16},{24,28},{28,24},{1,5},{5... | collective-permute-start | bytes 393224 | tf_op jit(solution)/shard_map/ppermute | solution.py:417

commit v5 on v4

--- a/solution.py
+++ b/solution.py
@@ -13,7 +13,8 @@
 WIDE = 128
 SWEEPS = 2
 CORES = 2
-ORDER = (3, 1, 2, 0)
+EARLY = (3, 1, 2)
+LATE = (0,)
 LIMIT = 24 * 1024 * 1024
 MOST = 60 * 1024 * 1024
 ANY = pl.ANY
@@ -228,18 +229,28 @@
     return const - (dot(high, halo_high) + (dot(high, halo_low) + dot(low, halo_high)))
 
 
-def first_traces(core_ref, const_ref, high_ref, low_ref, *refs):
-    halos, raw, (out_ref, halo_high, halo_low), outs = refs[:4], refs[4:9], refs[9:12], refs[12:15]
-    held, sems, scratch = refs[15], refs[16], refs[17:]
+def take_halos(kinds, core_ref, halos, halo_high, halo_low, held, sems):
     elements = held.shape[1]
     copies = load_rows([(halo.at[:, :, 0, :], held.at[k]) for k, halo in enumerate(halos)], sems)
-    for k, kind in enumerate(ORDER):
+    for k, kind in enumerate(kinds):
         copies[k].wait()
         owner = core_ref[0] if kind < 2 else 1 - core_ref[0]
         for e in range(elements):
             row = 2 * WIDE * (owner * elements + e) + south_north(core_ref, kind % 2)
             at = pl.ds(pl.multiple_of(row, WIDE), WIDE)
             halo_high[at, :], halo_low[at, :] = split(padded(held[k, e], WIDE))
+
+
+def early_halos(core_ref, *refs):
+    take_halos(EARLY, core_ref, refs[: len(EARLY)], *refs[len(EARLY) :])
+
+
+def first_traces(core_ref, const_ref, high_ref, low_ref, *refs):
+    count = len(LATE)
+    halos, raw, refs = refs[:count], refs[count : count + 5], refs[count + 7 :]
+    halo_high, halo_low, out_ref, *outs = refs[:6]
+    held, sems, *scratch = refs[6:]
+    take_halos(LATE, core_ref, halos, halo_high, halo_low, held, sems)
     out_ref[...] = traces(
         const_ref[:WIDE, :], high_ref[:WIDE, :], low_ref[:WIDE, :], halo_high[...], halo_low[...]
     )
@@ -481,14 +492,22 @@
     ]
     one_scratch = [VMEM((1,) + x.shape[1:], f32) for x in raw_scratch]
     one_scratch += [VMEM((depth, depth), f32), VMEM((3 * depth, columns + 3 * WIDE), bf16), dma((5,))]
-    out, *halo_parts = call(
+    halo_parts = call(
+        early_halos,
+        [(VMEM, halo_split, bf16)] * 2,
+        core, *[(HBM, halos[k]) for k in EARLY],
+        scratch=[VMEM((len(EARLY), elements, FACE, half), f32), dma((len(EARLY),))],
+        us=1,
+    )
+    folded_early = call(
         first_traces,
-        [(VMEM, (WIDE, half), f32)] + [(VMEM, halo_split, bf16)] * 2 + folded,
-        core, *held(trace_blocks), *[(HBM, halos[k]) for k in ORDER], *raw,
-        scratch=[VMEM((4, elements, FACE, half), f32), dma((4,))] + one_scratch,
+        [(VMEM, halo_split, bf16)] * 2 + [(VMEM, (WIDE, half), f32)] + folded,
+        core, *held(trace_blocks), *[(HBM, halos[k]) for k in LATE], *raw, *held(halo_parts),
+        scratch=[VMEM((len(LATE), elements, FACE, half), f32), dma((len(LATE),))] + one_scratch,
         us=2,
-    )
-    halo_parts, early = halo_parts[:2], halo_parts[2:]
+        aliases={9 + len(LATE): 0, 10 + len(LATE): 1},
+    )
+    halo_parts, out, early = folded_early[:2], folded_early[2], folded_early[3:]
     chips = from_chips(out)
     (faces,) = call(
         other_faces,

time: 82.9 us -> 82.3 us (level)
  starting transfers between devices: 27.1 us -> 25.9 us
    ppermute x8, starting transfers between devices: 11.1 us -> 9.89 us  [from_chips(): lax.ppermute(x, 'sweep', ring('sweep', CORES * back))]
    pallas_call x12 -> x13, Pallas kernels: 34.5 us -> 35 us  [call(): pl.pallas_call(body, out_shape=[jax.ShapeDtypeStruct(shape, kind) for _,...]
  transfers between devices with their start and end apart: 16 -> 16, of which waited for: 4 -> 3; matrix products, arithmetic and copies ran while one was open for 0% -> 0% of each run, Pallas kernels for 34% -> 35%
where the time goes in v5:
time: 82.3 us; the launch traced here: 82.1 us
  Pallas kernels  35 us (43%)
  starting transfers between devices  25.9 us (31%)
  waiting for transfers between devices  10.5 us (13%)
  blocking collectives  8.34 us (10%)
  local copies, waits for them, and re-layouts  1.8 us (2%)
    pallas_call x13, Pallas kernels, call(): pl.pallas_call(body, out_shape=[jax.ShapeDtypeStruct(shape, kind) for _,...  35 us
    ppermute x6, starting transfers between devices, along_span(): return lax.ppermute(x, ('sweep', 'span'), pairs)  9.95 us
    ppermute x8, starting transfers between devices, from_chips(): lax.ppermute(x, 'sweep', ring('sweep', CORES * back))  9.89 us
    ppermute x6, waiting for transfers between devices, along_span(): return lax.ppermute(x, ('sweep', 'span'), pairs)  8.92 us
    all_to_all x1, blocking collectives, per_device(): lax.all_to_all(own, 'sweep', 0, 0, axis_index_groups=[[i, i + 1] for i in...  8.34 us
    ppermute x2, starting transfers between devices, swap(): return lax.ppermute(x, 'sweep', [(i, i ^ 1) for i in range(devices)])  6.08 us
    unnamed x20, local copies, waits for them, and re-layouts  1.77 us
  transfers between devices with their start and end apart: 16, of which 3 were waited for; matrix products, arithmetic and copies ran while one was open for 0% of the time, Pallas kernels for 35%

profile of v5, /device:TPU:1, one launch (start us, length us, event | category | flops | bytes accessed | tf_op | source)
XLA Modules:
  0.0 82.1 jit_solution(14128446187172153724)
XLA Ops:
  0.0 0.1 pad_add_fusion.refs_0_
  0.1 0.0 copy-start.9
  0.1 1.7 %copy-done.9 = f32[2,1,625,512]{3,1,2,0:T(1,128)S(1)} copy-done((f32[2,1,625,512]{3,1,2,0:T(1,128)S(1)}, f32[2,1,625,512]{3,1,2,0:T(1,128)}, u32[]{:S(2)}) %copy-start.9) | copy-done | bytes 2560024
  1.8 1.0 %start_faces.1 = (f32[2,25,5,1,256]{4,3,2,1,0:T(1,128)S(1)}, f32[2,25,5,1,256]{4,3,2,1,0:T(1,128)S(1)}, f32[2,25,5,1,256]{4,3,2,1,0:T(1,128)S(1)}, f32[2,25,5,1,256]{4,3,2,1,0:T(1,128)S(1)}) custom-call(s32[3]{0:T(128)S(1)} %pad_add_fusion.refs_0_, f32[2,25,25,1,512]{4,3,2,1,0:T(1,128)S(1)} %bitcast.37), custom_call_target="tpu_custom_call" | custom-call | flops 1000000000 | tf_op jit(solution)/shard_map/start_faces/pallas_call | solution.py:68
  2.8 0.0 copy-start.5
  2.8 0.0 copy-start.6
  2.8 0.0 copy-start.7
  2.8 0.0 copy-start.8
  2.8 4.8 %collective-permute-start.1 = (f32[2,125,1,256]{3,2,1,0:T(1,128)S(1)}, f32[2,125,1,256]{3,2,1,0:T(1,128)S(1)}, u32[]{:S(2)}, u32[]{:S(2)}) collective-permute-start(f32[2,125,1,256]{3,2,1,0:T(1,128)S(1)} %bitcast.36), channel_id=1, source_target_pairs={{0,7},{1,6},{2,5},{3,4},{4,3},{5,2},{6,1},{7,0},{8,15},{9,14},{10,... | collective-permute-start | bytes 768008 | tf_op jit(solution)/shard_map/ppermute | solution.py:442
  7.6 0.0 collective-permute-start.2
  7.6 0.0 collective-permute-start.3
  7.6 1.8 %collective-permute-start = (f32[2,125,1,256]{3,2,1,0:T(1,128)S(1)}, f32[2,125,1,256]{3,2,1,0:T(1,128)S(1)}, u32[]{:S(2)}, u32[]{:S(2)}) collective-permute-start(f32[2,125,1,256]{3,2,1,0:T(1,128)S(1)} %bitcast.33), channel_id=1, source_target_pairs={{0,1},{1,0},{2,3},{3,2},{4,5},{5,4},{6,7},{7,6},{8,9},{9,8},{10,11... | collective-permute-start | bytes 768008 | tf_op jit(solution)/shard_map/ppermute | solution.py:442
  9.4 0.0 copy-done.5
  9.4 0.0 copy-done.6
  9.4 0.0 copy-done.7
  9.4 0.0 copy-done.8
  9.4 7.9 %fold_faces.1 = f32[2,2,384,640]{3,2,1,0:T(8,128)} custom-call(f32[2,625,1,625]{3,2,1,0:T(1,128)} %bitcast.18, f32[2,625,1,512]{3,2,1,0:T(1,128)} %bitcast.21, f32[2,625,1,125]{3,2,1,0:T(1,128)} %bitcast.24, f32[2,625,1,125]{3,2,1,0:T(1,128)} %bitcast.27, f32[2,625,1,125]{3,2,1,0:T(1,128)} %bitcast.30, f32[2,25,5,1,256]{4,3,2,1,0:T(1,128)} %copy-done.5, ...), custom_call_target="tpu_custom_call" | custom-call | tf_op jit(solution)/shard_map/fold_faces/pallas_call | solution.py:68
  17.4 0.0 copy-start.4
  17.4 8.3 %all_to_all.5.refs_0_ = f32[2,2,384,640]{3,2,1,0:T(8,128)S(1)} all-to-all(f32[2,2,384,640]{3,2,1,0:T(8,128)} %fold_faces.1), channel_id=1, replica_groups={{0,4},{8,12},{16,20},{24,28},{1,5},{9,13},{17,21},{25,29},{2,6},{10,14}..., dimensions={0} | all-to-all | bytes 7864320 | tf_op jit(solution)/shard_map/all_to_all | solution.py:468
  25.7 1.7 %chip_blocks.1 = (f32[4,384,256]{2,1,0:T(8,128)S(1)}, bf16[4,384,768]{2,1,0:T(8,128)(2,1)S(1)}, bf16[4,384,384]{2,1,0:T(8,128)(2,1)S(1)}, bf16[4,384,384]{2,1,0:...) custom-call(f32[2,2,384,640]{3,2,1,0:T(8,128)S(1)} %all_to_all.5.refs_0_), custom_call_target="tpu_custom_call" | custom-call | tf_op jit(solution)/shard_map/chip_blocks/pallas_call | solution.py:68
  27.4 0.0 copy-start
  27.4 1.3 %collective-permute-start.4 = (f32[128,128]{1,0:T(8,128)S(1)}, f32[128,128]{1,0:T(8,128)S(1)}, u32[]{:S(2)}, u32[]{:S(2)}) collective-permute-start(f32[128,128]{1,0:T(8,128)S(1)} %get-tuple-element.53), channel_id=1, source_target_pairs={{0,8},{4,12},{8,16},{12,20},{16,24},{20,28},{24,0},{28,4},{1,9},{5... | collective-permute-start | bytes 196616 | tf_op jit(solution)/shard_map/ppermute | solution.py:432
  28.7 0.0 collective-permute-done.1.refs_1_
  28.7 1.2 %collective-permute-start.5 = (f32[128,128]{1,0:T(8,128)S(1)}, f32[128,128]{1,0:T(8,128)S(1)}, u32[]{:S(2)}, u32[]{:S(2)}) collective-permute-start(f32[128,128]{1,0:T(8,128)S(1)} %get-tuple-element.53), channel_id=1, source_target_pairs={{0,16},{4,20},{8,24},{12,28},{16,0},{20,4},{24,8},{28,12},{1,17},{... | collective-permute-start | bytes 196616 | tf_op jit(solution)/shard_map/ppermute | solution.py:432
  29.9 0.0 collective-permute-done.2.refs_2_
  29.9 0.0 collective-permute-done.3.refs_3_
  29.9 1.2 %early_halos.1 = (bf16[1024,256]{1,0:T(8,128)(2,1)S(1)}, bf16[1024,256]{1,0:T(8,128)(2,1)S(1)}) custom-call(s32[3]{0:T(128)S(1)} %pad_add_fusion.refs_0_, f32[2,125,1,256]{3,2,1,0:T(1,128)S(1)} %collective-permute-done.1.refs_1_, f32[2,125,1,256]{3,2,1,0:T(1,128)S(1)} %collective-permute-done.2.refs_2_, f32[2,125,1,256]{3,2,1,0:T(1,128)S(1)} %collective-permute-done.3.refs_3_), custom_call_target="tpu_custom_call" | custom-call | flops 1000000000 | tf_op jit(solution)/shard_map/early_halos/pallas_call | solution.py:68
  31.1 0.0 collective-permute-done.refs_4_
  31.1 0.0 copy-done.4
  31.1 0.0 copy-done.1
  31.1 0.0 copy-done.2
  31.2 0.0 copy-done.3
  31.2 0.0 copy-done
  31.2 1.4 %first_traces.1 = (bf16[1024,256]{1,0:T(8,128)(2,1)S(1)}, bf16[1024,256]{1,0:T(8,128)(2,1)S(1)}, f32[128,256]{1,0:T(8,128)S(1)}, f32[640,512]{1,0:T(8,128)S(1)},...) custom-call(s32[3]{0:T(128)S(1)} %pad_add_fusion.refs_0_, ...), custom_call_target="tpu_custom_call", output_to_operand_aliasing={{0}: (10, {}), {1}: (11, {})} | custom-call | flops 2000000000 | tf_op jit(solution)/shard_map/first_traces/pallas_call | solution.py:68
  32.6 0.9 %collective-permute-start.6 = (f32[128,256]{1,0:T(8,128)S(1)}, f32[128,256]{1,0:T(8,128)S(1)}, u32[]{:S(2)}, u32[]{:S(2)}) collective-permute-start(f32[128,256]{1,0:T(8,128)S(1)} %get-tuple-element.55), channel_id=1, source_target_pairs={{0,8},{4,12},{8,16},{12,20},{16,24},{20,28},{24,0},{28,4},{1,9},{5... | collective-permute-start | bytes 393224 | tf_op jit(solution)/shard_map/ppermute | solution.py:432
  33.5 1.2 %collective-permute-start.7 = (f32[128,256]{1,0:T(8,128)S(1)}, f32[128,256]{1,0:T(8,128)S(1)}, u32[]{:S(2)}, u32[]{:S(2)}) collective-permute-start(f32[128,256]{1,0:T(8,128)S(1)} %get-tuple-element.55), channel_id=1, source_target_pairs={{0,16},{4,20},{8,24},{12,28},{16,0},{20,4},{24,8},{28,12},{1,17},{... | collective-permute-start | bytes 393224 | tf_op jit(solution)/shard_map/ppermute | solution.py:432
  34.7 1.2 %collective-permute-start.8 = (f32[128,256]{1,0:T(8,128)S(1)}, f32[128,256]{1,0:T(8,128)S(1)}, u32[]{:S(2)}, u32[]{:S(2)}) collective-permute-start(f32[128,256]{1,0:T(8,128)S(1)} %get-tuple-element.55), channel_id=1, source_target_pairs={{0,24},{4,28},{8,0},{12,4},{16,8},{20,12},{24,16},{28,20},{1,25},{... | collective-permute-start | bytes 393224 | tf_op jit(solution)/shard_map/ppermute | solution.py:432
  35.9 0.0 collective-permute-done.4.refs_5_.refs_6_
  35.9 0.0 collective-permute-done.5.refs_6_.refs_7_
  35.9 1.3 %other_faces.1.refs_1_ = f32[4,256,256]{2,1,0:T(8,128)S(1)} custom-call(f32[4,384,256]{2,1,0:T(8,128)S(1)} %get-tuple-element.48.refs_0_, bf16[4,384,768]{2,1,0:T(8,128)(2,1)S(1)} %get-tuple-element.49.refs_1_, bf16[4,384,384]{2,1,0:T(8,128)(2,1)S(1)} %get-tuple-element.50.refs_2_, bf16[1024,256]{1,0:T(8,128)(2,1)S(1)} %get-tuple-element.51.refs_3_, ...), custom_call_target="tpu_custom_call" | custom-call | flops 2000000000 | tf_op jit(solution)/shard_map/other_faces/pallas_call | solution.py:68
  37.2 0.3 collective-permute-done.6.refs_3_
  37.4 1.3 %collective-permute-done.7.refs_4_ = f32[128,256]{1,0:T(8,128)S(1)} collective-permute-done((f32[128,256]{1,0:T(8,128)S(1)}, f32[128,256]{1,0:T(8,128)S(1)}, u32[]{:S(2)}, u32[]{:S(2)}) %collective-permute-start.7) | collective-permute-done | bytes 131104 | tf_op jit(solution)/shard_map/ppermute | solution.py:432
  38.7 0.0 collective-permute-done.8.refs_5_
  38.7 1.1 %next_faces.1 = (f32[4,128,256]{2,1,0:T(8,128)S(1)}, f32[4,128,256]{2,1,0:T(8,128)S(1)}) custom-call(s32[3]{0:T(128)S(1)} %pad_add_fusion.refs_0_, f32[4,256,256]{2,1,0:T(8,128)S(1)} %other_faces.1.refs_1_, bf16[4,384,384]{2,1,0:T(8,128)(2,1)S(1)} %get-tuple-element.54.refs_2_, f32[128,256]{1,0:T(8,128)S(1)} %collective-permute-done.6.refs_3_, ...), custom_call_target="tpu_custom_call" | custom-call | flops 1000000000 | tf_op jit(solution)/shard_map/next_faces/pallas_call | solution.py:68
  39.8 3.3 %collective-permute-start.10 = (f32[4,128,256]{2,1,0:T(8,128)S(1)}, f32[4,128,256]{2,1,0:T(8,128)S(1)}, u32[]{:S(2)}, u32[]{:S(2)}) collective-permute-start(f32[4,128,256]{2,1,0:T(8,128)S(1)} %get-tuple-element.57.refs_7_), channel_id=1, source_target_pairs={{0,3},{1,2},{2,1},{3,0},{4,7},{5,6},{6,5},{7,4},{8,11},{9,10},{10,... | collective-permute-start | bytes 1572872 | tf_op jit(solution)/shard_map/ppermute | solution.py:442
  43.1 0.0 collective-permute-start.9
  43.1 11.7 %fold_rest.1 = (f32[640,512]{1,0:T(8,128)S(1)}, bf16[640,768]{1,0:T(8,128)(2,1)S(1)}, bf16[640,384]{1,0:T(8,128)(2,1)S(1)}, f32[640,512]{1,0:T(8,128)S(1)}, bf16...) custom-call(s32[3]{0:T(128)S(1)} %pad_add_fusion.refs_0_, f32[2,625,1,625]{3,2,1,0:T(1,128)S(1)} %bitcast.20, ...), custom_call_target="tpu_custom_call" | custom-call | flops 10000000000 | tf_op jit(solution)/shard_map/fold_rest/pallas_call | solution.py:68
  54.9 0.0 collective-permute-done.10.refs_4_.refs_8_
  54.9 8.9 %collective-permute-done.9.refs_5_.refs_7_ = f32[4,128,256]{2,1,0:T(8,128)S(1)} collective-permute-done((f32[4,128,256]{2,1,0:T(8,128)S(1)}, f32[4,128,256]{2,1,0:T(8,128)S(1)}, u32[]{:S(2)}, u32[]{:S(2)}) %collective-permute-start.9) | collective-permute-done | bytes 524320 | tf_op jit(solution)/shard_map/ppermute | solution.py:442
  63.8 1.3 %last_traces.1 = (f32[128,256]{1,0:T(8,128)S(1)}, f32[128,256]{1,0:T(8,128)S(1)}, f32[2,2,128,256]{3,2,1,0:T(8,128)S(1)}) custom-call(s32[3]{0:T(128)S(1)} %pad_add_fusion.refs_0_, f32[256,256]{1,0:T(8,128)S(1)} %get-tuple-element.42.refs_1_, bf16[256,1024]{1,0:T(8,128)(2,1)S(1)} %get-tuple-element.43.refs_2_, ...), custom_call_target="tpu_custom_call" | custom-call | flops 1000000000 | tf_op jit(solution)/shard_map/last_traces/pallas_call | solution.py:68
  65.1 0.9 %collective-permute-start.12 = (f32[128,256]{1,0:T(8,128)S(1)}, f32[128,256]{1,0:T(8,128)S(1)}, u32[]{:S(2)}, u32[]{:S(2)}) collective-permute-start(f32[128,256]{1,0:T(8,128)S(1)} %get-tuple-element.63.refs_9_), channel_id=1, source_target_pairs={{0,8},{4,12},{8,16},{12,20},{16,24},{20,28},{24,0},{28,4},{1,9},{5... | collective-permute-start | bytes 393224 | tf_op jit(solution)/shard_map/ppermute | solution.py:432
  66.0 1.5 %collective-permute-start.13 = (f32[128,256]{1,0:T(8,128)S(1)}, f32[128,256]{1,0:T(8,128)S(1)}, u32[]{:S(2)}, u32[]{:S(2)}) collective-permute-start(f32[128,256]{1,0:T(8,128)S(1)} %get-tuple-element.63.refs_9_), channel_id=1, source_target_pairs={{0,16},{4,20},{8,24},{12,28},{16,0},{20,4},{24,8},{28,12},{1,17},{... | collective-permute-start | bytes 393224 | tf_op jit(solution)/shard_map/ppermute | solution.py:432
  67.5 1.7 %collective-permute-start.14 = (f32[128,256]{1,0:T(8,128)S(1)}, f32[128,256]{1,0:T(8,128)S(1)}, u32[]{:S(2)}, u32[]{:S(2)}) collective-permute-start(f32[128,256]{1,0:T(8,128)S(1)} %get-tuple-element.63.refs_9_), channel_id=1, source_target_pairs={{0,24},{4,28},{8,0},{12,4},{16,8},{20,12},{24,16},{28,20},{1,25},{... | collective-permute-start | bytes 393224 | tf_op jit(solution)/shard_map/ppermute | solution.py:432
  69.2 4.0 %collective-permute-start.11 = (f32[2,2,128,256]{3,2,1,0:T(8,128)S(1)}, f32[2,2,128,256]{3,2,1,0:T(8,128)S(1)}, u32[]{:S(2)}, u32[]{:S(2)}) collective-permute-start(f32[2,2,128,256]{3,2,1,0:T(8,128)S(1)} %get-tuple-element.64), channel_id=1, source_target_pairs={{0,4},{4,0},{8,12},{12,8},{16,20},{20,16},{24,28},{28,24},{1,5},{5... | collective-permute-start | bytes 1572872 | tf_op jit(solution)/shard_map/ppermute | solution.py:428
  73.2 1.5 %field_without_inflow.2.refs_1_ = f32[2,640,256]{2,1,0:T(8,128)S(1)} custom-call(s32[3]{0:T(128)S(1)} %pad_add_fusion.refs_0_, f32[640,512]{1,0:T(8,128)S(1)} %get-tuple-element.47.refs_1_, f32[640,512]{1,0:T(8,128)S(1)} %get-tuple-element.58.refs_6_.refs_2_, f32[640,512]{1,0:T(8,128)S(1)} %get-tuple-element.59.refs_3_, ...), custom_call_target="tpu_custom_call" | custom-call | tf_op jit(solution)/shard_map/field_without_inflow/pallas_call | solution.py:68
  74.7 0.0 collective-permute-done.12.refs_3_
  74.7 0.0 collective-permute-done.13.refs_4_
  74.7 0.0 collective-permute-done.14.refs_5_
  74.7 0.8 inflow_of_cores.1
  75.5 2.1 %collective-permute-start.15 = (f32[128,256]{1,0:T(8,128)S(1)}, f32[128,256]{1,0:T(8,128)S(1)}, u32[]{:S(2)}, u32[]{:S(2)}) collective-permute-start(f32[128,256]{1,0:T(8,128)S(1)} %get-tuple-element.67), channel_id=1, source_target_pairs={{0,4},{4,0},{8,12},{12,8},{16,20},{20,16},{24,28},{28,24},{1,5},{5... | collective-permute-start | bytes 393224 | tf_op jit(solution)/shard_map/ppermute | solution.py:428
  77.6 0.0 collective-permute-done.11
  77.6 1.5 %field_without_inflow.3.refs_2_ = f32[2,640,256]{2,1,0:T(8,128)S(1)} custom-call(s32[3]{0:T(128)S(1)} %pad_add_fusion.refs_0_, f32[640,512]{1,0:T(8,128)S(1)} %get-tuple-element.47.refs_1_, f32[640,512]{1,0:T(8,128)S(1)} %get-tuple-element.58.refs_6_.refs_2_, f32[640,512]{1,0:T(8,128)S(1)} %get-tuple-element.59.refs_3_, ...), custom_call_target="tpu_custom_call" | custom-call | tf_op jit(solution)/shard_map/field_without_inflow/pallas_call | solution.py:68
  79.1 0.0 collective-permute-done.15.refs_4_
  79.1 2.7 %whole_field.1 = f32[2,625,1,512]{3,2,1,0:T(1,128)} custom-call(s32[3]{0:T(128)S(1)} %pad_add_fusion.refs_0_, f32[2,640,256]{2,1,0:T(8,128)S(1)} %field_without_inflow.2.refs_1_, f32[2,640,256]{2,1,0:T(8,128)S(1)} %field_without_inflow.3.refs_2_, f32[128,256]{1,0:T(8,128)S(1)} %get-tuple-element.66.refs_3_, f32[128,256]{1,0:T(8,128)S(1)} %collective-permute-done.15.refs_4_, ...), custom_call_target="tpu_custom_call" | custom-call | flops 1000000000 | tf_op jit(solution)/shard_map/whole_field/pallas_call | solution.py:68
  (4 shorter events, 0.0 us)
Async XLA Ops:
  0.1 1.7 %copy-start.9 = (f32[2,1,625,512]{3,1,2,0:T(1,128)S(1)}, f32[2,1,625,512]{3,1,2,0:T(1,128)}, u32[]{:S(2)}) copy-start(f32[2,1,625,512]{3,1,2,0:T(1,128)} %param.7) | copy-start | bytes 7680004
  2.8 6.6 %copy-start.5 = (f32[2,25,5,1,256]{4,3,2,1,0:T(1,128)}, f32[2,25,5,1,256]{4,3,2,1,0:T(1,128)S(1)}, u32[]{:S(2)}) copy-start(f32[2,25,5,1,256]{4,3,2,1,0:T(1,128)S(1)} %get-tuple-element.38.refs_5_) | copy-start | bytes 768004
  2.8 6.6 %copy-start.6 = (f32[2,25,5,1,256]{4,3,2,1,0:T(1,128)}, f32[2,25,5,1,256]{4,3,2,1,0:T(1,128)S(1)}, u32[]{:S(2)}) copy-start(f32[2,25,5,1,256]{4,3,2,1,0:T(1,128)S(1)} %get-tuple-element.40.refs_7_) | copy-start | bytes 768004
  2.8 6.6 %copy-start.7 = (f32[2,25,5,1,256]{4,3,2,1,0:T(1,128)}, f32[2,25,5,1,256]{4,3,2,1,0:T(1,128)S(1)}, u32[]{:S(2)}) copy-start(f32[2,25,5,1,256]{4,3,2,1,0:T(1,128)S(1)} %get-tuple-element.39.refs_6_) | copy-start | bytes 768004
  2.8 6.6 %copy-start.8 = (f32[2,25,5,1,256]{4,3,2,1,0:T(1,128)}, f32[2,25,5,1,256]{4,3,2,1,0:T(1,128)S(1)}, u32[]{:S(2)}) copy-start(f32[2,25,5,1,256]{4,3,2,1,0:T(1,128)S(1)} %get-tuple-element.41.refs_8_) | copy-start | bytes 768004
  2.8 25.9 %collective-permute-start.1 = (f32[2,125,1,256]{3,2,1,0:T(1,128)S(1)}, f32[2,125,1,256]{3,2,1,0:T(1,128)S(1)}, u32[]{:S(2)}, u32[]{:S(2)}) collective-permute-start(f32[2,125,1,256]{3,2,1,0:T(1,128)S(1)} %bitcast.36), channel_id=1, source_target_pairs={{0,7},{1,6},{2,5},{3,4},{4,3},{5,2},{6,1},{7,0},{8,15},{9,14},{10,... | collective-permute-start | bytes 768008 | tf_op jit(solution)/shard_map/ppermute | solution.py:442
  7.6 22.3 %collective-permute-start.2 = (f32[2,125,1,256]{3,2,1,0:T(1,128)S(1)}, f32[2,125,1,256]{3,2,1,0:T(1,128)S(1)}, u32[]{:S(2)}, u32[]{:S(2)}) collective-permute-start(f32[2,125,1,256]{3,2,1,0:T(1,128)S(1)} %bitcast.35), channel_id=1, source_target_pairs={{0,3},{1,2},{2,1},{3,0},{4,7},{5,6},{6,5},{7,4},{8,11},{9,10},{10,... | collective-permute-start | bytes 768008 | tf_op jit(solution)/shard_map/ppermute | solution.py:442
  7.6 22.3 %collective-permute-start.3 = (f32[2,125,1,256]{3,2,1,0:T(1,128)S(1)}, f32[2,125,1,256]{3,2,1,0:T(1,128)S(1)}, u32[]{:S(2)}, u32[]{:S(2)}) collective-permute-start(f32[2,125,1,256]{3,2,1,0:T(1,128)S(1)} %bitcast.34), channel_id=1, source_target_pairs={{0,5},{1,4},{2,7},{3,6},{4,1},{5,0},{6,3},{7,2},{8,13},{9,12},{10,... | collective-permute-start | bytes 768008 | tf_op jit(solution)/shard_map/ppermute | solution.py:442
  7.6 23.5 %collective-permute-start = (f32[2,125,1,256]{3,2,1,0:T(1,128)S(1)}, f32[2,125,1,256]{3,2,1,0:T(1,128)S(1)}, u32[]{:S(2)}, u32[]{:S(2)}) collective-permute-start(f32[2,125,1,256]{3,2,1,0:T(1,128)S(1)} %bitcast.33), channel_id=1, source_target_pairs={{0,1},{1,0},{2,3},{3,2},{4,5},{5,4},{6,7},{7,6},{8,9},{9,8},{10,11... | collective-permute-start | bytes 768008 | tf_op jit(solution)/shard_map/ppermute | solution.py:442
  17.4 13.8 %copy-start.4 = (f32[2,1,625,125]{3,1,2,0:T(1,128)S(1)}, f32[2,1,625,125]{3,1,2,0:T(1,128)}, u32[]{:S(2)}) copy-start(f32[2,1,625,125]{3,1,2,0:T(1,128)} %param.11) | copy-start | bytes 1875004
  25.7 5.4 %copy-start.1 = (f32[2,1,625,512]{3,1,2,0:T(1,128)S(1)}, f32[2,1,625,512]{3,1,2,0:T(1,128)}, u32[]{:S(2)}) copy-start(f32[2,1,625,512]{3,1,2,0:T(1,128)} %param.6) | copy-start | bytes 7680004
  25.7 5.4 %copy-start.2 = (f32[2,1,625,125]{3,1,2,0:T(1,128)S(1)}, f32[2,1,625,125]{3,1,2,0:T(1,128)}, u32[]{:S(2)}) copy-start(f32[2,1,625,125]{3,1,2,0:T(1,128)} %param.9) | copy-start | bytes 1875004
  25.7 5.4 %copy-start.3 = (f32[2,1,625,125]{3,1,2,0:T(1,128)S(1)}, f32[2,1,625,125]{3,1,2,0:T(1,128)}, u32[]{:S(2)}) copy-start(f32[2,1,625,125]{3,1,2,0:T(1,128)} %param.10) | copy-start | bytes 1875004
  27.4 3.8 %copy-start = (f32[2,1,625,625]{3,1,2,0:T(1,128)S(1)}, f32[2,1,625,625]{3,1,2,0:T(1,128)}, u32[]{:S(2)}) copy-start(f32[2,1,625,625]{3,1,2,0:T(1,128)} %param.8) | copy-start | bytes 9375004
  27.4 8.5 %collective-permute-start.4 = (f32[128,128]{1,0:T(8,128)S(1)}, f32[128,128]{1,0:T(8,128)S(1)}, u32[]{:S(2)}, u32[]{:S(2)}) collective-permute-start(f32[128,128]{1,0:T(8,128)S(1)} %get-tuple-element.53), channel_id=1, source_target_pairs={{0,8},{4,12},{8,16},{12,20},{16,24},{20,28},{24,0},{28,4},{1,9},{5... | collective-permute-start | bytes 196616 | tf_op jit(solution)/shard_map/ppermute | solution.py:432
  28.7 7.2 %collective-permute-start.5 = (f32[128,128]{1,0:T(8,128)S(1)}, f32[128,128]{1,0:T(8,128)S(1)}, u32[]{:S(2)}, u32[]{:S(2)}) collective-permute-start(f32[128,128]{1,0:T(8,128)S(1)} %get-tuple-element.53), channel_id=1, source_target_pairs={{0,16},{4,20},{8,24},{12,28},{16,0},{20,4},{24,8},{28,12},{1,17},{... | collective-permute-start | bytes 196616 | tf_op jit(solution)/shard_map/ppermute | solution.py:432
  32.6 4.9 %collective-permute-start.6 = (f32[128,256]{1,0:T(8,128)S(1)}, f32[128,256]{1,0:T(8,128)S(1)}, u32[]{:S(2)}, u32[]{:S(2)}) collective-permute-start(f32[128,256]{1,0:T(8,128)S(1)} %get-tuple-element.55), channel_id=1, source_target_pairs={{0,8},{4,12},{8,16},{12,20},{16,24},{20,28},{24,0},{28,4},{1,9},{5... | collective-permute-start | bytes 393224 | tf_op jit(solution)/shard_map/ppermute | solution.py:432
  33.5 5.2 %collective-permute-start.7 = (f32[128,256]{1,0:T(8,128)S(1)}, f32[128,256]{1,0:T(8,128)S(1)}, u32[]{:S(2)}, u32[]{:S(2)}) collective-permute-start(f32[128,256]{1,0:T(8,128)S(1)} %get-tuple-element.55), channel_id=1, source_target_pairs={{0,16},{4,20},{8,24},{12,28},{16,0},{20,4},{24,8},{28,12},{1,17},{... | collective-permute-start | bytes 393224 | tf_op jit(solution)/shard_map/ppermute | solution.py:432
  34.7 4.0 %collective-permute-start.8 = (f32[128,256]{1,0:T(8,128)S(1)}, f32[128,256]{1,0:T(8,128)S(1)}, u32[]{:S(2)}, u32[]{:S(2)}) collective-permute-start(f32[128,256]{1,0:T(8,128)S(1)} %get-tuple-element.55), channel_id=1, source_target_pairs={{0,24},{4,28},{8,0},{12,4},{16,8},{20,12},{24,16},{28,20},{1,25},{... | collective-permute-start | bytes 393224 | tf_op jit(solution)/shard_map/ppermute | solution.py:432
  39.8 15.1 %collective-permute-start.10 = (f32[4,128,256]{2,1,0:T(8,128)S(1)}, f32[4,128,256]{2,1,0:T(8,128)S(1)}, u32[]{:S(2)}, u32[]{:S(2)}) collective-permute-start(f32[4,128,256]{2,1,0:T(8,128)S(1)} %get-tuple-element.57.refs_7_), channel_id=1, source_target_pairs={{0,3},{1,2},{2,1},{3,0},{4,7},{5,6},{6,5},{7,4},{8,11},{9,10},{10,... | collective-permute-start | bytes 1572872 | tf_op jit(solution)/shard_map/ppermute | solution.py:442
  43.1 20.7 %collective-permute-start.9 = (f32[4,128,256]{2,1,0:T(8,128)S(1)}, f32[4,128,256]{2,1,0:T(8,128)S(1)}, u32[]{:S(2)}, u32[]{:S(2)}) collective-permute-start(f32[4,128,256]{2,1,0:T(8,128)S(1)} %get-tuple-element.56.refs_6_), channel_id=1, source_target_pairs={{0,1},{1,0},{2,3},{3,2},{4,5},{5,4},{6,7},{7,6},{8,9},{9,8},{10,11... | collective-permute-start | bytes 1572872 | tf_op jit(solution)/shard_map/ppermute | solution.py:442
  65.1 9.6 %collective-permute-start.12 = (f32[128,256]{1,0:T(8,128)S(1)}, f32[128,256]{1,0:T(8,128)S(1)}, u32[]{:S(2)}, u32[]{:S(2)}) collective-permute-start(f32[128,256]{1,0:T(8,128)S(1)} %get-tuple-element.63.refs_9_), channel_id=1, source_target_pairs={{0,8},{4,12},{8,16},{12,20},{16,24},{20,28},{24,0},{28,4},{1,9},{5... | collective-permute-start | bytes 393224 | tf_op jit(solution)/shard_map/ppermute | solution.py:432
  66.0 8.7 %collective-permute-start.13 = (f32[128,256]{1,0:T(8,128)S(1)}, f32[128,256]{1,0:T(8,128)S(1)}, u32[]{:S(2)}, u32[]{:S(2)}) collective-permute-start(f32[128,256]{1,0:T(8,128)S(1)} %get-tuple-element.63.refs_9_), channel_id=1, source_target_pairs={{0,16},{4,20},{8,24},{12,28},{16,0},{20,4},{24,8},{28,12},{1,17},{... | collective-permute-start | bytes 393224 | tf_op jit(solution)/shard_map/ppermute | solution.py:432
  67.5 7.2 %collective-permute-start.14 = (f32[128,256]{1,0:T(8,128)S(1)}, f32[128,256]{1,0:T(8,128)S(1)}, u32[]{:S(2)}, u32[]{:S(2)}) collective-permute-start(f32[128,256]{1,0:T(8,128)S(1)} %get-tuple-element.63.refs_9_), channel_id=1, source_target_pairs={{0,24},{4,28},{8,0},{12,4},{16,8},{20,12},{24,16},{28,20},{1,25},{... | collective-permute-start | bytes 393224 | tf_op jit(solution)/shard_map/ppermute | solution.py:432
  69.2 8.4 %collective-permute-start.11 = (f32[2,2,128,256]{3,2,1,0:T(8,128)S(1)}, f32[2,2,128,256]{3,2,1,0:T(8,128)S(1)}, u32[]{:S(2)}, u32[]{:S(2)}) collective-permute-start(f32[2,2,128,256]{3,2,1,0:T(8,128)S(1)} %get-tuple-element.64), channel_id=1, source_target_pairs={{0,4},{4,0},{8,12},{12,8},{16,20},{20,16},{24,28},{28,24},{1,5},{5... | collective-permute-start | bytes 1572872 | tf_op jit(solution)/shard_map/ppermute | solution.py:428
  75.5 3.6 %collective-permute-start.15 = (f32[128,256]{1,0:T(8,128)S(1)}, f32[128,256]{1,0:T(8,128)S(1)}, u32[]{:S(2)}, u32[]{:S(2)}) collective-permute-start(f32[128,256]{1,0:T(8,128)S(1)} %get-tuple-element.67), channel_id=1, source_target_pairs={{0,4},{4,0},{8,12},{12,8},{16,20},{20,16},{24,28},{28,24},{1,5},{5... | collective-permute-start | bytes 393224 | tf_op jit(solution)/shard_map/ppermute | solution.py:428

commit v6 on v5

--- a/solution.py
+++ b/solution.py
@@ -13,8 +13,8 @@
 WIDE = 128
 SWEEPS = 2
 CORES = 2
-EARLY = (3, 1, 2)
-LATE = (0,)
+EARLY = (0, 1, 3)
+LATE = (2,)
 LIMIT = 24 * 1024 * 1024
 MOST = 60 * 1024 * 1024
 ANY = pl.ANY
@@ -269,21 +269,22 @@
         faces_ref[e] = faces[WIDE:]
 
 
-def last_traces(core_ref, const_ref, high_ref, low_ref, second_ref, first_ref, out_ref, lead_ref, away_ref,
-                halo_high, halo_low):
+def last_traces(rows, core_ref, const_ref, high_ref, low_ref, second_ref, first_ref, out_ref, *refs):
+    halo_high, halo_low = refs[-2:]
     count = first_ref.shape[0]
-    elements = count // CORES
     for e in range(count):
         for k, ref in enumerate((first_ref, second_ref)):
             at = pl.ds(pl.multiple_of(south_north(core_ref, k) + 2 * e * WIDE, WIDE), WIDE)
             halo_high[at, :], halo_low[at, :] = split(ref[e])
-    both = traces(const_ref[...], high_ref[...], low_ref[...], halo_high[...], halo_low[...])
-    out_ref[...] = both[:WIDE]
-    lead_ref[...] = both[WIDE:]
-    other = (1 - core_ref[0]) * elements
-    for e in range(elements):
-        away_ref[0, e] = first_ref[other + e]
-        away_ref[1, e] = second_ref[other + e]
+    out_ref[...] = traces(
+        const_ref[rows, :], high_ref[rows, :], low_ref[rows, :], halo_high[...], halo_low[...]
+    )
+    if len(refs) > 2:
+        elements = count // CORES
+        other = (1 - core_ref[0]) * elements
+        for e in range(elements):
+            refs[0][0, e] = first_ref[other + e]
+            refs[0][1, e] = second_ref[other + e]
 
 
 def through_chips(core_ref, inflow_ref, chips, steps):
@@ -533,17 +534,21 @@
         after=last,
     )
     c, bsn, bu = [held([early[k], *late[k::3]]) for k in range(3)]
-    out, lead, away = call(
-        last_traces,
-        [
-            (VMEM, (WIDE, half), f32),
-            (VMEM, (WIDE, half), f32),
-            (VMEM, (2, elements, WIDE, half), f32),
-        ],
+    (out,) = call(
+        functools.partial(last_traces, slice(0, WIDE)),
+        [(VMEM, (WIDE, half), f32)],
         core, *held((*trace_blocks, *halos[::-1])),
         scratch=[VMEM(halo_split, bf16)] * 2,
         us=1,
         after=late[:1],
+    )
+    lead, away = call(
+        functools.partial(last_traces, slice(WIDE, 2 * WIDE)),
+        [(VMEM, (WIDE, half), f32), (VMEM, (2, elements, WIDE, half), f32)],
+        core, *held((*trace_blocks, *halos[::-1])),
+        scratch=[VMEM(halo_split, bf16)] * 2,
+        us=0,
+        after=[out],
     )
     chips = from_chips(out)
     got = swap(away)

time: 82.3 us -> 81.4 us (0.989)
  starting transfers between devices: 25.9 us -> 24.5 us
  Pallas kernels: 35 us -> 35.9 us
    ppermute x2, starting transfers between devices: 6.08 us -> 5.15 us  [swap(): return lax.ppermute(x, 'sweep', [(i, i ^ 1) for i in range(devices)])]
    pallas_call x13 -> x14, Pallas kernels: 35 us -> 35.9 us  [call(): pl.pallas_call(body, out_shape=[jax.ShapeDtypeStruct(shape, kind) for _,...]
  transfers between devices with their start and end apart: 16 -> 16, of which waited for: 3 -> 3; matrix products, arithmetic and copies ran while one was open for 0% -> 0% of each run, Pallas kernels for 35% -> 37%
where the time goes in v6:
time: 81.4 us; the launch traced here: 81.1 us
  Pallas kernels  35.9 us (44%)
  starting transfers between devices  24.5 us (30%)
  waiting for transfers between devices  10.4 us (13%)
  blocking collectives  8.03 us (10%)
  local copies, waits for them, and re-layouts  1.8 us (2%)
    pallas_call x14, Pallas kernels, call(): pl.pallas_call(body, out_shape=[jax.ShapeDtypeStruct(shape, kind) for _,...  35.9 us
    ppermute x6, starting transfers between devices, along_span(): return lax.ppermute(x, ('sweep', 'span'), pairs)  9.98 us
    ppermute x8, starting transfers between devices, from_chips(): lax.ppermute(x, 'sweep', ring('sweep', CORES * back))  9.33 us
    ppermute x6, waiting for transfers between devices, along_span(): return lax.ppermute(x, ('sweep', 'span'), pairs)  8.85 us
    all_to_all x1, blocking collectives, per_device(): lax.all_to_all(own, 'sweep', 0, 0, axis_index_groups=[[i, i + 1] for i in...  8.03 us
    ppermute x2, starting transfers between devices, swap(): return lax.ppermute(x, 'sweep', [(i, i ^ 1) for i in range(devices)])  5.15 us
    unnamed x20, local copies, waits for them, and re-layouts  1.77 us
  transfers between devices with their start and end apart: 16, of which 3 were waited for; matrix products, arithmetic and copies ran while one was open for 0% of the time, Pallas kernels for 37%

profile of v6, /device:TPU:1, one launch (start us, length us, event | category | flops | bytes accessed | tf_op | source)
XLA Modules:
  0.0 81.1 jit_solution(8131453049379719144)
XLA Ops:
  0.0 0.1 pad_add_fusion.refs_0_
  0.1 1.7 %copy-done.9 = f32[2,1,625,512]{3,1,2,0:T(1,128)S(1)} copy-done((f32[2,1,625,512]{3,1,2,0:T(1,128)S(1)}, f32[2,1,625,512]{3,1,2,0:T(1,128)}, u32[]{:S(2)}) %copy-start.9) | copy-done | bytes 2560024
  1.8 1.0 %start_faces.1 = (f32[2,25,5,1,256]{4,3,2,1,0:T(1,128)S(1)}, f32[2,25,5,1,256]{4,3,2,1,0:T(1,128)S(1)}, f32[2,25,5,1,256]{4,3,2,1,0:T(1,128)S(1)}, f32[2,25,5,1,256]{4,3,2,1,0:T(1,128)S(1)}) custom-call(s32[3]{0:T(128)S(1)} %pad_add_fusion.refs_0_, f32[2,25,25,1,512]{4,3,2,1,0:T(1,128)S(1)} %bitcast.37), custom_call_target="tpu_custom_call" | custom-call | flops 1000000000 | tf_op jit(solution)/shard_map/start_faces/pallas_call | solution.py:68
  2.8 0.0 copy-start.5
  2.8 0.0 copy-start.6
  2.8 0.0 copy-start.7
  2.8 0.0 copy-start.8
  2.8 2.2 %collective-permute-start.1 = (f32[2,125,1,256]{3,2,1,0:T(1,128)S(1)}, f32[2,125,1,256]{3,2,1,0:T(1,128)S(1)}, u32[]{:S(2)}, u32[]{:S(2)}) collective-permute-start(f32[2,125,1,256]{3,2,1,0:T(1,128)S(1)} %bitcast.36), channel_id=1, source_target_pairs={{0,1},{1,0},{2,3},{3,2},{4,5},{5,4},{6,7},{7,6},{8,9},{9,8},{10,11... | collective-permute-start | bytes 768008 | tf_op jit(solution)/shard_map/ppermute | solution.py:443
  5.0 2.2 %collective-permute-start.2 = (f32[2,125,1,256]{3,2,1,0:T(1,128)S(1)}, f32[2,125,1,256]{3,2,1,0:T(1,128)S(1)}, u32[]{:S(2)}, u32[]{:S(2)}) collective-permute-start(f32[2,125,1,256]{3,2,1,0:T(1,128)S(1)} %bitcast.35), channel_id=1, source_target_pairs={{0,3},{1,2},{2,1},{3,0},{4,7},{5,6},{6,5},{7,4},{8,11},{9,10},{10,... | collective-permute-start | bytes 768008 | tf_op jit(solution)/shard_map/ppermute | solution.py:443
  7.2 2.2 %collective-permute-start.3 = (f32[2,125,1,256]{3,2,1,0:T(1,128)S(1)}, f32[2,125,1,256]{3,2,1,0:T(1,128)S(1)}, u32[]{:S(2)}, u32[]{:S(2)}) collective-permute-start(f32[2,125,1,256]{3,2,1,0:T(1,128)S(1)} %bitcast.34), channel_id=1, source_target_pairs={{0,7},{1,6},{2,5},{3,4},{4,3},{5,2},{6,1},{7,0},{8,15},{9,14},{10,... | collective-permute-start | bytes 768008 | tf_op jit(solution)/shard_map/ppermute | solution.py:443
  9.4 0.0 collective-permute-start
  9.4 0.0 copy-done.5
  9.4 0.0 copy-done.6
  9.4 0.0 copy-done.7
  9.4 0.0 copy-done.8
  9.4 7.9 %fold_faces.1 = f32[2,2,384,640]{3,2,1,0:T(8,128)} custom-call(f32[2,625,1,625]{3,2,1,0:T(1,128)} %bitcast.18, f32[2,625,1,512]{3,2,1,0:T(1,128)} %bitcast.21, f32[2,625,1,125]{3,2,1,0:T(1,128)} %bitcast.24, f32[2,625,1,125]{3,2,1,0:T(1,128)} %bitcast.27, f32[2,625,1,125]{3,2,1,0:T(1,128)} %bitcast.30, f32[2,25,5,1,256]{4,3,2,1,0:T(1,128)} %copy-done.8, ...), custom_call_target="tpu_custom_call" | custom-call | tf_op jit(solution)/shard_map/fold_faces/pallas_call | solution.py:68
  17.4 0.0 copy-start.4
  17.4 8.0 %all_to_all.5.refs_0_ = f32[2,2,384,640]{3,2,1,0:T(8,128)S(1)} all-to-all(f32[2,2,384,640]{3,2,1,0:T(8,128)} %fold_faces.1), channel_id=1, replica_groups={{0,4},{8,12},{16,20},{24,28},{1,5},{9,13},{17,21},{25,29},{2,6},{10,14}..., dimensions={0} | all-to-all | bytes 7864320 | tf_op jit(solution)/shard_map/all_to_all | solution.py:469
  25.4 1.7 %chip_blocks.1 = (f32[4,384,256]{2,1,0:T(8,128)S(1)}, bf16[4,384,768]{2,1,0:T(8,128)(2,1)S(1)}, bf16[4,384,384]{2,1,0:T(8,128)(2,1)S(1)}, bf16[4,384,384]{2,1,0:...) custom-call(f32[2,2,384,640]{3,2,1,0:T(8,128)S(1)} %all_to_all.5.refs_0_), custom_call_target="tpu_custom_call" | custom-call | tf_op jit(solution)/shard_map/chip_blocks/pallas_call | solution.py:68
  27.1 0.0 copy-start
  27.1 1.3 %collective-permute-start.4 = (f32[128,128]{1,0:T(8,128)S(1)}, f32[128,128]{1,0:T(8,128)S(1)}, u32[]{:S(2)}, u32[]{:S(2)}) collective-permute-start(f32[128,128]{1,0:T(8,128)S(1)} %get-tuple-element.52), channel_id=1, source_target_pairs={{0,8},{4,12},{8,16},{12,20},{16,24},{20,28},{24,0},{28,4},{1,9},{5... | collective-permute-start | bytes 196616 | tf_op jit(solution)/shard_map/ppermute | solution.py:433
  28.4 0.0 collective-permute-done.1.refs_1_
  28.4 1.2 %collective-permute-start.5 = (f32[128,128]{1,0:T(8,128)S(1)}, f32[128,128]{1,0:T(8,128)S(1)}, u32[]{:S(2)}, u32[]{:S(2)}) collective-permute-start(f32[128,128]{1,0:T(8,128)S(1)} %get-tuple-element.52), channel_id=1, source_target_pairs={{0,16},{4,20},{8,24},{12,28},{16,0},{20,4},{24,8},{28,12},{1,17},{... | collective-permute-start | bytes 196616 | tf_op jit(solution)/shard_map/ppermute | solution.py:433
  29.6 0.0 collective-permute-done.2.refs_2_
  29.6 0.0 collective-permute-done.3.refs_3_
  29.6 1.2 %early_halos.1 = (bf16[1024,256]{1,0:T(8,128)(2,1)S(1)}, bf16[1024,256]{1,0:T(8,128)(2,1)S(1)}) custom-call(s32[3]{0:T(128)S(1)} %pad_add_fusion.refs_0_, f32[2,125,1,256]{3,2,1,0:T(1,128)S(1)} %collective-permute-done.1.refs_1_, f32[2,125,1,256]{3,2,1,0:T(1,128)S(1)} %collective-permute-done.2.refs_2_, f32[2,125,1,256]{3,2,1,0:T(1,128)S(1)} %collective-permute-done.3.refs_3_), custom_call_target="tpu_custom_call" | custom-call | flops 1000000000 | tf_op jit(solution)/shard_map/early_halos/pallas_call | solution.py:68
  30.8 0.0 collective-permute-done.refs_4_
  30.8 0.0 copy-done.4
  30.8 0.0 copy-done.1
  30.8 0.0 copy-done.2
  30.8 0.0 copy-done.3
  30.8 0.0 copy-done
  30.9 1.4 %first_traces.1 = (bf16[1024,256]{1,0:T(8,128)(2,1)S(1)}, bf16[1024,256]{1,0:T(8,128)(2,1)S(1)}, f32[128,256]{1,0:T(8,128)S(1)}, f32[640,512]{1,0:T(8,128)S(1)},...) custom-call(s32[3]{0:T(128)S(1)} %pad_add_fusion.refs_0_, ...), custom_call_target="tpu_custom_call", output_to_operand_aliasing={{0}: (10, {}), {1}: (11, {})} | custom-call | flops 2000000000 | tf_op jit(solution)/shard_map/first_traces/pallas_call | solution.py:68
  32.2 0.3 collective-permute-start.6
  32.5 1.2 %collective-permute-start.7 = (f32[128,256]{1,0:T(8,128)S(1)}, f32[128,256]{1,0:T(8,128)S(1)}, u32[]{:S(2)}, u32[]{:S(2)}) collective-permute-start(f32[128,256]{1,0:T(8,128)S(1)} %get-tuple-element.54), channel_id=1, source_target_pairs={{0,16},{4,20},{8,24},{12,28},{16,0},{20,4},{24,8},{28,12},{1,17},{... | collective-permute-start | bytes 393224 | tf_op jit(solution)/shard_map/ppermute | solution.py:433
  33.7 1.2 %collective-permute-start.8 = (f32[128,256]{1,0:T(8,128)S(1)}, f32[128,256]{1,0:T(8,128)S(1)}, u32[]{:S(2)}, u32[]{:S(2)}) collective-permute-start(f32[128,256]{1,0:T(8,128)S(1)} %get-tuple-element.54), channel_id=1, source_target_pairs={{0,24},{4,28},{8,0},{12,4},{16,8},{20,12},{24,16},{28,20},{1,25},{... | collective-permute-start | bytes 393224 | tf_op jit(solution)/shard_map/ppermute | solution.py:433
  34.9 0.0 collective-permute-done.4.refs_5_.refs_6_
  34.9 0.0 collective-permute-done.5.refs_6_.refs_7_
  34.9 1.3 %other_faces.1.refs_1_ = f32[4,256,256]{2,1,0:T(8,128)S(1)} custom-call(f32[4,384,256]{2,1,0:T(8,128)S(1)} %get-tuple-element.47.refs_0_, bf16[4,384,768]{2,1,0:T(8,128)(2,1)S(1)} %get-tuple-element.48.refs_1_, bf16[4,384,384]{2,1,0:T(8,128)(2,1)S(1)} %get-tuple-element.49.refs_2_, bf16[1024,256]{1,0:T(8,128)(2,1)S(1)} %get-tuple-element.50.refs_3_, ...), custom_call_target="tpu_custom_call" | custom-call | flops 2000000000 | tf_op jit(solution)/shard_map/other_faces/pallas_call | solution.py:68
  36.2 0.9 %collective-permute-done.6.refs_3_ = f32[128,256]{1,0:T(8,128)S(1)} collective-permute-done((f32[128,256]{1,0:T(8,128)S(1)}, f32[128,256]{1,0:T(8,128)S(1)}, u32[]{:S(2)}, u32[]{:S(2)}) %collective-permute-start.6) | collective-permute-done | bytes 131104 | tf_op jit(solution)/shard_map/ppermute | solution.py:433
  37.1 0.6 collective-permute-done.7.refs_4_
  37.7 0.0 collective-permute-done.8.refs_5_
  37.7 1.1 %next_faces.1 = (f32[4,128,256]{2,1,0:T(8,128)S(1)}, f32[4,128,256]{2,1,0:T(8,128)S(1)}) custom-call(s32[3]{0:T(128)S(1)} %pad_add_fusion.refs_0_, f32[4,256,256]{2,1,0:T(8,128)S(1)} %other_faces.1.refs_1_, bf16[4,384,384]{2,1,0:T(8,128)(2,1)S(1)} %get-tuple-element.53.refs_2_, f32[128,256]{1,0:T(8,128)S(1)} %collective-permute-done.6.refs_3_, ...), custom_call_target="tpu_custom_call" | custom-call | flops 1000000000 | tf_op jit(solution)/shard_map/next_faces/pallas_call | solution.py:68
  38.8 2.3 %collective-permute-start.10 = (f32[4,128,256]{2,1,0:T(8,128)S(1)}, f32[4,128,256]{2,1,0:T(8,128)S(1)}, u32[]{:S(2)}, u32[]{:S(2)}) collective-permute-start(f32[4,128,256]{2,1,0:T(8,128)S(1)} %get-tuple-element.56.refs_7_), channel_id=1, source_target_pairs={{0,3},{1,2},{2,1},{3,0},{4,7},{5,6},{6,5},{7,4},{8,11},{9,10},{10,... | collective-permute-start | bytes 1572872 | tf_op jit(solution)/shard_map/ppermute | solution.py:443
  41.1 1.1 %collective-permute-start.9 = (f32[4,128,256]{2,1,0:T(8,128)S(1)}, f32[4,128,256]{2,1,0:T(8,128)S(1)}, u32[]{:S(2)}, u32[]{:S(2)}) collective-permute-start(f32[4,128,256]{2,1,0:T(8,128)S(1)} %get-tuple-element.55.refs_6_), channel_id=1, source_target_pairs={{0,1},{1,0},{2,3},{3,2},{4,5},{5,4},{6,7},{7,6},{8,9},{9,8},{10,11... | collective-permute-start | bytes 1572872 | tf_op jit(solution)/shard_map/ppermute | solution.py:443
  42.2 11.7 %fold_rest.1 = (f32[640,512]{1,0:T(8,128)S(1)}, bf16[640,768]{1,0:T(8,128)(2,1)S(1)}, bf16[640,384]{1,0:T(8,128)(2,1)S(1)}, f32[640,512]{1,0:T(8,128)S(1)}, bf16...) custom-call(s32[3]{0:T(128)S(1)} %pad_add_fusion.refs_0_, f32[2,625,1,625]{3,2,1,0:T(1,128)S(1)} %bitcast.20, ...), custom_call_target="tpu_custom_call" | custom-call | flops 10000000000 | tf_op jit(solution)/shard_map/fold_rest/pallas_call | solution.py:68
  54.0 0.0 collective-permute-done.10.refs_4_.refs_8_
  54.0 8.8 %collective-permute-done.9.refs_5_.refs_7_ = f32[4,128,256]{2,1,0:T(8,128)S(1)} collective-permute-done((f32[4,128,256]{2,1,0:T(8,128)S(1)}, f32[4,128,256]{2,1,0:T(8,128)S(1)}, u32[]{:S(2)}, u32[]{:S(2)}) %collective-permute-start.9) | collective-permute-done | bytes 524320 | tf_op jit(solution)/shard_map/ppermute | solution.py:443
  62.8 1.1 %last_traces.2.refs_9_.refs_6_ = f32[128,256]{1,0:T(8,128)S(1)} custom-call(s32[3]{0:T(128)S(1)} %pad_add_fusion.refs_0_, f32[256,256]{1,0:T(8,128)S(1)} %get-tuple-element.41.refs_1_, bf16[256,1024]{1,0:T(8,128)(2,1)S(1)} %get-tuple-element.42.refs_2_, bf16[256,1024]{1,0:T(8,128)(2,1)S(1)} %get-tuple-element.43.refs_3_, ...), custom_call_target="tpu_custom_call" | custom-call | flops 1000000000 | tf_op jit(solution)/shard_map/last_traces/pallas_call | solution.py:68
  63.9 2.0 %collective-permute-start.12 = (f32[128,256]{1,0:T(8,128)S(1)}, f32[128,256]{1,0:T(8,128)S(1)}, u32[]{:S(2)}, u32[]{:S(2)}) collective-permute-start(f32[128,256]{1,0:T(8,128)S(1)} %last_traces.2.refs_9_.refs_6_), channel_id=1, source_target_pairs={{0,8},{4,12},{8,16},{12,20},{16,24},{20,28},{24,0},{28,4},{1,9},{5... | collective-permute-start | bytes 393224 | tf_op jit(solution)/shard_map/ppermute | solution.py:433
  65.9 1.0 %collective-permute-start.13 = (f32[128,256]{1,0:T(8,128)S(1)}, f32[128,256]{1,0:T(8,128)S(1)}, u32[]{:S(2)}, u32[]{:S(2)}) collective-permute-start(f32[128,256]{1,0:T(8,128)S(1)} %last_traces.2.refs_9_.refs_6_), channel_id=1, source_target_pairs={{0,16},{4,20},{8,24},{12,28},{16,0},{20,4},{24,8},{28,12},{1,17},{... | collective-permute-start | bytes 393224 | tf_op jit(solution)/shard_map/ppermute | solution.py:433
  66.9 1.2 %collective-permute-start.14 = (f32[128,256]{1,0:T(8,128)S(1)}, f32[128,256]{1,0:T(8,128)S(1)}, u32[]{:S(2)}, u32[]{:S(2)}) collective-permute-start(f32[128,256]{1,0:T(8,128)S(1)} %last_traces.2.refs_9_.refs_6_), channel_id=1, source_target_pairs={{0,24},{4,28},{8,0},{12,4},{16,8},{20,12},{24,16},{28,20},{1,25},{... | collective-permute-start | bytes 393224 | tf_op jit(solution)/shard_map/ppermute | solution.py:433
  68.1 1.1 %last_traces.3 = (f32[128,256]{1,0:T(8,128)S(1)}, f32[2,2,128,256]{3,2,1,0:T(8,128)S(1)}) custom-call(s32[3]{0:T(128)S(1)} %pad_add_fusion.refs_0_, f32[256,256]{1,0:T(8,128)S(1)} %get-tuple-element.41.refs_1_, bf16[256,1024]{1,0:T(8,128)(2,1)S(1)} %get-tuple-element.42.refs_2_, bf16[256,1024]{1,0:T(8,128)(2,1)S(1)} %get-tuple-element.43.refs_3_, ...), custom_call_target="tpu_custom_call" | custom-call | tf_op jit(solution)/shard_map/last_traces/pallas_call | solution.py:68
  69.2 4.0 %collective-permute-start.11 = (f32[2,2,128,256]{3,2,1,0:T(8,128)S(1)}, f32[2,2,128,256]{3,2,1,0:T(8,128)S(1)}, u32[]{:S(2)}, u32[]{:S(2)}) collective-permute-start(f32[2,2,128,256]{3,2,1,0:T(8,128)S(1)} %get-tuple-element.62), channel_id=1, source_target_pairs={{0,4},{4,0},{8,12},{12,8},{16,20},{20,16},{24,28},{28,24},{1,5},{5... | collective-permute-start | bytes 1572872 | tf_op jit(solution)/shard_map/ppermute | solution.py:429
  73.2 1.5 %field_without_inflow.2.refs_1_ = f32[2,640,256]{2,1,0:T(8,128)S(1)} custom-call(s32[3]{0:T(128)S(1)} %pad_add_fusion.refs_0_, f32[640,512]{1,0:T(8,128)S(1)} %get-tuple-element.46.refs_1_, f32[640,512]{1,0:T(8,128)S(1)} %get-tuple-element.57.refs_6_.refs_2_, f32[640,512]{1,0:T(8,128)S(1)} %get-tuple-element.58.refs_3_, ...), custom_call_target="tpu_custom_call" | custom-call | tf_op jit(solution)/shard_map/field_without_inflow/pallas_call | solution.py:68
  74.8 0.0 collective-permute-done.12.refs_3_
  74.8 0.0 collective-permute-done.13.refs_4_
  74.8 0.0 collective-permute-done.14.refs_5_
  74.8 0.8 inflow_of_cores.1
  75.6 1.1 %collective-permute-start.15 = (f32[128,256]{1,0:T(8,128)S(1)}, f32[128,256]{1,0:T(8,128)S(1)}, u32[]{:S(2)}, u32[]{:S(2)}) collective-permute-start(f32[128,256]{1,0:T(8,128)S(1)} %get-tuple-element.65), channel_id=1, source_target_pairs={{0,4},{4,0},{8,12},{12,8},{16,20},{20,16},{24,28},{28,24},{1,5},{5... | collective-permute-start | bytes 393224 | tf_op jit(solution)/shard_map/ppermute | solution.py:429
  76.7 0.0 collective-permute-done.11
  76.7 1.5 %field_without_inflow.3.refs_2_ = f32[2,640,256]{2,1,0:T(8,128)S(1)} custom-call(s32[3]{0:T(128)S(1)} %pad_add_fusion.refs_0_, f32[640,512]{1,0:T(8,128)S(1)} %get-tuple-element.46.refs_1_, f32[640,512]{1,0:T(8,128)S(1)} %get-tuple-element.57.refs_6_.refs_2_, f32[640,512]{1,0:T(8,128)S(1)} %get-tuple-element.58.refs_3_, ...), custom_call_target="tpu_custom_call" | custom-call | tf_op jit(solution)/shard_map/field_without_inflow/pallas_call | solution.py:68
  78.2 0.0 collective-permute-done.15.refs_4_
  78.2 2.7 %whole_field.1 = f32[2,625,1,512]{3,2,1,0:T(1,128)} custom-call(s32[3]{0:T(128)S(1)} %pad_add_fusion.refs_0_, f32[2,640,256]{2,1,0:T(8,128)S(1)} %field_without_inflow.2.refs_1_, f32[2,640,256]{2,1,0:T(8,128)S(1)} %field_without_inflow.3.refs_2_, f32[128,256]{1,0:T(8,128)S(1)} %get-tuple-element.64.refs_3_, f32[128,256]{1,0:T(8,128)S(1)} %collective-permute-done.15.refs_4_, ...), custom_call_target="tpu_custom_call" | custom-call | flops 1000000000 | tf_op jit(solution)/shard_map/whole_field/pallas_call | solution.py:68
  (5 shorter events, 0.0 us)
Async XLA Ops:
  0.1 1.7 %copy-start.9 = (f32[2,1,625,512]{3,1,2,0:T(1,128)S(1)}, f32[2,1,625,512]{3,1,2,0:T(1,128)}, u32[]{:S(2)}) copy-start(f32[2,1,625,512]{3,1,2,0:T(1,128)} %param.7) | copy-start | bytes 7680004
  2.8 6.6 %copy-start.5 = (f32[2,25,5,1,256]{4,3,2,1,0:T(1,128)}, f32[2,25,5,1,256]{4,3,2,1,0:T(1,128)S(1)}, u32[]{:S(2)}) copy-start(f32[2,25,5,1,256]{4,3,2,1,0:T(1,128)S(1)} %get-tuple-element.39.refs_7_) | copy-start | bytes 768004
  2.8 6.6 %copy-start.6 = (f32[2,25,5,1,256]{4,3,2,1,0:T(1,128)}, f32[2,25,5,1,256]{4,3,2,1,0:T(1,128)S(1)}, u32[]{:S(2)}) copy-start(f32[2,25,5,1,256]{4,3,2,1,0:T(1,128)S(1)} %get-tuple-element.40.refs_8_) | copy-start | bytes 768004
  2.8 6.6 %copy-start.7 = (f32[2,25,5,1,256]{4,3,2,1,0:T(1,128)}, f32[2,25,5,1,256]{4,3,2,1,0:T(1,128)S(1)}, u32[]{:S(2)}) copy-start(f32[2,25,5,1,256]{4,3,2,1,0:T(1,128)S(1)} %get-tuple-element.38.refs_6_) | copy-start | bytes 768004
  2.8 6.6 %copy-start.8 = (f32[2,25,5,1,256]{4,3,2,1,0:T(1,128)}, f32[2,25,5,1,256]{4,3,2,1,0:T(1,128)S(1)}, u32[]{:S(2)}) copy-start(f32[2,25,5,1,256]{4,3,2,1,0:T(1,128)S(1)} %get-tuple-element.37.refs_5_) | copy-start | bytes 768004
  2.8 25.6 %collective-permute-start.1 = (f32[2,125,1,256]{3,2,1,0:T(1,128)S(1)}, f32[2,125,1,256]{3,2,1,0:T(1,128)S(1)}, u32[]{:S(2)}, u32[]{:S(2)}) collective-permute-start(f32[2,125,1,256]{3,2,1,0:T(1,128)S(1)} %bitcast.36), channel_id=1, source_target_pairs={{0,1},{1,0},{2,3},{3,2},{4,5},{5,4},{6,7},{7,6},{8,9},{9,8},{10,11... | collective-permute-start | bytes 768008 | tf_op jit(solution)/shard_map/ppermute | solution.py:443
  5.0 24.6 %collective-permute-start.2 = (f32[2,125,1,256]{3,2,1,0:T(1,128)S(1)}, f32[2,125,1,256]{3,2,1,0:T(1,128)S(1)}, u32[]{:S(2)}, u32[]{:S(2)}) collective-permute-start(f32[2,125,1,256]{3,2,1,0:T(1,128)S(1)} %bitcast.35), channel_id=1, source_target_pairs={{0,3},{1,2},{2,1},{3,0},{4,7},{5,6},{6,5},{7,4},{8,11},{9,10},{10,... | collective-permute-start | bytes 768008 | tf_op jit(solution)/shard_map/ppermute | solution.py:443
  7.2 22.4 %collective-permute-start.3 = (f32[2,125,1,256]{3,2,1,0:T(1,128)S(1)}, f32[2,125,1,256]{3,2,1,0:T(1,128)S(1)}, u32[]{:S(2)}, u32[]{:S(2)}) collective-permute-start(f32[2,125,1,256]{3,2,1,0:T(1,128)S(1)} %bitcast.34), channel_id=1, source_target_pairs={{0,7},{1,6},{2,5},{3,4},{4,3},{5,2},{6,1},{7,0},{8,15},{9,14},{10,... | collective-permute-start | bytes 768008 | tf_op jit(solution)/shard_map/ppermute | solution.py:443
  9.4 21.4 %collective-permute-start = (f32[2,125,1,256]{3,2,1,0:T(1,128)S(1)}, f32[2,125,1,256]{3,2,1,0:T(1,128)S(1)}, u32[]{:S(2)}, u32[]{:S(2)}) collective-permute-start(f32[2,125,1,256]{3,2,1,0:T(1,128)S(1)} %bitcast.33), channel_id=1, source_target_pairs={{0,5},{1,4},{2,7},{3,6},{4,1},{5,0},{6,3},{7,2},{8,13},{9,12},{10,... | collective-permute-start | bytes 768008 | tf_op jit(solution)/shard_map/ppermute | solution.py:443
  17.4 13.4 %copy-start.4 = (f32[2,1,625,125]{3,1,2,0:T(1,128)S(1)}, f32[2,1,625,125]{3,1,2,0:T(1,128)}, u32[]{:S(2)}) copy-start(f32[2,1,625,125]{3,1,2,0:T(1,128)} %param.11) | copy-start | bytes 1875004
  25.4 5.4 %copy-start.1 = (f32[2,1,625,512]{3,1,2,0:T(1,128)S(1)}, f32[2,1,625,512]{3,1,2,0:T(1,128)}, u32[]{:S(2)}) copy-start(f32[2,1,625,512]{3,1,2,0:T(1,128)} %param.6) | copy-start | bytes 7680004
  25.4 5.4 %copy-start.2 = (f32[2,1,625,125]{3,1,2,0:T(1,128)S(1)}, f32[2,1,625,125]{3,1,2,0:T(1,128)}, u32[]{:S(2)}) copy-start(f32[2,1,625,125]{3,1,2,0:T(1,128)} %param.9) | copy-start | bytes 1875004
  25.4 5.4 %copy-start.3 = (f32[2,1,625,125]{3,1,2,0:T(1,128)S(1)}, f32[2,1,625,125]{3,1,2,0:T(1,128)}, u32[]{:S(2)}) copy-start(f32[2,1,625,125]{3,1,2,0:T(1,128)} %param.10) | copy-start | bytes 1875004
  27.1 3.8 %copy-start = (f32[2,1,625,625]{3,1,2,0:T(1,128)S(1)}, f32[2,1,625,625]{3,1,2,0:T(1,128)}, u32[]{:S(2)}) copy-start(f32[2,1,625,625]{3,1,2,0:T(1,128)} %param.8) | copy-start | bytes 9375004
  27.1 7.8 %collective-permute-start.4 = (f32[128,128]{1,0:T(8,128)S(1)}, f32[128,128]{1,0:T(8,128)S(1)}, u32[]{:S(2)}, u32[]{:S(2)}) collective-permute-start(f32[128,128]{1,0:T(8,128)S(1)} %get-tuple-element.52), channel_id=1, source_target_pairs={{0,8},{4,12},{8,16},{12,20},{16,24},{20,28},{24,0},{28,4},{1,9},{5... | collective-permute-start | bytes 196616 | tf_op jit(solution)/shard_map/ppermute | solution.py:433
  28.4 6.5 %collective-permute-start.5 = (f32[128,128]{1,0:T(8,128)S(1)}, f32[128,128]{1,0:T(8,128)S(1)}, u32[]{:S(2)}, u32[]{:S(2)}) collective-permute-start(f32[128,128]{1,0:T(8,128)S(1)} %get-tuple-element.52), channel_id=1, source_target_pairs={{0,16},{4,20},{8,24},{12,28},{16,0},{20,4},{24,8},{28,12},{1,17},{... | collective-permute-start | bytes 196616 | tf_op jit(solution)/shard_map/ppermute | solution.py:433
  32.2 4.9 %collective-permute-start.6 = (f32[128,256]{1,0:T(8,128)S(1)}, f32[128,256]{1,0:T(8,128)S(1)}, u32[]{:S(2)}, u32[]{:S(2)}) collective-permute-start(f32[128,256]{1,0:T(8,128)S(1)} %get-tuple-element.54), channel_id=1, source_target_pairs={{0,8},{4,12},{8,16},{12,20},{16,24},{20,28},{24,0},{28,4},{1,9},{5... | collective-permute-start | bytes 393224 | tf_op jit(solution)/shard_map/ppermute | solution.py:433
  32.5 5.2 %collective-permute-start.7 = (f32[128,256]{1,0:T(8,128)S(1)}, f32[128,256]{1,0:T(8,128)S(1)}, u32[]{:S(2)}, u32[]{:S(2)}) collective-permute-start(f32[128,256]{1,0:T(8,128)S(1)} %get-tuple-element.54), channel_id=1, source_target_pairs={{0,16},{4,20},{8,24},{12,28},{16,0},{20,4},{24,8},{28,12},{1,17},{... | collective-permute-start | bytes 393224 | tf_op jit(solution)/shard_map/ppermute | solution.py:433
  33.7 4.0 %collective-permute-start.8 = (f32[128,256]{1,0:T(8,128)S(1)}, f32[128,256]{1,0:T(8,128)S(1)}, u32[]{:S(2)}, u32[]{:S(2)}) collective-permute-start(f32[128,256]{1,0:T(8,128)S(1)} %get-tuple-element.54), channel_id=1, source_target_pairs={{0,24},{4,28},{8,0},{12,4},{16,8},{20,12},{24,16},{28,20},{1,25},{... | collective-permute-start | bytes 393224 | tf_op jit(solution)/shard_map/ppermute | solution.py:433
  38.8 15.2 %collective-permute-start.10 = (f32[4,128,256]{2,1,0:T(8,128)S(1)}, f32[4,128,256]{2,1,0:T(8,128)S(1)}, u32[]{:S(2)}, u32[]{:S(2)}) collective-permute-start(f32[4,128,256]{2,1,0:T(8,128)S(1)} %get-tuple-element.56.refs_7_), channel_id=1, source_target_pairs={{0,3},{1,2},{2,1},{3,0},{4,7},{5,6},{6,5},{7,4},{8,11},{9,10},{10,... | collective-permute-start | bytes 1572872 | tf_op jit(solution)/shard_map/ppermute | solution.py:443
  41.1 21.8 %collective-permute-start.9 = (f32[4,128,256]{2,1,0:T(8,128)S(1)}, f32[4,128,256]{2,1,0:T(8,128)S(1)}, u32[]{:S(2)}, u32[]{:S(2)}) collective-permute-start(f32[4,128,256]{2,1,0:T(8,128)S(1)} %get-tuple-element.55.refs_6_), channel_id=1, source_target_pairs={{0,1},{1,0},{2,3},{3,2},{4,5},{5,4},{6,7},{7,6},{8,9},{9,8},{10,11... | collective-permute-start | bytes 1572872 | tf_op jit(solution)/shard_map/ppermute | solution.py:443
  63.9 10.8 %collective-permute-start.12 = (f32[128,256]{1,0:T(8,128)S(1)}, f32[128,256]{1,0:T(8,128)S(1)}, u32[]{:S(2)}, u32[]{:S(2)}) collective-permute-start(f32[128,256]{1,0:T(8,128)S(1)} %last_traces.2.refs_9_.refs_6_), channel_id=1, source_target_pairs={{0,8},{4,12},{8,16},{12,20},{16,24},{20,28},{24,0},{28,4},{1,9},{5... | collective-permute-start | bytes 393224 | tf_op jit(solution)/shard_map/ppermute | solution.py:433
  65.9 8.8 %collective-permute-start.13 = (f32[128,256]{1,0:T(8,128)S(1)}, f32[128,256]{1,0:T(8,128)S(1)}, u32[]{:S(2)}, u32[]{:S(2)}) collective-permute-start(f32[128,256]{1,0:T(8,128)S(1)} %last_traces.2.refs_9_.refs_6_), channel_id=1, source_target_pairs={{0,16},{4,20},{8,24},{12,28},{16,0},{20,4},{24,8},{28,12},{1,17},{... | collective-permute-start | bytes 393224 | tf_op jit(solution)/shard_map/ppermute | solution.py:433
  66.9 7.9 %collective-permute-start.14 = (f32[128,256]{1,0:T(8,128)S(1)}, f32[128,256]{1,0:T(8,128)S(1)}, u32[]{:S(2)}, u32[]{:S(2)}) collective-permute-start(f32[128,256]{1,0:T(8,128)S(1)} %last_traces.2.refs_9_.refs_6_), channel_id=1, source_target_pairs={{0,24},{4,28},{8,0},{12,4},{16,8},{20,12},{24,16},{28,20},{1,25},{... | collective-permute-start | bytes 393224 | tf_op jit(solution)/shard_map/ppermute | solution.py:433
  69.2 7.5 %collective-permute-start.11 = (f32[2,2,128,256]{3,2,1,0:T(8,128)S(1)}, f32[2,2,128,256]{3,2,1,0:T(8,128)S(1)}, u32[]{:S(2)}, u32[]{:S(2)}) collective-permute-start(f32[2,2,128,256]{3,2,1,0:T(8,128)S(1)} %get-tuple-element.62), channel_id=1, source_target_pairs={{0,4},{4,0},{8,12},{12,8},{16,20},{20,16},{24,28},{28,24},{1,5},{5... | collective-permute-start | bytes 1572872 | tf_op jit(solution)/shard_map/ppermute | solution.py:429
  75.6 2.7 %collective-permute-start.15 = (f32[128,256]{1,0:T(8,128)S(1)}, f32[128,256]{1,0:T(8,128)S(1)}, u32[]{:S(2)}, u32[]{:S(2)}) collective-permute-start(f32[128,256]{1,0:T(8,128)S(1)} %get-tuple-element.65), channel_id=1, source_target_pairs={{0,4},{4,0},{8,12},{12,8},{16,20},{20,16},{24,28},{28,24},{1,5},{5... | collective-permute-start | bytes 393224 | tf_op jit(solution)/shard_map/ppermute | solution.py:429

commit v7 on v6

--- a/solution.py
+++ b/solution.py
@@ -269,22 +269,30 @@
         faces_ref[e] = faces[WIDE:]
 
 
+def face_of(ref, e):
+    return padded(ref[e * FACE : (e + 1) * FACE, :], WIDE)
+
+
 def last_traces(rows, core_ref, const_ref, high_ref, low_ref, second_ref, first_ref, out_ref, *refs):
     halo_high, halo_low = refs[-2:]
-    count = first_ref.shape[0]
+    count = first_ref.shape[0] // FACE
     for e in range(count):
         for k, ref in enumerate((first_ref, second_ref)):
             at = pl.ds(pl.multiple_of(south_north(core_ref, k) + 2 * e * WIDE, WIDE), WIDE)
-            halo_high[at, :], halo_low[at, :] = split(ref[e])
+            halo_high[at, :], halo_low[at, :] = split(face_of(ref, e))
     out_ref[...] = traces(
         const_ref[rows, :], high_ref[rows, :], low_ref[rows, :], halo_high[...], halo_low[...]
     )
     if len(refs) > 2:
         elements = count // CORES
-        other = (1 - core_ref[0]) * elements
-        for e in range(elements):
-            refs[0][0, e] = first_ref[other + e]
-            refs[0][1, e] = second_ref[other + e]
+
+        def take(other):
+            for e in range(elements):
+                refs[0][0, e] = face_of(first_ref, other * elements + e)
+                refs[0][1, e] = face_of(second_ref, other * elements + e)
+
+        for k in range(CORES):
+            pl.when(core_ref[0] == k)(functools.partial(take, 1 - k))
 
 
 def through_chips(core_ref, inflow_ref, chips, steps):
@@ -310,8 +318,8 @@
     for e in range(faces_ref.shape[0]):
         both[e] = faces_ref[e] + stacked(resp_ref[e, WIDE:, :], inflow)
     for e in range(faces_ref.shape[0]):
-        first_ref[e] = both[e, pl.ds(first, WIDE), :]
-        second_ref[e] = both[e, pl.ds(second, WIDE), :]
+        first_ref[e * FACE : (e + 1) * FACE, :] = both[e, pl.ds(first, WIDE), :][:FACE]
+        second_ref[e * FACE : (e + 1) * FACE, :] = both[e, pl.ds(second, WIDE), :][:FACE]
 
 
 def inflow_of_cores(core_ref, lead_ref, resp_ref, *refs):
@@ -348,11 +356,19 @@
     first_ref, second_ref, p_ref, halo = refs[-4:]
     elements, half = p_ref.shape[0], p_ref.shape[2]
     c_refs, bsn_refs = refs[: elements + 1], refs[elements + 1 : 2 * elements + 2]
-    own = 0 if other else core_ref[0] * elements
     at = pl.ds(pl.multiple_of((1 - core_ref[0] if other else core_ref[0]) * half, half), half)
     for e in range(elements):
         for k, ref in enumerate((first_ref, second_ref)):
-            halo[pl.ds(south_north(core_ref, k), WIDE), :] = ref[own + e]
+            rows = pl.ds(south_north(core_ref, k), WIDE)
+            if other:
+                halo[rows, :] = ref[e]
+                continue
+
+            def take(own):
+                halo[rows, :] = face_of(ref, own * elements + e)
+
+            for c in range(CORES):
+                pl.when(core_ref[0] == c)(functools.partial(take, c))
         halos = right(halo[...])
 
         def place(c_ref, bsn_ref):
@@ -519,7 +535,7 @@
     )
     last = call(
         next_faces,
-        [(VMEM, (count, WIDE, half), f32)] * 2,
+        [(VMEM, (count * FACE, half), f32)] * 2,
         core, *held((faces, resp, *chips, *steps)),
         scratch=[VMEM((WIDE, half), f32), VMEM((count, 2 * WIDE, half), f32)],
         us=1,

time: 81.4 us -> 81.1 us (level)
  no operation moved by 1% of the time
where the time goes in v7:
time: 81.1 us; the launch traced here: 80.9 us
  Pallas kernels  36.2 us (45%)
  starting transfers between devices  24.4 us (30%)
  waiting for transfers between devices  9.95 us (12%)
  blocking collectives  8.03 us (10%)
  local copies, waits for them, and re-layouts  1.8 us (2%)
    pallas_call x14, Pallas kernels, call(): pl.pallas_call(body, out_shape=[jax.ShapeDtypeStruct(shape, kind) for _,...  36.2 us
    ppermute x6, starting transfers between devices, along_span(): return lax.ppermute(x, ('sweep', 'span'), pairs)  9.98 us
    ppermute x8, starting transfers between devices, from_chips(): lax.ppermute(x, 'sweep', ring('sweep', CORES * back))  9.33 us
    ppermute x6, waiting for transfers between devices, along_span(): return lax.ppermute(x, ('sweep', 'span'), pairs)  8.41 us
    all_to_all x1, blocking collectives, per_device(): lax.all_to_all(own, 'sweep', 0, 0, axis_index_groups=[[i, i + 1] for i in...  8.03 us
    ppermute x2, starting transfers between devices, swap(): return lax.ppermute(x, 'sweep', [(i, i ^ 1) for i in range(devices)])  5.08 us
    unnamed x20, local copies, waits for them, and re-layouts  1.77 us
  transfers between devices with their start and end apart: 16, of which 3 were waited for; matrix products, arithmetic and copies ran while one was open for 0% of the time, Pallas kernels for 37%

profile of v7, /device:TPU:1, one launch (start us, length us, event | category | flops | bytes accessed | tf_op | source)
XLA Modules:
  0.0 80.9 jit_solution(5564082223951956284)
XLA Ops:
  0.0 0.1 pad_add_fusion.refs_0_
  0.1 1.7 %copy-done.9 = f32[2,1,625,512]{3,1,2,0:T(1,128)S(1)} copy-done((f32[2,1,625,512]{3,1,2,0:T(1,128)S(1)}, f32[2,1,625,512]{3,1,2,0:T(1,128)}, u32[]{:S(2)}) %copy-start.9) | copy-done | bytes 2560024
  1.8 1.0 %start_faces.1 = (f32[2,25,5,1,256]{4,3,2,1,0:T(1,128)S(1)}, f32[2,25,5,1,256]{4,3,2,1,0:T(1,128)S(1)}, f32[2,25,5,1,256]{4,3,2,1,0:T(1,128)S(1)}, f32[2,25,5,1,256]{4,3,2,1,0:T(1,128)S(1)}) custom-call(s32[3]{0:T(128)S(1)} %pad_add_fusion.refs_0_, f32[2,25,25,1,512]{4,3,2,1,0:T(1,128)S(1)} %bitcast.37), custom_call_target="tpu_custom_call" | custom-call | flops 1000000000 | tf_op jit(solution)/shard_map/start_faces/pallas_call | solution.py:68
  2.8 0.0 copy-start.5
  2.8 0.0 copy-start.6
  2.8 0.0 copy-start.7
  2.8 0.0 copy-start.8
  2.8 2.2 %collective-permute-start.1 = (f32[2,125,1,256]{3,2,1,0:T(1,128)S(1)}, f32[2,125,1,256]{3,2,1,0:T(1,128)S(1)}, u32[]{:S(2)}, u32[]{:S(2)}) collective-permute-start(f32[2,125,1,256]{3,2,1,0:T(1,128)S(1)} %bitcast.36), channel_id=1, source_target_pairs={{0,1},{1,0},{2,3},{3,2},{4,5},{5,4},{6,7},{7,6},{8,9},{9,8},{10,11... | collective-permute-start | bytes 768008 | tf_op jit(solution)/shard_map/ppermute | solution.py:459
  5.0 2.2 %collective-permute-start.2 = (f32[2,125,1,256]{3,2,1,0:T(1,128)S(1)}, f32[2,125,1,256]{3,2,1,0:T(1,128)S(1)}, u32[]{:S(2)}, u32[]{:S(2)}) collective-permute-start(f32[2,125,1,256]{3,2,1,0:T(1,128)S(1)} %bitcast.35), channel_id=1, source_target_pairs={{0,3},{1,2},{2,1},{3,0},{4,7},{5,6},{6,5},{7,4},{8,11},{9,10},{10,... | collective-permute-start | bytes 768008 | tf_op jit(solution)/shard_map/ppermute | solution.py:459
  7.2 2.2 %collective-permute-start.3 = (f32[2,125,1,256]{3,2,1,0:T(1,128)S(1)}, f32[2,125,1,256]{3,2,1,0:T(1,128)S(1)}, u32[]{:S(2)}, u32[]{:S(2)}) collective-permute-start(f32[2,125,1,256]{3,2,1,0:T(1,128)S(1)} %bitcast.34), channel_id=1, source_target_pairs={{0,7},{1,6},{2,5},{3,4},{4,3},{5,2},{6,1},{7,0},{8,15},{9,14},{10,... | collective-permute-start | bytes 768008 | tf_op jit(solution)/shard_map/ppermute | solution.py:459
  9.4 0.0 collective-permute-start
  9.4 0.0 copy-done.5
  9.4 0.0 copy-done.6
  9.4 0.0 copy-done.7
  9.4 0.0 copy-done.8
  9.4 7.9 %fold_faces.1 = f32[2,2,384,640]{3,2,1,0:T(8,128)} custom-call(f32[2,625,1,625]{3,2,1,0:T(1,128)} %bitcast.18, f32[2,625,1,512]{3,2,1,0:T(1,128)} %bitcast.21, f32[2,625,1,125]{3,2,1,0:T(1,128)} %bitcast.24, f32[2,625,1,125]{3,2,1,0:T(1,128)} %bitcast.27, f32[2,625,1,125]{3,2,1,0:T(1,128)} %bitcast.30, f32[2,25,5,1,256]{4,3,2,1,0:T(1,128)} %copy-done.8, ...), custom_call_target="tpu_custom_call" | custom-call | tf_op jit(solution)/shard_map/fold_faces/pallas_call | solution.py:68
  17.4 0.0 copy-start.4
  17.4 8.0 %all_to_all.5.refs_0_ = f32[2,2,384,640]{3,2,1,0:T(8,128)S(1)} all-to-all(f32[2,2,384,640]{3,2,1,0:T(8,128)} %fold_faces.1), channel_id=1, replica_groups={{0,4},{8,12},{16,20},{24,28},{1,5},{9,13},{17,21},{25,29},{2,6},{10,14}..., dimensions={0} | all-to-all | bytes 7864320 | tf_op jit(solution)/shard_map/all_to_all | solution.py:485
  25.4 1.7 %chip_blocks.1 = (f32[4,384,256]{2,1,0:T(8,128)S(1)}, bf16[4,384,768]{2,1,0:T(8,128)(2,1)S(1)}, bf16[4,384,384]{2,1,0:T(8,128)(2,1)S(1)}, bf16[4,384,384]{2,1,0:...) custom-call(f32[2,2,384,640]{3,2,1,0:T(8,128)S(1)} %all_to_all.5.refs_0_), custom_call_target="tpu_custom_call" | custom-call | tf_op jit(solution)/shard_map/chip_blocks/pallas_call | solution.py:68
  27.1 0.0 copy-start
  27.1 1.3 %collective-permute-start.4 = (f32[128,128]{1,0:T(8,128)S(1)}, f32[128,128]{1,0:T(8,128)S(1)}, u32[]{:S(2)}, u32[]{:S(2)}) collective-permute-start(f32[128,128]{1,0:T(8,128)S(1)} %get-tuple-element.52), channel_id=1, source_target_pairs={{0,8},{4,12},{8,16},{12,20},{16,24},{20,28},{24,0},{28,4},{1,9},{5... | collective-permute-start | bytes 196616 | tf_op jit(solution)/shard_map/ppermute | solution.py:449
  28.4 0.0 collective-permute-done.1.refs_1_
  28.4 1.2 %collective-permute-start.5 = (f32[128,128]{1,0:T(8,128)S(1)}, f32[128,128]{1,0:T(8,128)S(1)}, u32[]{:S(2)}, u32[]{:S(2)}) collective-permute-start(f32[128,128]{1,0:T(8,128)S(1)} %get-tuple-element.52), channel_id=1, source_target_pairs={{0,16},{4,20},{8,24},{12,28},{16,0},{20,4},{24,8},{28,12},{1,17},{... | collective-permute-start | bytes 196616 | tf_op jit(solution)/shard_map/ppermute | solution.py:449
  29.6 0.0 collective-permute-done.2.refs_2_
  29.6 0.0 collective-permute-done.3.refs_3_
  29.6 1.2 %early_halos.1 = (bf16[1024,256]{1,0:T(8,128)(2,1)S(1)}, bf16[1024,256]{1,0:T(8,128)(2,1)S(1)}) custom-call(s32[3]{0:T(128)S(1)} %pad_add_fusion.refs_0_, f32[2,125,1,256]{3,2,1,0:T(1,128)S(1)} %collective-permute-done.1.refs_1_, f32[2,125,1,256]{3,2,1,0:T(1,128)S(1)} %collective-permute-done.2.refs_2_, f32[2,125,1,256]{3,2,1,0:T(1,128)S(1)} %collective-permute-done.3.refs_3_), custom_call_target="tpu_custom_call" | custom-call | flops 1000000000 | tf_op jit(solution)/shard_map/early_halos/pallas_call | solution.py:68
  30.8 0.0 collective-permute-done.refs_4_
  30.8 0.0 copy-done.4
  30.8 0.0 copy-done.1
  30.8 0.0 copy-done.2
  30.8 0.0 copy-done.3
  30.8 0.0 copy-done
  30.9 1.4 %first_traces.1 = (bf16[1024,256]{1,0:T(8,128)(2,1)S(1)}, bf16[1024,256]{1,0:T(8,128)(2,1)S(1)}, f32[128,256]{1,0:T(8,128)S(1)}, f32[640,512]{1,0:T(8,128)S(1)},...) custom-call(s32[3]{0:T(128)S(1)} %pad_add_fusion.refs_0_, ...), custom_call_target="tpu_custom_call", output_to_operand_aliasing={{0}: (10, {}), {1}: (11, {})} | custom-call | flops 2000000000 | tf_op jit(solution)/shard_map/first_traces/pallas_call | solution.py:68
  32.2 0.3 collective-permute-start.6
  32.5 1.2 %collective-permute-start.7 = (f32[128,256]{1,0:T(8,128)S(1)}, f32[128,256]{1,0:T(8,128)S(1)}, u32[]{:S(2)}, u32[]{:S(2)}) collective-permute-start(f32[128,256]{1,0:T(8,128)S(1)} %get-tuple-element.54), channel_id=1, source_target_pairs={{0,16},{4,20},{8,24},{12,28},{16,0},{20,4},{24,8},{28,12},{1,17},{... | collective-permute-start | bytes 393224 | tf_op jit(solution)/shard_map/ppermute | solution.py:449
  33.7 1.2 %collective-permute-start.8 = (f32[128,256]{1,0:T(8,128)S(1)}, f32[128,256]{1,0:T(8,128)S(1)}, u32[]{:S(2)}, u32[]{:S(2)}) collective-permute-start(f32[128,256]{1,0:T(8,128)S(1)} %get-tuple-element.54), channel_id=1, source_target_pairs={{0,24},{4,28},{8,0},{12,4},{16,8},{20,12},{24,16},{28,20},{1,25},{... | collective-permute-start | bytes 393224 | tf_op jit(solution)/shard_map/ppermute | solution.py:449
  34.9 0.0 collective-permute-done.4.refs_5_.refs_6_
  34.9 0.0 collective-permute-done.5.refs_6_.refs_7_
  34.9 1.3 %other_faces.1.refs_1_ = f32[4,256,256]{2,1,0:T(8,128)S(1)} custom-call(f32[4,384,256]{2,1,0:T(8,128)S(1)} %get-tuple-element.47.refs_0_, bf16[4,384,768]{2,1,0:T(8,128)(2,1)S(1)} %get-tuple-element.48.refs_1_, bf16[4,384,384]{2,1,0:T(8,128)(2,1)S(1)} %get-tuple-element.49.refs_2_, bf16[1024,256]{1,0:T(8,128)(2,1)S(1)} %get-tuple-element.50.refs_3_, ...), custom_call_target="tpu_custom_call" | custom-call | flops 2000000000 | tf_op jit(solution)/shard_map/other_faces/pallas_call | solution.py:68
  36.2 0.9 %collective-permute-done.6.refs_3_ = f32[128,256]{1,0:T(8,128)S(1)} collective-permute-done((f32[128,256]{1,0:T(8,128)S(1)}, f32[128,256]{1,0:T(8,128)S(1)}, u32[]{:S(2)}, u32[]{:S(2)}) %collective-permute-start.6) | collective-permute-done | bytes 131104 | tf_op jit(solution)/shard_map/ppermute | solution.py:449
  37.1 0.6 collective-permute-done.7.refs_4_
  37.7 0.0 collective-permute-done.8.refs_5_
  37.7 1.1 %next_faces.1 = (f32[500,256]{1,0:T(8,128)S(1)}, f32[500,256]{1,0:T(8,128)S(1)}) custom-call(s32[3]{0:T(128)S(1)} %pad_add_fusion.refs_0_, f32[4,256,256]{2,1,0:T(8,128)S(1)} %other_faces.1.refs_1_, bf16[4,384,384]{2,1,0:T(8,128)(2,1)S(1)} %get-tuple-element.53.refs_2_, f32[128,256]{1,0:T(8,128)S(1)} %collective-permute-done.6.refs_3_, ...), custom_call_target="tpu_custom_call" | custom-call | flops 1000000000 | tf_op jit(solution)/shard_map/next_faces/pallas_call | solution.py:68
  38.8 2.3 %collective-permute-start.10 = (f32[500,256]{1,0:T(8,128)S(1)}, f32[500,256]{1,0:T(8,128)S(1)}, u32[]{:S(2)}, u32[]{:S(2)}) collective-permute-start(f32[500,256]{1,0:T(8,128)S(1)} %get-tuple-element.56.refs_7_), channel_id=1, source_target_pairs={{0,3},{1,2},{2,1},{3,0},{4,7},{5,6},{6,5},{7,4},{8,11},{9,10},{10,... | collective-permute-start | bytes 1536008 | tf_op jit(solution)/shard_map/ppermute | solution.py:459
  41.1 1.1 %collective-permute-start.9 = (f32[500,256]{1,0:T(8,128)S(1)}, f32[500,256]{1,0:T(8,128)S(1)}, u32[]{:S(2)}, u32[]{:S(2)}) collective-permute-start(f32[500,256]{1,0:T(8,128)S(1)} %get-tuple-element.55.refs_6_), channel_id=1, source_target_pairs={{0,1},{1,0},{2,3},{3,2},{4,5},{5,4},{6,7},{7,6},{8,9},{9,8},{10,11... | collective-permute-start | bytes 1536008 | tf_op jit(solution)/shard_map/ppermute | solution.py:459
  42.2 11.7 %fold_rest.1 = (f32[640,512]{1,0:T(8,128)S(1)}, bf16[640,768]{1,0:T(8,128)(2,1)S(1)}, bf16[640,384]{1,0:T(8,128)(2,1)S(1)}, f32[640,512]{1,0:T(8,128)S(1)}, bf16...) custom-call(s32[3]{0:T(128)S(1)} %pad_add_fusion.refs_0_, f32[2,625,1,625]{3,2,1,0:T(1,128)S(1)} %bitcast.20, ...), custom_call_target="tpu_custom_call" | custom-call | flops 10000000000 | tf_op jit(solution)/shard_map/fold_rest/pallas_call | solution.py:68
  54.0 0.0 collective-permute-done.10.refs_4_.refs_8_
  54.0 8.4 %collective-permute-done.9.refs_5_.refs_7_ = f32[500,256]{1,0:T(8,128)S(1)} collective-permute-done((f32[500,256]{1,0:T(8,128)S(1)}, f32[500,256]{1,0:T(8,128)S(1)}, u32[]{:S(2)}, u32[]{:S(2)}) %collective-permute-start.9) | collective-permute-done | bytes 512032 | tf_op jit(solution)/shard_map/ppermute | solution.py:459
  62.4 1.2 %last_traces.2.refs_9_.refs_6_ = f32[128,256]{1,0:T(8,128)S(1)} custom-call(s32[3]{0:T(128)S(1)} %pad_add_fusion.refs_0_, f32[256,256]{1,0:T(8,128)S(1)} %get-tuple-element.41.refs_1_, bf16[256,1024]{1,0:T(8,128)(2,1)S(1)} %get-tuple-element.42.refs_2_, bf16[256,1024]{1,0:T(8,128)(2,1)S(1)} %get-tuple-element.43.refs_3_, ...), custom_call_target="tpu_custom_call" | custom-call | flops 1000000000 | tf_op jit(solution)/shard_map/last_traces/pallas_call | solution.py:68
  63.5 2.0 %collective-permute-start.12 = (f32[128,256]{1,0:T(8,128)S(1)}, f32[128,256]{1,0:T(8,128)S(1)}, u32[]{:S(2)}, u32[]{:S(2)}) collective-permute-start(f32[128,256]{1,0:T(8,128)S(1)} %last_traces.2.refs_9_.refs_6_), channel_id=1, source_target_pairs={{0,8},{4,12},{8,16},{12,20},{16,24},{20,28},{24,0},{28,4},{1,9},{5... | collective-permute-start | bytes 393224 | tf_op jit(solution)/shard_map/ppermute | solution.py:449
  65.6 1.0 %collective-permute-start.13 = (f32[128,256]{1,0:T(8,128)S(1)}, f32[128,256]{1,0:T(8,128)S(1)}, u32[]{:S(2)}, u32[]{:S(2)}) collective-permute-start(f32[128,256]{1,0:T(8,128)S(1)} %last_traces.2.refs_9_.refs_6_), channel_id=1, source_target_pairs={{0,16},{4,20},{8,24},{12,28},{16,0},{20,4},{24,8},{28,12},{1,17},{... | collective-permute-start | bytes 393224 | tf_op jit(solution)/shard_map/ppermute | solution.py:449
  66.5 1.2 %collective-permute-start.14 = (f32[128,256]{1,0:T(8,128)S(1)}, f32[128,256]{1,0:T(8,128)S(1)}, u32[]{:S(2)}, u32[]{:S(2)}) collective-permute-start(f32[128,256]{1,0:T(8,128)S(1)} %last_traces.2.refs_9_.refs_6_), channel_id=1, source_target_pairs={{0,24},{4,28},{8,0},{12,4},{16,8},{20,12},{24,16},{28,20},{1,25},{... | collective-permute-start | bytes 393224 | tf_op jit(solution)/shard_map/ppermute | solution.py:449
  67.7 1.2 %last_traces.3 = (f32[128,256]{1,0:T(8,128)S(1)}, f32[2,2,128,256]{3,2,1,0:T(8,128)S(1)}) custom-call(s32[3]{0:T(128)S(1)} %pad_add_fusion.refs_0_, f32[256,256]{1,0:T(8,128)S(1)} %get-tuple-element.41.refs_1_, bf16[256,1024]{1,0:T(8,128)(2,1)S(1)} %get-tuple-element.42.refs_2_, bf16[256,1024]{1,0:T(8,128)(2,1)S(1)} %get-tuple-element.43.refs_3_, ...), custom_call_target="tpu_custom_call" | custom-call | tf_op jit(solution)/shard_map/last_traces/pallas_call | solution.py:68
  68.9 4.1 %collective-permute-start.11 = (f32[2,2,128,256]{3,2,1,0:T(8,128)S(1)}, f32[2,2,128,256]{3,2,1,0:T(8,128)S(1)}, u32[]{:S(2)}, u32[]{:S(2)}) collective-permute-start(f32[2,2,128,256]{3,2,1,0:T(8,128)S(1)} %get-tuple-element.62), channel_id=1, source_target_pairs={{0,4},{4,0},{8,12},{12,8},{16,20},{20,16},{24,28},{28,24},{1,5},{5... | collective-permute-start | bytes 1572872 | tf_op jit(solution)/shard_map/ppermute | solution.py:445
  73.1 1.6 %field_without_inflow.2.refs_1_ = f32[2,640,256]{2,1,0:T(8,128)S(1)} custom-call(s32[3]{0:T(128)S(1)} %pad_add_fusion.refs_0_, f32[640,512]{1,0:T(8,128)S(1)} %get-tuple-element.46.refs_1_, f32[640,512]{1,0:T(8,128)S(1)} %get-tuple-element.57.refs_6_.refs_2_, f32[640,512]{1,0:T(8,128)S(1)} %get-tuple-element.58.refs_3_, ...), custom_call_target="tpu_custom_call" | custom-call | tf_op jit(solution)/shard_map/field_without_inflow/pallas_call | solution.py:68
  74.6 0.0 collective-permute-done.12.refs_3_
  74.6 0.0 collective-permute-done.13.refs_4_
  74.7 0.0 collective-permute-done.14.refs_5_
  74.7 0.8 inflow_of_cores.1
  75.4 1.0 %collective-permute-start.15 = (f32[128,256]{1,0:T(8,128)S(1)}, f32[128,256]{1,0:T(8,128)S(1)}, u32[]{:S(2)}, u32[]{:S(2)}) collective-permute-start(f32[128,256]{1,0:T(8,128)S(1)} %get-tuple-element.65), channel_id=1, source_target_pairs={{0,4},{4,0},{8,12},{12,8},{16,20},{20,16},{24,28},{28,24},{1,5},{5... | collective-permute-start | bytes 393224 | tf_op jit(solution)/shard_map/ppermute | solution.py:445
  76.4 0.0 collective-permute-done.11
  76.4 1.5 %field_without_inflow.3.refs_2_ = f32[2,640,256]{2,1,0:T(8,128)S(1)} custom-call(s32[3]{0:T(128)S(1)} %pad_add_fusion.refs_0_, f32[640,512]{1,0:T(8,128)S(1)} %get-tuple-element.46.refs_1_, f32[640,512]{1,0:T(8,128)S(1)} %get-tuple-element.57.refs_6_.refs_2_, f32[640,512]{1,0:T(8,128)S(1)} %get-tuple-element.58.refs_3_, ...), custom_call_target="tpu_custom_call" | custom-call | tf_op jit(solution)/shard_map/field_without_inflow/pallas_call | solution.py:68
  77.9 0.0 collective-permute-done.15.refs_4_
  77.9 2.7 %whole_field.1 = f32[2,625,1,512]{3,2,1,0:T(1,128)} custom-call(s32[3]{0:T(128)S(1)} %pad_add_fusion.refs_0_, f32[2,640,256]{2,1,0:T(8,128)S(1)} %field_without_inflow.2.refs_1_, f32[2,640,256]{2,1,0:T(8,128)S(1)} %field_without_inflow.3.refs_2_, f32[128,256]{1,0:T(8,128)S(1)} %get-tuple-element.64.refs_3_, f32[128,256]{1,0:T(8,128)S(1)} %collective-permute-done.15.refs_4_, ...), custom_call_target="tpu_custom_call" | custom-call | flops 1000000000 | tf_op jit(solution)/shard_map/whole_field/pallas_call | solution.py:68
  (5 shorter events, 0.0 us)
Async XLA Ops:
  0.1 1.7 %copy-start.9 = (f32[2,1,625,512]{3,1,2,0:T(1,128)S(1)}, f32[2,1,625,512]{3,1,2,0:T(1,128)}, u32[]{:S(2)}) copy-start(f32[2,1,625,512]{3,1,2,0:T(1,128)} %param.7) | copy-start | bytes 7680004
  2.8 6.6 %copy-start.5 = (f32[2,25,5,1,256]{4,3,2,1,0:T(1,128)}, f32[2,25,5,1,256]{4,3,2,1,0:T(1,128)S(1)}, u32[]{:S(2)}) copy-start(f32[2,25,5,1,256]{4,3,2,1,0:T(1,128)S(1)} %get-tuple-element.39.refs_7_) | copy-start | bytes 768004
  2.8 6.6 %copy-start.6 = (f32[2,25,5,1,256]{4,3,2,1,0:T(1,128)}, f32[2,25,5,1,256]{4,3,2,1,0:T(1,128)S(1)}, u32[]{:S(2)}) copy-start(f32[2,25,5,1,256]{4,3,2,1,0:T(1,128)S(1)} %get-tuple-element.40.refs_8_) | copy-start | bytes 768004
  2.8 6.6 %copy-start.7 = (f32[2,25,5,1,256]{4,3,2,1,0:T(1,128)}, f32[2,25,5,1,256]{4,3,2,1,0:T(1,128)S(1)}, u32[]{:S(2)}) copy-start(f32[2,25,5,1,256]{4,3,2,1,0:T(1,128)S(1)} %get-tuple-element.38.refs_6_) | copy-start | bytes 768004
  2.8 6.6 %copy-start.8 = (f32[2,25,5,1,256]{4,3,2,1,0:T(1,128)}, f32[2,25,5,1,256]{4,3,2,1,0:T(1,128)S(1)}, u32[]{:S(2)}) copy-start(f32[2,25,5,1,256]{4,3,2,1,0:T(1,128)S(1)} %get-tuple-element.37.refs_5_) | copy-start | bytes 768004
  2.8 25.6 %collective-permute-start.1 = (f32[2,125,1,256]{3,2,1,0:T(1,128)S(1)}, f32[2,125,1,256]{3,2,1,0:T(1,128)S(1)}, u32[]{:S(2)}, u32[]{:S(2)}) collective-permute-start(f32[2,125,1,256]{3,2,1,0:T(1,128)S(1)} %bitcast.36), channel_id=1, source_target_pairs={{0,1},{1,0},{2,3},{3,2},{4,5},{5,4},{6,7},{7,6},{8,9},{9,8},{10,11... | collective-permute-start | bytes 768008 | tf_op jit(solution)/shard_map/ppermute | solution.py:459
  5.0 24.6 %collective-permute-start.2 = (f32[2,125,1,256]{3,2,1,0:T(1,128)S(1)}, f32[2,125,1,256]{3,2,1,0:T(1,128)S(1)}, u32[]{:S(2)}, u32[]{:S(2)}) collective-permute-start(f32[2,125,1,256]{3,2,1,0:T(1,128)S(1)} %bitcast.35), channel_id=1, source_target_pairs={{0,3},{1,2},{2,1},{3,0},{4,7},{5,6},{6,5},{7,4},{8,11},{9,10},{10,... | collective-permute-start | bytes 768008 | tf_op jit(solution)/shard_map/ppermute | solution.py:459
  7.2 22.4 %collective-permute-start.3 = (f32[2,125,1,256]{3,2,1,0:T(1,128)S(1)}, f32[2,125,1,256]{3,2,1,0:T(1,128)S(1)}, u32[]{:S(2)}, u32[]{:S(2)}) collective-permute-start(f32[2,125,1,256]{3,2,1,0:T(1,128)S(1)} %bitcast.34), channel_id=1, source_target_pairs={{0,7},{1,6},{2,5},{3,4},{4,3},{5,2},{6,1},{7,0},{8,15},{9,14},{10,... | collective-permute-start | bytes 768008 | tf_op jit(solution)/shard_map/ppermute | solution.py:459
  9.4 21.4 %collective-permute-start = (f32[2,125,1,256]{3,2,1,0:T(1,128)S(1)}, f32[2,125,1,256]{3,2,1,0:T(1,128)S(1)}, u32[]{:S(2)}, u32[]{:S(2)}) collective-permute-start(f32[2,125,1,256]{3,2,1,0:T(1,128)S(1)} %bitcast.33), channel_id=1, source_target_pairs={{0,5},{1,4},{2,7},{3,6},{4,1},{5,0},{6,3},{7,2},{8,13},{9,12},{10,... | collective-permute-start | bytes 768008 | tf_op jit(solution)/shard_map/ppermute | solution.py:459
  17.4 13.4 %copy-start.4 = (f32[2,1,625,125]{3,1,2,0:T(1,128)S(1)}, f32[2,1,625,125]{3,1,2,0:T(1,128)}, u32[]{:S(2)}) copy-start(f32[2,1,625,125]{3,1,2,0:T(1,128)} %param.11) | copy-start | bytes 1875004
  25.4 5.4 %copy-start.1 = (f32[2,1,625,512]{3,1,2,0:T(1,128)S(1)}, f32[2,1,625,512]{3,1,2,0:T(1,128)}, u32[]{:S(2)}) copy-start(f32[2,1,625,512]{3,1,2,0:T(1,128)} %param.6) | copy-start | bytes 7680004
  25.4 5.4 %copy-start.2 = (f32[2,1,625,125]{3,1,2,0:T(1,128)S(1)}, f32[2,1,625,125]{3,1,2,0:T(1,128)}, u32[]{:S(2)}) copy-start(f32[2,1,625,125]{3,1,2,0:T(1,128)} %param.9) | copy-start | bytes 1875004
  25.4 5.4 %copy-start.3 = (f32[2,1,625,125]{3,1,2,0:T(1,128)S(1)}, f32[2,1,625,125]{3,1,2,0:T(1,128)}, u32[]{:S(2)}) copy-start(f32[2,1,625,125]{3,1,2,0:T(1,128)} %param.10) | copy-start | bytes 1875004
  27.1 3.8 %copy-start = (f32[2,1,625,625]{3,1,2,0:T(1,128)S(1)}, f32[2,1,625,625]{3,1,2,0:T(1,128)}, u32[]{:S(2)}) copy-start(f32[2,1,625,625]{3,1,2,0:T(1,128)} %param.8) | copy-start | bytes 9375004
  27.1 7.8 %collective-permute-start.4 = (f32[128,128]{1,0:T(8,128)S(1)}, f32[128,128]{1,0:T(8,128)S(1)}, u32[]{:S(2)}, u32[]{:S(2)}) collective-permute-start(f32[128,128]{1,0:T(8,128)S(1)} %get-tuple-element.52), channel_id=1, source_target_pairs={{0,8},{4,12},{8,16},{12,20},{16,24},{20,28},{24,0},{28,4},{1,9},{5... | collective-permute-start | bytes 196616 | tf_op jit(solution)/shard_map/ppermute | solution.py:449
  28.4 6.5 %collective-permute-start.5 = (f32[128,128]{1,0:T(8,128)S(1)}, f32[128,128]{1,0:T(8,128)S(1)}, u32[]{:S(2)}, u32[]{:S(2)}) collective-permute-start(f32[128,128]{1,0:T(8,128)S(1)} %get-tuple-element.52), channel_id=1, source_target_pairs={{0,16},{4,20},{8,24},{12,28},{16,0},{20,4},{24,8},{28,12},{1,17},{... | collective-permute-start | bytes 196616 | tf_op jit(solution)/shard_map/ppermute | solution.py:449
  32.2 4.9 %collective-permute-start.6 = (f32[128,256]{1,0:T(8,128)S(1)}, f32[128,256]{1,0:T(8,128)S(1)}, u32[]{:S(2)}, u32[]{:S(2)}) collective-permute-start(f32[128,256]{1,0:T(8,128)S(1)} %get-tuple-element.54), channel_id=1, source_target_pairs={{0,8},{4,12},{8,16},{12,20},{16,24},{20,28},{24,0},{28,4},{1,9},{5... | collective-permute-start | bytes 393224 | tf_op jit(solution)/shard_map/ppermute | solution.py:449
  32.5 5.2 %collective-permute-start.7 = (f32[128,256]{1,0:T(8,128)S(1)}, f32[128,256]{1,0:T(8,128)S(1)}, u32[]{:S(2)}, u32[]{:S(2)}) collective-permute-start(f32[128,256]{1,0:T(8,128)S(1)} %get-tuple-element.54), channel_id=1, source_target_pairs={{0,16},{4,20},{8,24},{12,28},{16,0},{20,4},{24,8},{28,12},{1,17},{... | collective-permute-start | bytes 393224 | tf_op jit(solution)/shard_map/ppermute | solution.py:449
  33.7 4.0 %collective-permute-start.8 = (f32[128,256]{1,0:T(8,128)S(1)}, f32[128,256]{1,0:T(8,128)S(1)}, u32[]{:S(2)}, u32[]{:S(2)}) collective-permute-start(f32[128,256]{1,0:T(8,128)S(1)} %get-tuple-element.54), channel_id=1, source_target_pairs={{0,24},{4,28},{8,0},{12,4},{16,8},{20,12},{24,16},{28,20},{1,25},{... | collective-permute-start | bytes 393224 | tf_op jit(solution)/shard_map/ppermute | solution.py:449
  38.8 15.2 %collective-permute-start.10 = (f32[500,256]{1,0:T(8,128)S(1)}, f32[500,256]{1,0:T(8,128)S(1)}, u32[]{:S(2)}, u32[]{:S(2)}) collective-permute-start(f32[500,256]{1,0:T(8,128)S(1)} %get-tuple-element.56.refs_7_), channel_id=1, source_target_pairs={{0,3},{1,2},{2,1},{3,0},{4,7},{5,6},{6,5},{7,4},{8,11},{9,10},{10,... | collective-permute-start | bytes 1536008 | tf_op jit(solution)/shard_map/ppermute | solution.py:459
  41.1 21.3 %collective-permute-start.9 = (f32[500,256]{1,0:T(8,128)S(1)}, f32[500,256]{1,0:T(8,128)S(1)}, u32[]{:S(2)}, u32[]{:S(2)}) collective-permute-start(f32[500,256]{1,0:T(8,128)S(1)} %get-tuple-element.55.refs_6_), channel_id=1, source_target_pairs={{0,1},{1,0},{2,3},{3,2},{4,5},{5,4},{6,7},{7,6},{8,9},{9,8},{10,11... | collective-permute-start | bytes 1536008 | tf_op jit(solution)/shard_map/ppermute | solution.py:459
  63.5 11.1 %collective-permute-start.12 = (f32[128,256]{1,0:T(8,128)S(1)}, f32[128,256]{1,0:T(8,128)S(1)}, u32[]{:S(2)}, u32[]{:S(2)}) collective-permute-start(f32[128,256]{1,0:T(8,128)S(1)} %last_traces.2.refs_9_.refs_6_), channel_id=1, source_target_pairs={{0,8},{4,12},{8,16},{12,20},{16,24},{20,28},{24,0},{28,4},{1,9},{5... | collective-permute-start | bytes 393224 | tf_op jit(solution)/shard_map/ppermute | solution.py:449
  65.6 9.1 %collective-permute-start.13 = (f32[128,256]{1,0:T(8,128)S(1)}, f32[128,256]{1,0:T(8,128)S(1)}, u32[]{:S(2)}, u32[]{:S(2)}) collective-permute-start(f32[128,256]{1,0:T(8,128)S(1)} %last_traces.2.refs_9_.refs_6_), channel_id=1, source_target_pairs={{0,16},{4,20},{8,24},{12,28},{16,0},{20,4},{24,8},{28,12},{1,17},{... | collective-permute-start | bytes 393224 | tf_op jit(solution)/shard_map/ppermute | solution.py:449
  66.5 8.1 %collective-permute-start.14 = (f32[128,256]{1,0:T(8,128)S(1)}, f32[128,256]{1,0:T(8,128)S(1)}, u32[]{:S(2)}, u32[]{:S(2)}) collective-permute-start(f32[128,256]{1,0:T(8,128)S(1)} %last_traces.2.refs_9_.refs_6_), channel_id=1, source_target_pairs={{0,24},{4,28},{8,0},{12,4},{16,8},{20,12},{24,16},{28,20},{1,25},{... | collective-permute-start | bytes 393224 | tf_op jit(solution)/shard_map/ppermute | solution.py:449
  68.9 7.5 %collective-permute-start.11 = (f32[2,2,128,256]{3,2,1,0:T(8,128)S(1)}, f32[2,2,128,256]{3,2,1,0:T(8,128)S(1)}, u32[]{:S(2)}, u32[]{:S(2)}) collective-permute-start(f32[2,2,128,256]{3,2,1,0:T(8,128)S(1)} %get-tuple-element.62), channel_id=1, source_target_pairs={{0,4},{4,0},{8,12},{12,8},{16,20},{20,16},{24,28},{28,24},{1,5},{5... | collective-permute-start | bytes 1572872 | tf_op jit(solution)/shard_map/ppermute | solution.py:445
  75.4 2.5 %collective-permute-start.15 = (f32[128,256]{1,0:T(8,128)S(1)}, f32[128,256]{1,0:T(8,128)S(1)}, u32[]{:S(2)}, u32[]{:S(2)}) collective-permute-start(f32[128,256]{1,0:T(8,128)S(1)} %get-tuple-element.65), channel_id=1, source_target_pairs={{0,4},{4,0},{8,12},{12,8},{16,20},{20,16},{24,28},{28,24},{1,5},{5... | collective-permute-start | bytes 393224 | tf_op jit(solution)/shard_map/ppermute | solution.py:445

commit v8 on v7

--- a/solution.py
+++ b/solution.py
@@ -13,7 +13,7 @@
 WIDE = 128
 SWEEPS = 2
 CORES = 2
-EARLY = (0, 1, 3)
+EARLY = (0, 3, 1)
 LATE = (2,)
 LIMIT = 24 * 1024 * 1024
 MOST = 60 * 1024 * 1024

time: 81.1 us -> 80.7 us (level)
  waiting for transfers between devices: 9.95 us -> 9.06 us
    ppermute x6, waiting for transfers between devices: 8.41 us -> 7.53 us  [along_span(): return lax.ppermute(x, ('sweep', 'span'), pairs)]
  transfers between devices with their start and end apart: 16 -> 16, of which waited for: 3 -> 3; matrix products, arithmetic and copies ran while one was open for 0% -> 0% of each run, Pallas kernels for 37% -> 38%
where the time goes in v8:
time: 80.7 us; the launch traced here: 80.5 us
  Pallas kernels  36.2 us (45%)
  starting transfers between devices  25 us (31%)
  waiting for transfers between devices  9.06 us (11%)
  blocking collectives  8.03 us (10%)
  local copies, waits for them, and re-layouts  1.8 us (2%)
    pallas_call x14, Pallas kernels, call(): pl.pallas_call(body, out_shape=[jax.ShapeDtypeStruct(shape, kind) for _,...  36.2 us
    ppermute x6, starting transfers between devices, along_span(): return lax.ppermute(x, ('sweep', 'span'), pairs)  10.4 us
    ppermute x8, starting transfers between devices, from_chips(): lax.ppermute(x, 'sweep', ring('sweep', CORES * back))  9.37 us
    all_to_all x1, blocking collectives, per_device(): lax.all_to_all(own, 'sweep', 0, 0, axis_index_groups=[[i, i + 1] for i in...  8.03 us
    ppermute x6, waiting for transfers between devices, along_span(): return lax.ppermute(x, ('sweep', 'span'), pairs)  7.53 us
    ppermute x2, starting transfers between devices, swap(): return lax.ppermute(x, 'sweep', [(i, i ^ 1) for i in range(devices)])  5.16 us
    unnamed x20, local copies, waits for them, and re-layouts  1.77 us
  transfers between devices with their start and end apart: 16, of which 3 were waited for; matrix products, arithmetic and copies ran while one was open for 0% of the time, Pallas kernels for 38%

profile of v8, /device:TPU:1, one launch (start us, length us, event | category | flops | bytes accessed | tf_op | source)
XLA Modules:
  0.0 80.5 jit_solution(2145264855289988522)
XLA Ops:
  0.0 0.1 pad_add_fusion.refs_0_
  0.1 1.7 %copy-done.9 = f32[2,1,625,512]{3,1,2,0:T(1,128)S(1)} copy-done((f32[2,1,625,512]{3,1,2,0:T(1,128)S(1)}, f32[2,1,625,512]{3,1,2,0:T(1,128)}, u32[]{:S(2)}) %copy-start.9) | copy-done | bytes 2560024
  1.8 1.0 %start_faces.1 = (f32[2,25,5,1,256]{4,3,2,1,0:T(1,128)S(1)}, f32[2,25,5,1,256]{4,3,2,1,0:T(1,128)S(1)}, f32[2,25,5,1,256]{4,3,2,1,0:T(1,128)S(1)}, f32[2,25,5,1,256]{4,3,2,1,0:T(1,128)S(1)}) custom-call(s32[3]{0:T(128)S(1)} %pad_add_fusion.refs_0_, f32[2,25,25,1,512]{4,3,2,1,0:T(1,128)S(1)} %bitcast.37), custom_call_target="tpu_custom_call" | custom-call | flops 1000000000 | tf_op jit(solution)/shard_map/start_faces/pallas_call | solution.py:68
  2.8 0.0 copy-start.5
  2.8 0.0 copy-start.6
  2.8 0.0 copy-start.7
  2.8 0.0 copy-start.8
  2.8 2.2 %collective-permute-start.1 = (f32[2,125,1,256]{3,2,1,0:T(1,128)S(1)}, f32[2,125,1,256]{3,2,1,0:T(1,128)S(1)}, u32[]{:S(2)}, u32[]{:S(2)}) collective-permute-start(f32[2,125,1,256]{3,2,1,0:T(1,128)S(1)} %bitcast.36), channel_id=1, source_target_pairs={{0,1},{1,0},{2,3},{3,2},{4,5},{5,4},{6,7},{7,6},{8,9},{9,8},{10,11... | collective-permute-start | bytes 768008 | tf_op jit(solution)/shard_map/ppermute | solution.py:459
  5.0 3.0 %collective-permute-start.2 = (f32[2,125,1,256]{3,2,1,0:T(1,128)S(1)}, f32[2,125,1,256]{3,2,1,0:T(1,128)S(1)}, u32[]{:S(2)}, u32[]{:S(2)}) collective-permute-start(f32[2,125,1,256]{3,2,1,0:T(1,128)S(1)} %bitcast.35), channel_id=1, source_target_pairs={{0,7},{1,6},{2,5},{3,4},{4,3},{5,2},{6,1},{7,0},{8,15},{9,14},{10,... | collective-permute-start | bytes 768008 | tf_op jit(solution)/shard_map/ppermute | solution.py:459
  8.0 1.1 %collective-permute-start.3 = (f32[2,125,1,256]{3,2,1,0:T(1,128)S(1)}, f32[2,125,1,256]{3,2,1,0:T(1,128)S(1)}, u32[]{:S(2)}, u32[]{:S(2)}) collective-permute-start(f32[2,125,1,256]{3,2,1,0:T(1,128)S(1)} %bitcast.34), channel_id=1, source_target_pairs={{0,3},{1,2},{2,1},{3,0},{4,7},{5,6},{6,5},{7,4},{8,11},{9,10},{10,... | collective-permute-start | bytes 768008 | tf_op jit(solution)/shard_map/ppermute | solution.py:459
  9.1 0.0 collective-permute-start
  9.1 0.0 copy-done.5
  9.1 0.0 copy-done.6
  9.1 0.0 copy-done.7
  9.1 0.0 copy-done.8
  9.1 7.9 %fold_faces.1 = f32[2,2,384,640]{3,2,1,0:T(8,128)} custom-call(f32[2,625,1,625]{3,2,1,0:T(1,128)} %bitcast.18, f32[2,625,1,512]{3,2,1,0:T(1,128)} %bitcast.21, f32[2,625,1,125]{3,2,1,0:T(1,128)} %bitcast.24, f32[2,625,1,125]{3,2,1,0:T(1,128)} %bitcast.27, f32[2,625,1,125]{3,2,1,0:T(1,128)} %bitcast.30, f32[2,25,5,1,256]{4,3,2,1,0:T(1,128)} %copy-done.8, ...), custom_call_target="tpu_custom_call" | custom-call | tf_op jit(solution)/shard_map/fold_faces/pallas_call | solution.py:68
  17.1 0.0 copy-start.4
  17.1 8.0 %all_to_all.5.refs_0_ = f32[2,2,384,640]{3,2,1,0:T(8,128)S(1)} all-to-all(f32[2,2,384,640]{3,2,1,0:T(8,128)} %fold_faces.1), channel_id=1, replica_groups={{0,4},{8,12},{16,20},{24,28},{1,5},{9,13},{17,21},{25,29},{2,6},{10,14}..., dimensions={0} | all-to-all | bytes 7864320 | tf_op jit(solution)/shard_map/all_to_all | solution.py:485
  25.1 1.7 %chip_blocks.1 = (f32[4,384,256]{2,1,0:T(8,128)S(1)}, bf16[4,384,768]{2,1,0:T(8,128)(2,1)S(1)}, bf16[4,384,384]{2,1,0:T(8,128)(2,1)S(1)}, bf16[4,384,384]{2,1,0:...) custom-call(f32[2,2,384,640]{3,2,1,0:T(8,128)S(1)} %all_to_all.5.refs_0_), custom_call_target="tpu_custom_call" | custom-call | tf_op jit(solution)/shard_map/chip_blocks/pallas_call | solution.py:68
  26.8 0.0 copy-start
  26.8 1.3 %collective-permute-start.4 = (f32[128,128]{1,0:T(8,128)S(1)}, f32[128,128]{1,0:T(8,128)S(1)}, u32[]{:S(2)}, u32[]{:S(2)}) collective-permute-start(f32[128,128]{1,0:T(8,128)S(1)} %get-tuple-element.52), channel_id=1, source_target_pairs={{0,8},{4,12},{8,16},{12,20},{16,24},{20,28},{24,0},{28,4},{1,9},{5... | collective-permute-start | bytes 196616 | tf_op jit(solution)/shard_map/ppermute | solution.py:449
  28.1 0.0 collective-permute-done.1.refs_1_
  28.1 1.2 %collective-permute-start.5 = (f32[128,128]{1,0:T(8,128)S(1)}, f32[128,128]{1,0:T(8,128)S(1)}, u32[]{:S(2)}, u32[]{:S(2)}) collective-permute-start(f32[128,128]{1,0:T(8,128)S(1)} %get-tuple-element.52), channel_id=1, source_target_pairs={{0,16},{4,20},{8,24},{12,28},{16,0},{20,4},{24,8},{28,12},{1,17},{... | collective-permute-start | bytes 196616 | tf_op jit(solution)/shard_map/ppermute | solution.py:449
  29.3 0.0 collective-permute-done.2.refs_2_
  29.3 0.0 collective-permute-done.3.refs_3_
  29.3 1.2 %early_halos.1 = (bf16[1024,256]{1,0:T(8,128)(2,1)S(1)}, bf16[1024,256]{1,0:T(8,128)(2,1)S(1)}) custom-call(s32[3]{0:T(128)S(1)} %pad_add_fusion.refs_0_, f32[2,125,1,256]{3,2,1,0:T(1,128)S(1)} %collective-permute-done.1.refs_1_, f32[2,125,1,256]{3,2,1,0:T(1,128)S(1)} %collective-permute-done.2.refs_2_, f32[2,125,1,256]{3,2,1,0:T(1,128)S(1)} %collective-permute-done.3.refs_3_), custom_call_target="tpu_custom_call" | custom-call | flops 1000000000 | tf_op jit(solution)/shard_map/early_halos/pallas_call | solution.py:68
  30.5 0.0 collective-permute-done.refs_4_
  30.5 0.0 copy-done.4
  30.5 0.0 copy-done.1
  30.6 0.0 copy-done.2
  30.6 0.0 copy-done.3
  30.6 0.0 copy-done
  30.6 1.4 %first_traces.1 = (bf16[1024,256]{1,0:T(8,128)(2,1)S(1)}, bf16[1024,256]{1,0:T(8,128)(2,1)S(1)}, f32[128,256]{1,0:T(8,128)S(1)}, f32[640,512]{1,0:T(8,128)S(1)},...) custom-call(s32[3]{0:T(128)S(1)} %pad_add_fusion.refs_0_, ...), custom_call_target="tpu_custom_call", output_to_operand_aliasing={{0}: (10, {}), {1}: (11, {})} | custom-call | flops 2000000000 | tf_op jit(solution)/shard_map/first_traces/pallas_call | solution.py:68
  32.0 0.2 collective-permute-start.6
  32.2 1.2 %collective-permute-start.7 = (f32[128,256]{1,0:T(8,128)S(1)}, f32[128,256]{1,0:T(8,128)S(1)}, u32[]{:S(2)}, u32[]{:S(2)}) collective-permute-start(f32[128,256]{1,0:T(8,128)S(1)} %get-tuple-element.54), channel_id=1, source_target_pairs={{0,16},{4,20},{8,24},{12,28},{16,0},{20,4},{24,8},{28,12},{1,17},{... | collective-permute-start | bytes 393224 | tf_op jit(solution)/shard_map/ppermute | solution.py:449
  33.5 1.2 %collective-permute-start.8 = (f32[128,256]{1,0:T(8,128)S(1)}, f32[128,256]{1,0:T(8,128)S(1)}, u32[]{:S(2)}, u32[]{:S(2)}) collective-permute-start(f32[128,256]{1,0:T(8,128)S(1)} %get-tuple-element.54), channel_id=1, source_target_pairs={{0,24},{4,28},{8,0},{12,4},{16,8},{20,12},{24,16},{28,20},{1,25},{... | collective-permute-start | bytes 393224 | tf_op jit(solution)/shard_map/ppermute | solution.py:449
  34.6 0.0 collective-permute-done.4.refs_5_.refs_6_
  34.6 0.0 collective-permute-done.5.refs_6_.refs_7_
  34.6 1.3 %other_faces.1.refs_1_ = f32[4,256,256]{2,1,0:T(8,128)S(1)} custom-call(f32[4,384,256]{2,1,0:T(8,128)S(1)} %get-tuple-element.47.refs_0_, bf16[4,384,768]{2,1,0:T(8,128)(2,1)S(1)} %get-tuple-element.48.refs_1_, bf16[4,384,384]{2,1,0:T(8,128)(2,1)S(1)} %get-tuple-element.49.refs_2_, bf16[1024,256]{1,0:T(8,128)(2,1)S(1)} %get-tuple-element.50.refs_3_, ...), custom_call_target="tpu_custom_call" | custom-call | flops 2000000000 | tf_op jit(solution)/shard_map/other_faces/pallas_call | solution.py:68
  35.9 0.9 %collective-permute-done.6.refs_3_ = f32[128,256]{1,0:T(8,128)S(1)} collective-permute-done((f32[128,256]{1,0:T(8,128)S(1)}, f32[128,256]{1,0:T(8,128)S(1)}, u32[]{:S(2)}, u32[]{:S(2)}) %collective-permute-start.6) | collective-permute-done | bytes 131104 | tf_op jit(solution)/shard_map/ppermute | solution.py:449
  36.8 0.6 collective-permute-done.7.refs_4_
  37.4 0.0 collective-permute-done.8.refs_5_
  37.4 1.1 %next_faces.1 = (f32[500,256]{1,0:T(8,128)S(1)}, f32[500,256]{1,0:T(8,128)S(1)}) custom-call(s32[3]{0:T(128)S(1)} %pad_add_fusion.refs_0_, f32[4,256,256]{2,1,0:T(8,128)S(1)} %other_faces.1.refs_1_, bf16[4,384,384]{2,1,0:T(8,128)(2,1)S(1)} %get-tuple-element.53.refs_2_, f32[128,256]{1,0:T(8,128)S(1)} %collective-permute-done.6.refs_3_, ...), custom_call_target="tpu_custom_call" | custom-call | flops 1000000000 | tf_op jit(solution)/shard_map/next_faces/pallas_call | solution.py:68
  38.5 2.3 %collective-permute-start.10 = (f32[500,256]{1,0:T(8,128)S(1)}, f32[500,256]{1,0:T(8,128)S(1)}, u32[]{:S(2)}, u32[]{:S(2)}) collective-permute-start(f32[500,256]{1,0:T(8,128)S(1)} %get-tuple-element.56.refs_7_), channel_id=1, source_target_pairs={{0,3},{1,2},{2,1},{3,0},{4,7},{5,6},{6,5},{7,4},{8,11},{9,10},{10,... | collective-permute-start | bytes 1536008 | tf_op jit(solution)/shard_map/ppermute | solution.py:459
  40.8 1.9 %collective-permute-start.9 = (f32[500,256]{1,0:T(8,128)S(1)}, f32[500,256]{1,0:T(8,128)S(1)}, u32[]{:S(2)}, u32[]{:S(2)}) collective-permute-start(f32[500,256]{1,0:T(8,128)S(1)} %get-tuple-element.55.refs_6_), channel_id=1, source_target_pairs={{0,1},{1,0},{2,3},{3,2},{4,5},{5,4},{6,7},{7,6},{8,9},{9,8},{10,11... | collective-permute-start | bytes 1536008 | tf_op jit(solution)/shard_map/ppermute | solution.py:459
  42.7 11.7 %fold_rest.1 = (f32[640,512]{1,0:T(8,128)S(1)}, bf16[640,768]{1,0:T(8,128)(2,1)S(1)}, bf16[640,384]{1,0:T(8,128)(2,1)S(1)}, f32[640,512]{1,0:T(8,128)S(1)}, bf16...) custom-call(s32[3]{0:T(128)S(1)} %pad_add_fusion.refs_0_, f32[2,625,1,625]{3,2,1,0:T(1,128)S(1)} %bitcast.20, ...), custom_call_target="tpu_custom_call" | custom-call | flops 10000000000 | tf_op jit(solution)/shard_map/fold_rest/pallas_call | solution.py:68
  54.4 0.0 collective-permute-done.10.refs_4_.refs_8_
  54.4 7.5 %collective-permute-done.9.refs_5_.refs_7_ = f32[500,256]{1,0:T(8,128)S(1)} collective-permute-done((f32[500,256]{1,0:T(8,128)S(1)}, f32[500,256]{1,0:T(8,128)S(1)}, u32[]{:S(2)}, u32[]{:S(2)}) %collective-permute-start.9) | collective-permute-done | bytes 512032 | tf_op jit(solution)/shard_map/ppermute | solution.py:459
  61.9 1.2 %last_traces.2.refs_9_.refs_6_ = f32[128,256]{1,0:T(8,128)S(1)} custom-call(s32[3]{0:T(128)S(1)} %pad_add_fusion.refs_0_, f32[256,256]{1,0:T(8,128)S(1)} %get-tuple-element.41.refs_1_, bf16[256,1024]{1,0:T(8,128)(2,1)S(1)} %get-tuple-element.42.refs_2_, bf16[256,1024]{1,0:T(8,128)(2,1)S(1)} %get-tuple-element.43.refs_3_, ...), custom_call_target="tpu_custom_call" | custom-call | flops 1000000000 | tf_op jit(solution)/shard_map/last_traces/pallas_call | solution.py:68
  63.1 2.2 %collective-permute-start.12 = (f32[128,256]{1,0:T(8,128)S(1)}, f32[128,256]{1,0:T(8,128)S(1)}, u32[]{:S(2)}, u32[]{:S(2)}) collective-permute-start(f32[128,256]{1,0:T(8,128)S(1)} %last_traces.2.refs_9_.refs_6_), channel_id=1, source_target_pairs={{0,8},{4,12},{8,16},{12,20},{16,24},{20,28},{24,0},{28,4},{1,9},{5... | collective-permute-start | bytes 393224 | tf_op jit(solution)/shard_map/ppermute | solution.py:449
  65.3 0.8 %collective-permute-start.13 = (f32[128,256]{1,0:T(8,128)S(1)}, f32[128,256]{1,0:T(8,128)S(1)}, u32[]{:S(2)}, u32[]{:S(2)}) collective-permute-start(f32[128,256]{1,0:T(8,128)S(1)} %last_traces.2.refs_9_.refs_6_), channel_id=1, source_target_pairs={{0,16},{4,20},{8,24},{12,28},{16,0},{20,4},{24,8},{28,12},{1,17},{... | collective-permute-start | bytes 393224 | tf_op jit(solution)/shard_map/ppermute | solution.py:449
  66.1 1.2 %collective-permute-start.14 = (f32[128,256]{1,0:T(8,128)S(1)}, f32[128,256]{1,0:T(8,128)S(1)}, u32[]{:S(2)}, u32[]{:S(2)}) collective-permute-start(f32[128,256]{1,0:T(8,128)S(1)} %last_traces.2.refs_9_.refs_6_), channel_id=1, source_target_pairs={{0,24},{4,28},{8,0},{12,4},{16,8},{20,12},{24,16},{28,20},{1,25},{... | collective-permute-start | bytes 393224 | tf_op jit(solution)/shard_map/ppermute | solution.py:449
  67.3 1.2 %last_traces.3 = (f32[128,256]{1,0:T(8,128)S(1)}, f32[2,2,128,256]{3,2,1,0:T(8,128)S(1)}) custom-call(s32[3]{0:T(128)S(1)} %pad_add_fusion.refs_0_, f32[256,256]{1,0:T(8,128)S(1)} %get-tuple-element.41.refs_1_, bf16[256,1024]{1,0:T(8,128)(2,1)S(1)} %get-tuple-element.42.refs_2_, bf16[256,1024]{1,0:T(8,128)(2,1)S(1)} %get-tuple-element.43.refs_3_, ...), custom_call_target="tpu_custom_call" | custom-call | tf_op jit(solution)/shard_map/last_traces/pallas_call | solution.py:68
  68.5 4.2 %collective-permute-start.11 = (f32[2,2,128,256]{3,2,1,0:T(8,128)S(1)}, f32[2,2,128,256]{3,2,1,0:T(8,128)S(1)}, u32[]{:S(2)}, u32[]{:S(2)}) collective-permute-start(f32[2,2,128,256]{3,2,1,0:T(8,128)S(1)} %get-tuple-element.62), channel_id=1, source_target_pairs={{0,4},{4,0},{8,12},{12,8},{16,20},{20,16},{24,28},{28,24},{1,5},{5... | collective-permute-start | bytes 1572872 | tf_op jit(solution)/shard_map/ppermute | solution.py:445
  72.7 1.6 %field_without_inflow.2.refs_1_ = f32[2,640,256]{2,1,0:T(8,128)S(1)} custom-call(s32[3]{0:T(128)S(1)} %pad_add_fusion.refs_0_, f32[640,512]{1,0:T(8,128)S(1)} %get-tuple-element.46.refs_1_, f32[640,512]{1,0:T(8,128)S(1)} %get-tuple-element.57.refs_6_.refs_2_, f32[640,512]{1,0:T(8,128)S(1)} %get-tuple-element.58.refs_3_, ...), custom_call_target="tpu_custom_call" | custom-call | tf_op jit(solution)/shard_map/field_without_inflow/pallas_call | solution.py:68
  74.3 0.0 collective-permute-done.12.refs_3_
  74.3 0.0 collective-permute-done.13.refs_4_
  74.3 0.0 collective-permute-done.14.refs_5_
  74.3 0.8 inflow_of_cores.1
  75.1 1.0 %collective-permute-start.15 = (f32[128,256]{1,0:T(8,128)S(1)}, f32[128,256]{1,0:T(8,128)S(1)}, u32[]{:S(2)}, u32[]{:S(2)}) collective-permute-start(f32[128,256]{1,0:T(8,128)S(1)} %get-tuple-element.65), channel_id=1, source_target_pairs={{0,4},{4,0},{8,12},{12,8},{16,20},{20,16},{24,28},{28,24},{1,5},{5... | collective-permute-start | bytes 393224 | tf_op jit(solution)/shard_map/ppermute | solution.py:445
  76.0 0.0 collective-permute-done.11
  76.1 1.5 %field_without_inflow.3.refs_2_ = f32[2,640,256]{2,1,0:T(8,128)S(1)} custom-call(s32[3]{0:T(128)S(1)} %pad_add_fusion.refs_0_, f32[640,512]{1,0:T(8,128)S(1)} %get-tuple-element.46.refs_1_, f32[640,512]{1,0:T(8,128)S(1)} %get-tuple-element.57.refs_6_.refs_2_, f32[640,512]{1,0:T(8,128)S(1)} %get-tuple-element.58.refs_3_, ...), custom_call_target="tpu_custom_call" | custom-call | tf_op jit(solution)/shard_map/field_without_inflow/pallas_call | solution.py:68
  77.6 0.0 collective-permute-done.15.refs_4_
  77.6 2.7 %whole_field.1 = f32[2,625,1,512]{3,2,1,0:T(1,128)} custom-call(s32[3]{0:T(128)S(1)} %pad_add_fusion.refs_0_, f32[2,640,256]{2,1,0:T(8,128)S(1)} %field_without_inflow.2.refs_1_, f32[2,640,256]{2,1,0:T(8,128)S(1)} %field_without_inflow.3.refs_2_, f32[128,256]{1,0:T(8,128)S(1)} %get-tuple-element.64.refs_3_, f32[128,256]{1,0:T(8,128)S(1)} %collective-permute-done.15.refs_4_, ...), custom_call_target="tpu_custom_call" | custom-call | flops 1000000000 | tf_op jit(solution)/shard_map/whole_field/pallas_call | solution.py:68
  (5 shorter events, 0.0 us)
Async XLA Ops:
  0.1 1.7 %copy-start.9 = (f32[2,1,625,512]{3,1,2,0:T(1,128)S(1)}, f32[2,1,625,512]{3,1,2,0:T(1,128)}, u32[]{:S(2)}) copy-start(f32[2,1,625,512]{3,1,2,0:T(1,128)} %param.7) | copy-start | bytes 7680004
  2.8 6.3 %copy-start.5 = (f32[2,25,5,1,256]{4,3,2,1,0:T(1,128)}, f32[2,25,5,1,256]{4,3,2,1,0:T(1,128)S(1)}, u32[]{:S(2)}) copy-start(f32[2,25,5,1,256]{4,3,2,1,0:T(1,128)S(1)} %get-tuple-element.39.refs_7_) | copy-start | bytes 768004
  2.8 6.3 %copy-start.6 = (f32[2,25,5,1,256]{4,3,2,1,0:T(1,128)}, f32[2,25,5,1,256]{4,3,2,1,0:T(1,128)S(1)}, u32[]{:S(2)}) copy-start(f32[2,25,5,1,256]{4,3,2,1,0:T(1,128)S(1)} %get-tuple-element.38.refs_6_) | copy-start | bytes 768004
  2.8 6.3 %copy-start.7 = (f32[2,25,5,1,256]{4,3,2,1,0:T(1,128)}, f32[2,25,5,1,256]{4,3,2,1,0:T(1,128)S(1)}, u32[]{:S(2)}) copy-start(f32[2,25,5,1,256]{4,3,2,1,0:T(1,128)S(1)} %get-tuple-element.40.refs_8_) | copy-start | bytes 768004
  2.8 6.3 %copy-start.8 = (f32[2,25,5,1,256]{4,3,2,1,0:T(1,128)}, f32[2,25,5,1,256]{4,3,2,1,0:T(1,128)S(1)}, u32[]{:S(2)}) copy-start(f32[2,25,5,1,256]{4,3,2,1,0:T(1,128)S(1)} %get-tuple-element.37.refs_5_) | copy-start | bytes 768004
  2.8 25.3 %collective-permute-start.1 = (f32[2,125,1,256]{3,2,1,0:T(1,128)S(1)}, f32[2,125,1,256]{3,2,1,0:T(1,128)S(1)}, u32[]{:S(2)}, u32[]{:S(2)}) collective-permute-start(f32[2,125,1,256]{3,2,1,0:T(1,128)S(1)} %bitcast.36), channel_id=1, source_target_pairs={{0,1},{1,0},{2,3},{3,2},{4,5},{5,4},{6,7},{7,6},{8,9},{9,8},{10,11... | collective-permute-start | bytes 768008 | tf_op jit(solution)/shard_map/ppermute | solution.py:459
  5.0 24.3 %collective-permute-start.2 = (f32[2,125,1,256]{3,2,1,0:T(1,128)S(1)}, f32[2,125,1,256]{3,2,1,0:T(1,128)S(1)}, u32[]{:S(2)}, u32[]{:S(2)}) collective-permute-start(f32[2,125,1,256]{3,2,1,0:T(1,128)S(1)} %bitcast.35), channel_id=1, source_target_pairs={{0,7},{1,6},{2,5},{3,4},{4,3},{5,2},{6,1},{7,0},{8,15},{9,14},{10,... | collective-permute-start | bytes 768008 | tf_op jit(solution)/shard_map/ppermute | solution.py:459
  8.0 21.3 %collective-permute-start.3 = (f32[2,125,1,256]{3,2,1,0:T(1,128)S(1)}, f32[2,125,1,256]{3,2,1,0:T(1,128)S(1)}, u32[]{:S(2)}, u32[]{:S(2)}) collective-permute-start(f32[2,125,1,256]{3,2,1,0:T(1,128)S(1)} %bitcast.34), channel_id=1, source_target_pairs={{0,3},{1,2},{2,1},{3,0},{4,7},{5,6},{6,5},{7,4},{8,11},{9,10},{10,... | collective-permute-start | bytes 768008 | tf_op jit(solution)/shard_map/ppermute | solution.py:459
  9.1 21.4 %collective-permute-start = (f32[2,125,1,256]{3,2,1,0:T(1,128)S(1)}, f32[2,125,1,256]{3,2,1,0:T(1,128)S(1)}, u32[]{:S(2)}, u32[]{:S(2)}) collective-permute-start(f32[2,125,1,256]{3,2,1,0:T(1,128)S(1)} %bitcast.33), channel_id=1, source_target_pairs={{0,5},{1,4},{2,7},{3,6},{4,1},{5,0},{6,3},{7,2},{8,13},{9,12},{10,... | collective-permute-start | bytes 768008 | tf_op jit(solution)/shard_map/ppermute | solution.py:459
  17.1 13.5 %copy-start.4 = (f32[2,1,625,125]{3,1,2,0:T(1,128)S(1)}, f32[2,1,625,125]{3,1,2,0:T(1,128)}, u32[]{:S(2)}) copy-start(f32[2,1,625,125]{3,1,2,0:T(1,128)} %param.11) | copy-start | bytes 1875004
  25.1 5.4 %copy-start.1 = (f32[2,1,625,512]{3,1,2,0:T(1,128)S(1)}, f32[2,1,625,512]{3,1,2,0:T(1,128)}, u32[]{:S(2)}) copy-start(f32[2,1,625,512]{3,1,2,0:T(1,128)} %param.6) | copy-start | bytes 7680004
  25.1 5.4 %copy-start.2 = (f32[2,1,625,125]{3,1,2,0:T(1,128)S(1)}, f32[2,1,625,125]{3,1,2,0:T(1,128)}, u32[]{:S(2)}) copy-start(f32[2,1,625,125]{3,1,2,0:T(1,128)} %param.9) | copy-start | bytes 1875004
  25.1 5.4 %copy-start.3 = (f32[2,1,625,125]{3,1,2,0:T(1,128)S(1)}, f32[2,1,625,125]{3,1,2,0:T(1,128)}, u32[]{:S(2)}) copy-start(f32[2,1,625,125]{3,1,2,0:T(1,128)} %param.10) | copy-start | bytes 1875004
  26.8 3.8 %copy-start = (f32[2,1,625,625]{3,1,2,0:T(1,128)S(1)}, f32[2,1,625,625]{3,1,2,0:T(1,128)}, u32[]{:S(2)}) copy-start(f32[2,1,625,625]{3,1,2,0:T(1,128)} %param.8) | copy-start | bytes 9375004
  26.8 7.8 %collective-permute-start.4 = (f32[128,128]{1,0:T(8,128)S(1)}, f32[128,128]{1,0:T(8,128)S(1)}, u32[]{:S(2)}, u32[]{:S(2)}) collective-permute-start(f32[128,128]{1,0:T(8,128)S(1)} %get-tuple-element.52), channel_id=1, source_target_pairs={{0,8},{4,12},{8,16},{12,20},{16,24},{20,28},{24,0},{28,4},{1,9},{5... | collective-permute-start | bytes 196616 | tf_op jit(solution)/shard_map/ppermute | solution.py:449
  28.1 6.5 %collective-permute-start.5 = (f32[128,128]{1,0:T(8,128)S(1)}, f32[128,128]{1,0:T(8,128)S(1)}, u32[]{:S(2)}, u32[]{:S(2)}) collective-permute-start(f32[128,128]{1,0:T(8,128)S(1)} %get-tuple-element.52), channel_id=1, source_target_pairs={{0,16},{4,20},{8,24},{12,28},{16,0},{20,4},{24,8},{28,12},{1,17},{... | collective-permute-start | bytes 196616 | tf_op jit(solution)/shard_map/ppermute | solution.py:449
  32.0 4.9 %collective-permute-start.6 = (f32[128,256]{1,0:T(8,128)S(1)}, f32[128,256]{1,0:T(8,128)S(1)}, u32[]{:S(2)}, u32[]{:S(2)}) collective-permute-start(f32[128,256]{1,0:T(8,128)S(1)} %get-tuple-element.54), channel_id=1, source_target_pairs={{0,8},{4,12},{8,16},{12,20},{16,24},{20,28},{24,0},{28,4},{1,9},{5... | collective-permute-start | bytes 393224 | tf_op jit(solution)/shard_map/ppermute | solution.py:449
  32.2 5.2 %collective-permute-start.7 = (f32[128,256]{1,0:T(8,128)S(1)}, f32[128,256]{1,0:T(8,128)S(1)}, u32[]{:S(2)}, u32[]{:S(2)}) collective-permute-start(f32[128,256]{1,0:T(8,128)S(1)} %get-tuple-element.54), channel_id=1, source_target_pairs={{0,16},{4,20},{8,24},{12,28},{16,0},{20,4},{24,8},{28,12},{1,17},{... | collective-permute-start | bytes 393224 | tf_op jit(solution)/shard_map/ppermute | solution.py:449
  33.5 4.0 %collective-permute-start.8 = (f32[128,256]{1,0:T(8,128)S(1)}, f32[128,256]{1,0:T(8,128)S(1)}, u32[]{:S(2)}, u32[]{:S(2)}) collective-permute-start(f32[128,256]{1,0:T(8,128)S(1)} %get-tuple-element.54), channel_id=1, source_target_pairs={{0,24},{4,28},{8,0},{12,4},{16,8},{20,12},{24,16},{28,20},{1,25},{... | collective-permute-start | bytes 393224 | tf_op jit(solution)/shard_map/ppermute | solution.py:449
  38.5 15.9 %collective-permute-start.10 = (f32[500,256]{1,0:T(8,128)S(1)}, f32[500,256]{1,0:T(8,128)S(1)}, u32[]{:S(2)}, u32[]{:S(2)}) collective-permute-start(f32[500,256]{1,0:T(8,128)S(1)} %get-tuple-element.56.refs_7_), channel_id=1, source_target_pairs={{0,3},{1,2},{2,1},{3,0},{4,7},{5,6},{6,5},{7,4},{8,11},{9,10},{10,... | collective-permute-start | bytes 1536008 | tf_op jit(solution)/shard_map/ppermute | solution.py:459
  40.8 21.1 %collective-permute-start.9 = (f32[500,256]{1,0:T(8,128)S(1)}, f32[500,256]{1,0:T(8,128)S(1)}, u32[]{:S(2)}, u32[]{:S(2)}) collective-permute-start(f32[500,256]{1,0:T(8,128)S(1)} %get-tuple-element.55.refs_6_), channel_id=1, source_target_pairs={{0,1},{1,0},{2,3},{3,2},{4,5},{5,4},{6,7},{7,6},{8,9},{9,8},{10,11... | collective-permute-start | bytes 1536008 | tf_op jit(solution)/shard_map/ppermute | solution.py:459
  63.1 11.2 %collective-permute-start.12 = (f32[128,256]{1,0:T(8,128)S(1)}, f32[128,256]{1,0:T(8,128)S(1)}, u32[]{:S(2)}, u32[]{:S(2)}) collective-permute-start(f32[128,256]{1,0:T(8,128)S(1)} %last_traces.2.refs_9_.refs_6_), channel_id=1, source_target_pairs={{0,8},{4,12},{8,16},{12,20},{16,24},{20,28},{24,0},{28,4},{1,9},{5... | collective-permute-start | bytes 393224 | tf_op jit(solution)/shard_map/ppermute | solution.py:449
  65.3 9.0 %collective-permute-start.13 = (f32[128,256]{1,0:T(8,128)S(1)}, f32[128,256]{1,0:T(8,128)S(1)}, u32[]{:S(2)}, u32[]{:S(2)}) collective-permute-start(f32[128,256]{1,0:T(8,128)S(1)} %last_traces.2.refs_9_.refs_6_), channel_id=1, source_target_pairs={{0,16},{4,20},{8,24},{12,28},{16,0},{20,4},{24,8},{28,12},{1,17},{... | collective-permute-start | bytes 393224 | tf_op jit(solution)/shard_map/ppermute | solution.py:449
  66.1 8.2 %collective-permute-start.14 = (f32[128,256]{1,0:T(8,128)S(1)}, f32[128,256]{1,0:T(8,128)S(1)}, u32[]{:S(2)}, u32[]{:S(2)}) collective-permute-start(f32[128,256]{1,0:T(8,128)S(1)} %last_traces.2.refs_9_.refs_6_), channel_id=1, source_target_pairs={{0,24},{4,28},{8,0},{12,4},{16,8},{20,12},{24,16},{28,20},{1,25},{... | collective-permute-start | bytes 393224 | tf_op jit(solution)/shard_map/ppermute | solution.py:449
  68.5 7.5 %collective-permute-start.11 = (f32[2,2,128,256]{3,2,1,0:T(8,128)S(1)}, f32[2,2,128,256]{3,2,1,0:T(8,128)S(1)}, u32[]{:S(2)}, u32[]{:S(2)}) collective-permute-start(f32[2,2,128,256]{3,2,1,0:T(8,128)S(1)} %get-tuple-element.62), channel_id=1, source_target_pairs={{0,4},{4,0},{8,12},{12,8},{16,20},{20,16},{24,28},{28,24},{1,5},{5... | collective-permute-start | bytes 1572872 | tf_op jit(solution)/shard_map/ppermute | solution.py:445
  75.1 2.5 %collective-permute-start.15 = (f32[128,256]{1,0:T(8,128)S(1)}, f32[128,256]{1,0:T(8,128)S(1)}, u32[]{:S(2)}, u32[]{:S(2)}) collective-permute-start(f32[128,256]{1,0:T(8,128)S(1)} %get-tuple-element.65), channel_id=1, source_target_pairs={{0,4},{4,0},{8,12},{12,8},{16,20},{20,16},{24,28},{28,24},{1,5},{5... | collective-permute-start | bytes 393224 | tf_op jit(solution)/shard_map/ppermute | solution.py:445
